TPU v7x, 768 devices: a whole 4x8x12 slice. The times are simulated.
768 devices in a mesh: outer: 8 (over y_lo, core), inner: 96 (over z, x, y_hi).
Axes of the slice: x: 4, y: 8 (y_hi: 2, y_lo: 4; y = y_hi * 4 + y_lo), z: 12, core: 2. Of those that a mesh axis runs over, the one named last changes fastest.
Arguments:
- image_emb: bfloat16 [196608, 1152], P(('outer', 'inner')), may hold values from -0.3 to 0.3
- text_emb: bfloat16 [196608, 1152], P(('outer', 'inner')), may hold values from -0.3 to 0.3
- positive: int32 [196608], P(('outer', 'inner')), may hold values from 0 to 196607, as said below
- log_scale: float32 [1], replicated, may hold values from 1.8 to 2.5
- logit_bias: float32 [1], replicated, may hold values from -3 to -1
Outputs:
- image_grad: float32 [196608, 1152], P(('outer', 'inner'))
- text_grad: float32 [196608, 1152], P(('outer', 'inner'))
- loss: float32 [1], replicated
- head_grad: float32 [2], replicated
Inputs may be any that keep to these rules, and one draw needn't show every extreme that they name: `positive`: each image's matching text lies in one of the text blocks that the image is scored against.
All inputs are finite; a program needn't handle non-finite values.
Results may differ from a plain program's by a relative error of at most 0.00047.
Values may be sent and summed in bfloat16 or wider, within the bound.
No kernel may reach another device: no remote copies, remote signals or barrier semaphores. Data moves between devices by JAX's collectives and lax.ppermute only.
A program may use at most 32 MiB of HBM per device.

v0:
```python
import jax
import jax.numpy as jnp
from jax import lax
from jax.sharding import PartitionSpec as P

IN_SPAN = 3


NORM_EPS = 1e-06


def passed_along(block, axis, distance):
    devices = range(lax.axis_size(axis))
    route = [((i - distance) % len(devices), i) for i in devices]
    return lax.ppermute(block, axis, route)


def normalize(values):
    values32 = values.astype(jnp.float32)
    inv_norm = lax.rsqrt(jnp.sum(values32 * values32, axis=-1, keepdims=True) + NORM_EPS)
    return (values32 * inv_norm, inv_norm)


def unnormalize(unit32, inv_norm, grad_unit):
    return inv_norm * (grad_unit - unit32 * jnp.sum(unit32 * grad_unit, axis=-1, keepdims=True))


def score_tile(img_unit, txt_unit, matches, text_start, temp_scale, bias_value):
    cosine = jnp.dot(img_unit, txt_unit.T, preferred_element_type=jnp.float32)
    logit = temp_scale * cosine + bias_value
    text_ids = text_start + jnp.arange(txt_unit.shape[0], dtype=jnp.int32)
    labels = jnp.where(matches[:, None] == text_ids[None, :], 1.0, -1.0).astype(jnp.float32)
    margin = labels * logit
    tile_loss = jnp.sum(jax.nn.softplus(-margin))
    slope = -labels * jax.nn.sigmoid(-margin)
    weights = slope.astype(jnp.bfloat16)
    img_part = jnp.dot(weights, txt_unit, preferred_element_type=jnp.float32)
    txt_part = None
    txt_part = lax.dot_general(
        weights, img_unit, (((0,), (0,)), ((), ())), preferred_element_type=jnp.float32
    )
    return (tile_loss, jnp.sum(slope * cosine), jnp.sum(slope), img_part, txt_part)


def shards(image_emb, text_emb, positive, log_scale, logit_bias):
    block_rows = image_emb.shape[0]
    width = image_emb.shape[1]
    temp_scale = jnp.exp(log_scale[0])
    bias_value = logit_bias[0]
    img_unit32, img_inv = normalize(image_emb)
    txt_unit32, txt_inv = normalize(text_emb)
    img_unit = img_unit32.astype(jnp.bfloat16)
    txt_unit = txt_unit32.astype(jnp.bfloat16)
    outer_pos = lax.axis_index("outer")
    inner_pos = lax.axis_index("inner")
    outer_size = lax.axis_size("outer")
    inner_size = lax.axis_size("inner")
    route_list = [(0, inner_off) for inner_off in range(IN_SPAN)]
    route_list = route_list + [(1, inner_off) for inner_off in reversed(range(IN_SPAN))]
    visiting = txt_unit
    carried = jnp.zeros((block_rows, width), jnp.float32)
    img_total = jnp.zeros((block_rows, width), jnp.float32)
    loss_sum = jnp.float32(0.0)
    slope_cos_sum = jnp.float32(0.0)
    slope_total = jnp.float32(0.0)
    before = route_list[0]
    for section, (outer_off, inner_off) in enumerate(route_list):
        if section > 0:
            if outer_off == before[0]:
                towards = inner_off - before[1]
                visiting = passed_along(visiting, "inner", towards)
                carried = passed_along(carried, "inner", towards)
            else:
                visiting = passed_along(visiting, "outer", 1)
                carried = passed_along(carried, "outer", 1)
        before = (outer_off, inner_off)
        owner_id = (outer_pos - outer_off) % outer_size * inner_size + (
            inner_pos - inner_off
        ) % inner_size
        tile_loss, slope_cos, slope_sum, img_part, txt_part = score_tile(
            img_unit, visiting, positive, owner_id * block_rows, temp_scale, bias_value
        )
        img_total = img_total + img_part
        loss_sum = loss_sum + tile_loss
        slope_cos_sum = slope_cos_sum + slope_cos
        slope_total = slope_total + slope_sum
        carried = carried + txt_part
    txt_total = passed_along(carried, "outer", -1)
    loss_all, slope_cos_all, slope_all = lax.psum(
        (loss_sum, slope_cos_sum, slope_total), ("outer", "inner")
    )
    image_grad = unnormalize(img_unit32, img_inv, temp_scale * img_total)
    text_grad = unnormalize(txt_unit32, txt_inv, temp_scale * txt_total)
    pair_count = jnp.float32(block_rows * outer_size * inner_size * 2 * IN_SPAN * block_rows)
    loss = (loss_all / pair_count).reshape(1)
    head_grad = jnp.stack([temp_scale * slope_cos_all, slope_all]) / pair_count
    return (image_grad, text_grad, loss, head_grad)


def solution(mesh):
    return jax.shard_map(
        shards,
        mesh=mesh,
        in_specs=(
            P(("outer", "inner"), None),
            P(("outer", "inner"), None),
            P(("outer", "inner")),
            P(),
            P(),
        ),
        out_specs=(P(("outer", "inner"), None), P(("outer", "inner"), None), P(), P()),
        check_vma=False,
    )
```

profile of v0, /device:TPU:1, one launch (start us, length us, event | category | flops | bytes accessed | tf_op | source)
XLA Modules:
  0.0 565.1 jit_solution(4698997864823649702)
XLA Ops:
  5.3 1.5 fusion.41
  6.8 8.3 %collective-permute-start.5 = (f32[256,1152]{1,0:T(8,128)}, f32[256,1152]{1,0:T(8,128)S(1)}, u32[]{:S(2)}, u32[]{:S(2)}) collective-permute-start(f32[256,1152]{1,0:T(8,128)} %fusion.41), channel_id=1, source_target_pairs={{95,0},{0,1},{1,2},{2,3},{3,4},{4,5},{5,6},{6,7},{7,8},{8,9},{9,10... | collective-permute-start | bytes 3538952 | tf_op jit(solution)/shard_map/ppermute | solution.py:15
  15.1 2.7 collective-permute-start
  17.8 84.7 %collective-permute-done = bf16[256,1152]{1,0:T(8,128)(2,1)} collective-permute-done((bf16[256,1152]{1,0:T(8,128)(2,1)S(1)}, bf16[256,1152]{1,0:T(8,128)(2,1)}, u32[]{:S(2)}, u32[]{:S(2)}) %collective-permute-start) | collective-permute-done | bytes 589856 | tf_op jit(solution)/shard_map/ppermute | solution.py:15
  104.7 1.9 collective-permute-start.6
  106.6 1.9 collective-permute-start.1
  108.6 76.1 %collective-permute-done.1 = bf16[256,1152]{1,0:T(8,128)(2,1)} collective-permute-done((bf16[256,1152]{1,0:T(8,128)(2,1)}, bf16[256,1152]{1,0:T(8,128)(2,1)}, u32[]{:S(2)}, u32[]{:S(2)}) %collective-permute-start.1) | collective-permute-done | bytes 589856 | tf_op jit(solution)/shard_map/ppermute | solution.py:15
  186.9 8.1 %collective-permute-start.7 = (f32[256,1152]{1,0:T(8,128)S(1)}, f32[256,1152]{1,0:T(8,128)S(1)}, u32[]{:S(2)}, u32[]{:S(2)}) collective-permute-start(f32[256,1152]{1,0:T(8,128)S(1)} %add.308), channel_id=1, source_target_pairs={{672,0},{0,96},{96,192},{192,288},{288,384},{384,480},{480,576},{5... | collective-permute-start | bytes 3538952 | tf_op jit(solution)/shard_map/ppermute | solution.py:15
  195.1 1.9 collective-permute-start.2
  197.1 17.6 %collective-permute-done.2 = bf16[256,1152]{1,0:T(8,128)(2,1)} collective-permute-done((bf16[256,1152]{1,0:T(8,128)(2,1)}, bf16[256,1152]{1,0:T(8,128)(2,1)}, u32[]{:S(2)}, u32[]{:S(2)}) %collective-permute-start.2) | collective-permute-done | bytes 589856 | tf_op jit(solution)/shard_map/ppermute | solution.py:15
  214.6 13.3 %collective-permute-start.3 = (bf16[256,1152]{1,0:T(8,128)(2,1)}, bf16[256,1152]{1,0:T(8,128)(2,1)S(1)}, u32[]{:S(2)}, u32[]{:S(2)}) collective-permute-start(bf16[256,1152]{1,0:T(8,128)(2,1)} %collective-permute-done.2), channel_id=1, source_target_pairs={{1,0},{2,1},{3,2},{4,3},{5,4},{6,5},{7,6},{8,7},{9,8},{10,9},{11,1... | collective-permute-start | bytes 1769480 | tf_op jit(solution)/shard_map/ppermute | solution.py:15
  230.1 2.1 collective-permute-start.8
  232.7 1.5 convolution_add_fusion.5
  234.2 21.7 %collective-permute-done.3 = bf16[256,1152]{1,0:T(8,128)(2,1)S(1)} collective-permute-done((bf16[256,1152]{1,0:T(8,128)(2,1)}, bf16[256,1152]{1,0:T(8,128)(2,1)S(1)}, u32[]{:S(2)}, u32[]{:S(2)}) %collective-permute-start.3) | collective-permute-done | bytes 589856 | tf_op jit(solution)/shard_map/ppermute | solution.py:15
  255.9 14.4 %collective-permute-start.4 = (bf16[256,1152]{1,0:T(8,128)(2,1)S(1)}, bf16[256,1152]{1,0:T(8,128)(2,1)S(1)}, u32[]{:S(2)}, u32[]{:S(2)}) collective-permute-start(bf16[256,1152]{1,0:T(8,128)(2,1)S(1)} %collective-permute-done.3), channel_id=1, source_target_pairs={{1,0},{2,1},{3,2},{4,3},{5,4},{6,5},{7,6},{8,7},{9,8},{10,9},{11,1... | collective-permute-start | bytes 1769480 | tf_op jit(solution)/shard_map/ppermute | solution.py:15
  271.2 35.3 %collective-permute-done.8 = f32[256,1152]{1,0:T(8,128)S(1)} collective-permute-done((f32[256,1152]{1,0:T(8,128)S(1)}, f32[256,1152]{1,0:T(8,128)S(1)}, u32[]{:S(2)}, u32[]{:S(2)}) %collective-permute-start.8) | collective-permute-done | bytes 1179680 | tf_op jit(solution)/shard_map/ppermute | solution.py:15
  306.6 15.3 %collective-permute-start.9 = (f32[256,1152]{1,0:T(8,128)S(1)}, f32[256,1152]{1,0:T(8,128)S(1)}, u32[]{:S(2)}, u32[]{:S(2)}) collective-permute-start(f32[256,1152]{1,0:T(8,128)S(1)} %add.310), channel_id=1, source_target_pairs={{1,0},{2,1},{3,2},{4,3},{5,4},{6,5},{7,6},{8,7},{9,8},{10,9},{11,1... | collective-permute-start | bytes 3538952 | tf_op jit(solution)/shard_map/ppermute | solution.py:15
  323.4 1.5 convolution_add_fusion.3
  324.9 7.2 %collective-permute-done.4 = bf16[256,1152]{1,0:T(8,128)(2,1)S(1)} collective-permute-done((bf16[256,1152]{1,0:T(8,128)(2,1)S(1)}, bf16[256,1152]{1,0:T(8,128)(2,1)S(1)}, u32[]{:S(2)}, u32[]{:S(2)}) %collective-permute-start.4) | collective-permute-done | bytes 589856 | tf_op jit(solution)/shard_map/ppermute | solution.py:15
  332.2 2.7 multiply_reduce_fusion
  335.5 40.6 %collective-permute-done.9 = f32[256,1152]{1,0:T(8,128)S(1)} collective-permute-done((f32[256,1152]{1,0:T(8,128)S(1)}, f32[256,1152]{1,0:T(8,128)S(1)}, u32[]{:S(2)}, u32[]{:S(2)}) %collective-permute-start.9) | collective-permute-done | bytes 1179680 | tf_op jit(solution)/shard_map/ppermute | solution.py:15
  377.2 1.9 collective-permute-start.10
  390.9 166.0 %all-reduce = (f32[]{:T(128)}, f32[1]{0:T(128)}, f32[]{:T(128)}) all-reduce(f32[]{:T(128)S(6)} %add.322, f32[1]{0:T(128)} %bitcast.4, f32[]{:T(128)S(6)} %add.327), channel_id=1, replica_groups=mesh['outer'=8,'inner'=96] {'outer','inner'}, use_global_device_ids=true, to_apply=%region_10.11 | all-reduce | flops 3 | bytes 24 | tf_op jit(solution)/shard_map/psum | solution.py:89
  559.4 1.7 fusion.7
  (74 shorter events, 19.0 us)
Async XLA Ops:
  0.6 2.7 copy-start
  0.7 4.2 copy-start.1
  3.5 11.6 %copy-start.4 = (bf16[256,1152]{1,0:T(8,128)(2,1)}, bf16[256,1152]{1,0:T(8,128)(2,1)S(1)}, u32[]{:S(2)}) copy-start(bf16[256,1152]{1,0:T(8,128)(2,1)S(1)} %fusion.3) | copy-start | bytes 1769476
  6.8 97.1 %collective-permute-start.5 = (f32[256,1152]{1,0:T(8,128)}, f32[256,1152]{1,0:T(8,128)S(1)}, u32[]{:S(2)}, u32[]{:S(2)}) collective-permute-start(f32[256,1152]{1,0:T(8,128)} %fusion.41), channel_id=1, source_target_pairs={{95,0},{0,1},{1,2},{2,3},{3,4},{4,5},{5,6},{6,7},{7,8},{8,9},{9,10... | collective-permute-start | bytes 3538952 | tf_op jit(solution)/shard_map/ppermute | solution.py:15
  15.1 87.4 %collective-permute-start = (bf16[256,1152]{1,0:T(8,128)(2,1)S(1)}, bf16[256,1152]{1,0:T(8,128)(2,1)}, u32[]{:S(2)}, u32[]{:S(2)}) collective-permute-start(bf16[256,1152]{1,0:T(8,128)(2,1)S(1)} %fusion.3), channel_id=1, source_target_pairs={{95,0},{0,1},{1,2},{2,3},{3,4},{4,5},{5,6},{6,7},{7,8},{8,9},{9,10... | collective-permute-start | bytes 1769480 | tf_op jit(solution)/shard_map/ppermute | solution.py:15
  104.7 82.1 %collective-permute-start.6 = (f32[256,1152]{1,0:T(8,128)S(1)}, f32[256,1152]{1,0:T(8,128)S(1)}, u32[]{:S(2)}, u32[]{:S(2)}) collective-permute-start(f32[256,1152]{1,0:T(8,128)S(1)} %convolution_add_fusion), channel_id=1, source_target_pairs={{95,0},{0,1},{1,2},{2,3},{3,4},{4,5},{5,6},{6,7},{7,8},{8,9},{9,10... | collective-permute-start | bytes 3538952 | tf_op jit(solution)/shard_map/ppermute | solution.py:15
  106.6 78.1 %collective-permute-start.1 = (bf16[256,1152]{1,0:T(8,128)(2,1)}, bf16[256,1152]{1,0:T(8,128)(2,1)}, u32[]{:S(2)}, u32[]{:S(2)}) collective-permute-start(bf16[256,1152]{1,0:T(8,128)(2,1)} %collective-permute-done), channel_id=1, source_target_pairs={{95,0},{0,1},{1,2},{2,3},{3,4},{4,5},{5,6},{6,7},{7,8},{8,9},{9,10... | collective-permute-start | bytes 1769480 | tf_op jit(solution)/shard_map/ppermute | solution.py:15
  108.6 78.1 %copy-start.11 = (s32[256]{0:T(256)}, s32[256]{0:T(256)S(1)}, u32[]{:S(2)}) copy-start(s32[256]{0:T(256)S(1)} %iota_add_fusion.3) | copy-start | bytes 3076
  186.9 43.1 %collective-permute-start.7 = (f32[256,1152]{1,0:T(8,128)S(1)}, f32[256,1152]{1,0:T(8,128)S(1)}, u32[]{:S(2)}, u32[]{:S(2)}) collective-permute-start(f32[256,1152]{1,0:T(8,128)S(1)} %add.308), channel_id=1, source_target_pairs={{672,0},{0,96},{96,192},{192,288},{288,384},{384,480},{480,576},{5... | collective-permute-start | bytes 3538952 | tf_op jit(solution)/shard_map/ppermute | solution.py:15
  195.1 19.6 %collective-permute-start.2 = (bf16[256,1152]{1,0:T(8,128)(2,1)}, bf16[256,1152]{1,0:T(8,128)(2,1)}, u32[]{:S(2)}, u32[]{:S(2)}) collective-permute-start(bf16[256,1152]{1,0:T(8,128)(2,1)} %collective-permute-done.1), channel_id=1, source_target_pairs={{672,0},{0,96},{96,192},{192,288},{288,384},{384,480},{480,576},{5... | collective-permute-start | bytes 1769480 | tf_op jit(solution)/shard_map/ppermute | solution.py:15
  214.6 41.3 %collective-permute-start.3 = (bf16[256,1152]{1,0:T(8,128)(2,1)}, bf16[256,1152]{1,0:T(8,128)(2,1)S(1)}, u32[]{:S(2)}, u32[]{:S(2)}) collective-permute-start(bf16[256,1152]{1,0:T(8,128)(2,1)} %collective-permute-done.2), channel_id=1, source_target_pairs={{1,0},{2,1},{3,2},{4,3},{5,4},{6,5},{7,6},{8,7},{9,8},{10,9},{11,1... | collective-permute-start | bytes 1769480 | tf_op jit(solution)/shard_map/ppermute | solution.py:15
  230.0 2.3 copy-start.5
  230.0 2.3 copy-start.16
  230.0 2.3 copy-start.18
  230.1 2.6 copy-start.3
  230.1 76.3 %collective-permute-start.8 = (f32[256,1152]{1,0:T(8,128)S(1)}, f32[256,1152]{1,0:T(8,128)S(1)}, u32[]{:S(2)}, u32[]{:S(2)}) collective-permute-start(f32[256,1152]{1,0:T(8,128)S(1)} %add.309), channel_id=1, source_target_pairs={{1,0},{2,1},{3,2},{4,3},{5,4},{6,5},{7,6},{8,7},{9,8},{10,9},{11,1... | collective-permute-start | bytes 3538952 | tf_op jit(solution)/shard_map/ppermute | solution.py:15
  232.2 102.6 %copy-start.13 = (s32[256]{0:T(256)}, s32[256]{0:T(256)S(1)}, u32[]{:S(2)}) copy-start(s32[256]{0:T(256)S(1)} %iota_add_fusion) | copy-start | bytes 3076
  255.9 76.3 %collective-permute-start.4 = (bf16[256,1152]{1,0:T(8,128)(2,1)S(1)}, bf16[256,1152]{1,0:T(8,128)(2,1)S(1)}, u32[]{:S(2)}, u32[]{:S(2)}) collective-permute-start(bf16[256,1152]{1,0:T(8,128)(2,1)S(1)} %collective-permute-done.3), channel_id=1, source_target_pairs={{1,0},{2,1},{3,2},{4,3},{5,4},{6,5},{7,6},{8,7},{9,8},{10,9},{11,1... | collective-permute-start | bytes 1769480 | tf_op jit(solution)/shard_map/ppermute | solution.py:15
  271.2 50.7 %copy-start.8 = (f32[256,256]{1,0:T(8,128)S(1)}, f32[256,256]{1,0:T(8,128)}, u32[]{:S(2)}) copy-start(f32[256,256]{1,0:T(8,128)} %copy-done.7) | copy-start | bytes 786436
  271.2 50.7 %copy-start.12 = (s32[256]{0:T(256)S(1)}, s32[256]{0:T(256)}, u32[]{:S(2)}) copy-start(s32[256]{0:T(256)} %copy-done.11) | copy-start | bytes 3076
  306.6 69.5 %collective-permute-start.9 = (f32[256,1152]{1,0:T(8,128)S(1)}, f32[256,1152]{1,0:T(8,128)S(1)}, u32[]{:S(2)}, u32[]{:S(2)}) collective-permute-start(f32[256,1152]{1,0:T(8,128)S(1)} %add.310), channel_id=1, source_target_pairs={{1,0},{2,1},{3,2},{4,3},{5,4},{6,5},{7,6},{8,7},{9,8},{10,9},{11,1... | collective-permute-start | bytes 3538952 | tf_op jit(solution)/shard_map/ppermute | solution.py:15
  332.1 2.7 copy-start.6
  377.2 185.1 %collective-permute-start.10 = (f32[256,1152]{1,0:T(8,128)}, f32[256,1152]{1,0:T(8,128)S(1)}, u32[]{:S(2)}, u32[]{:S(2)}) collective-permute-start(f32[256,1152]{1,0:T(8,128)} %add.311), channel_id=1, source_target_pairs={{96,0},{192,96},{288,192},{384,288},{480,384},{576,480},{672,576},... | collective-permute-start | bytes 3538952 | tf_op jit(solution)/shard_map/ppermute | solution.py:15
  379.1 180.2 %copy-start.14 = (s32[256]{0:T(256)S(1)}, s32[256]{0:T(256)}, u32[]{:S(2)}) copy-start(s32[256]{0:T(256)} %copy-done.13) | copy-start | bytes 3076
  (6 other events, 7.6 us)
where the time goes:
time: 568 us; the launch traced here: 565 us
  waiting for transfers between devices  283 us (50%)
  blocking collectives  166 us (29%)
  starting transfers between devices  71.8 us (13%)
  matrix products  18.9 us (3%)
  between operations  16.3 us (3%)
  other arithmetic  8.34 us (1%)
    ppermute x11, waiting for transfers between devices, passed_along(): return lax.ppermute(block, axis, route)  283 us
    psum x1, blocking collectives, shards(): lax.psum((loss_sum, slope_cos_sum, slope_total), ('outer', 'inner'))  166 us
    ppermute x11, starting transfers between devices, passed_along(): return lax.ppermute(block, axis, route)  71.8 us
  transfers between devices with their start and end apart: 11, of which 7 were waited for; matrix products, arithmetic and copies ran while one was open for 3% of the time, Pallas kernels for 0%

commit v1 on v0

v1 whole, which is shorter than its diff:
```python
import functools

import jax
import jax.numpy as jnp
from jax import lax
from jax.experimental import pallas as pl
from jax.experimental.pallas import tpu as pltpu
from jax.sharding import PartitionSpec as P

IN_SPAN = 3
NORM_EPS = 1e-06
AXES = ("outer", "inner")
SEND_SCALE = 64.0
VMEM_LIMIT = 48 * 1024 * 1024


def moved(block, outer_step, inner_step):
    n_outer, n_inner = lax.axis_size("outer"), lax.axis_size("inner")
    route = [
        (o * n_inner + p, (o + outer_step) % n_outer * n_inner + (p + inner_step) % n_inner)
        for o in range(n_outer)
        for p in range(n_inner)
    ]
    return lax.ppermute(block, AXES, route)


def unit_of(ref):
    values = ref[...].astype(jnp.float32)
    inv = lax.rsqrt(jnp.sum(values * values, axis=-1, keepdims=True) + NORM_EPS)
    return (values * inv).astype(jnp.bfloat16)


def score(img, txt, pos, text_start, head, stats):
    cosine = lax.dot_general(
        img, txt, (((1,), (1,)), ((), ())), preferred_element_type=jnp.float32
    )
    logit = head[0] * cosine + head[1]
    ids = text_start + lax.broadcasted_iota(jnp.int32, cosine.shape, 1)
    hit = pos == ids
    z = jnp.where(hit, -logit, logit)
    tail = jnp.exp(-jnp.abs(z))
    loss = jnp.maximum(z, 0.0) + jnp.log1p(tail)
    sig = jnp.where(z >= 0.0, 1.0, tail) / (1.0 + tail)
    slope = jnp.where(hit, -sig, sig)
    for row, term in enumerate((loss, slope * cosine, slope)):
        col = jnp.sum(term, axis=0, keepdims=True)
        width = stats.shape[1]
        part = col[:, :width]
        for at in range(width, col.shape[1], width):
            part = part + col[:, at : at + width]
        stats[row : row + 1, :] += part
    return slope.astype(jnp.bfloat16)


def times(a, b):
    return jnp.dot(a, b, preferred_element_type=jnp.float32)


def times_t(a, b):
    return lax.dot_general(a, b, (((0,), (0,)), ((), ())), preferred_element_type=jnp.float32)


def first_kernel(head, start, img_raw, txt_raw, pos, img_u, txt_u, img_acc, txt_acc, stats):
    stats[...] = jnp.zeros_like(stats)
    img_u[...] = unit_of(img_raw)
    txt_u[...] = unit_of(txt_raw)
    s = score(img_u[...], txt_u[...], pos[...], start[0], head, stats)
    img_acc[...] = times(s, txt_u[...])
    txt_acc[...] = times_t(s, img_u[...])


def second_kernel(
    head, start, img_u, txt_u, far_raw, img2_raw, pos, pos2, img_in, txt_in, stats_in,
    img2_u, img_acc, img2_acc, txt_acc, far_acc, stats,
):
    stats[...] = stats_in[...]
    img2_u[...] = unit_of(img2_raw)
    far = unit_of(far_raw)
    s = score(img_u[...], far, pos[...], start[2], head, stats)
    s2 = score(img2_u[...], far, pos2[...], start[2], head, stats)
    s0 = score(img2_u[...], txt_u[...], pos2[...], start[0], head, stats)
    far_acc[...] = times_t(s, img_u[...]) + times_t(s2, img2_u[...])
    img_acc[...] = img_in[...] + times(s, far)
    img2_acc[...] = times(s2, far) + times(s0, txt_u[...])
    txt_acc[...] = txt_in[...] + times_t(s0, img2_u[...])


def third_kernel(
    head, start, img_u, img2_u, mid_raw, pos, pos2, img_in, img2_in, stats_in,
    img_acc, img2_acc, mid_acc, stats,
):
    stats[...] = stats_in[...]
    mid = unit_of(mid_raw)
    s = score(img_u[...], mid, pos[...], start[1], head, stats)
    s2 = score(img2_u[...], mid, pos2[...], start[1], head, stats)
    mid_acc[...] = SEND_SCALE * (times_t(s, img_u[...]) + times_t(s2, img2_u[...]))
    img_acc[...] = img_in[...] + times(s, mid)
    img2_acc[...] = SEND_SCALE * (img2_in[...] + times(s2, mid))


def finish(raw, total, temp):
    values = raw[...].astype(jnp.float32)
    inv = lax.rsqrt(jnp.sum(values * values, axis=-1, keepdims=True) + NORM_EPS)
    unit = values * inv
    grad = temp * total
    return inv * (grad - unit * jnp.sum(unit * grad, axis=-1, keepdims=True))


def call(kernel, ins, outs):
    scalars = [pl.BlockSpec(memory_space=pltpu.SMEM)] * 2
    arrays = [pl.BlockSpec(memory_space=pltpu.VMEM)] * (len(ins) - 2)
    return pl.pallas_call(
        kernel,
        in_specs=scalars + arrays,
        out_specs=[pl.BlockSpec(memory_space=pltpu.VMEM)] * len(outs),
        out_shape=outs,
        compiler_params=pltpu.CompilerParams(vmem_limit_bytes=VMEM_LIMIT),
    )(*ins)


def total_over_devices(s):
    n_outer, n_inner = lax.axis_size("outer"), lax.axis_size("inner")
    step = n_outer // 2
    while step:
        s = s + moved(s, step, 0)
        step //= 2
    third = n_inner // 3
    group = lax.axis_index("inner") // third
    parts = [s, moved(s, 0, third), moved(s, 0, 2 * third)]
    ordered = [
        jnp.where(group == g, parts[0], jnp.where((group - 1) % 3 == g, parts[1], parts[2]))
        for g in range(3)
    ]
    s = ordered[0] + ordered[1] + ordered[2]
    step = third // 2
    while step:
        s = s + moved(s, 0, step)
        step //= 2
    return s


def shards(image_emb, text_emb, positive, log_scale, logit_bias):
    rows, width = image_emb.shape
    n_outer, n_inner = lax.axis_size("outer"), lax.axis_size("inner")
    f32, bf16 = jnp.float32, jnp.bfloat16
    temp_scale = jnp.exp(log_scale[0])
    head = jnp.stack([temp_scale, logit_bias[0]])
    outer_pos, inner_pos = lax.axis_index("outer"), lax.axis_index("inner")
    start = jnp.stack(
        [(outer_pos * n_inner + (inner_pos - b) % n_inner) * rows for b in range(IN_SPAN)]
    ).astype(jnp.int32)
    pos = positive.reshape(rows, 1)

    mid_raw = moved(text_emb, 0, 1)
    img2_raw = moved(image_emb, -1, 0)
    far_raw = moved(text_emb, 0, 2)
    pos2 = moved(positive, -1, 0).reshape(rows, 1)

    wide = jax.ShapeDtypeStruct((rows, width), f32)
    unit = jax.ShapeDtypeStruct((rows, width), bf16)
    sums = jax.ShapeDtypeStruct((8, 128), f32)
    img_u, txt_u, img_acc, txt_acc, stats = call(
        first_kernel, (head, start, image_emb, text_emb, pos), [unit, unit, wide, wide, sums]
    )
    img2_u, img_acc, img2_acc, txt_acc, far_acc, stats = call(
        second_kernel,
        (head, start, img_u, txt_u, far_raw, img2_raw, pos, pos2, img_acc, txt_acc, stats),
        [unit, wide, wide, wide, wide, sums],
    )
    far_back = moved(far_acc, 0, -2)
    img_acc, img2_acc, mid_acc, stats = call(
        third_kernel,
        (head, start, img_u, img2_u, mid_raw, pos, pos2, img_acc, img2_acc, stats),
        [wide, wide, wide, sums],
    )
    mid_back = moved(mid_acc.astype(jnp.float16), 0, -1)
    img_back = moved(img2_acc.astype(jnp.float16), 1, 0)
    totals = jnp.sum(total_over_devices(stats), axis=1)

    img_total = img_acc + img_back.astype(f32) * (1.0 / SEND_SCALE)
    txt_total = txt_acc + far_back + mid_back.astype(f32) * (1.0 / SEND_SCALE)
    image_grad = finish(image_emb, img_total, temp_scale)
    text_grad = finish(text_emb, txt_total, temp_scale)
    pair_count = f32(rows * n_outer * n_inner * 2 * IN_SPAN * rows)
    loss = (totals[0] / pair_count).reshape(1)
    head_grad = jnp.stack([temp_scale * totals[1], totals[2]]) / pair_count
    return (image_grad, text_grad, loss, head_grad)


def solution(mesh):
    return jax.shard_map(
        shards,
        mesh=mesh,
        in_specs=(P(AXES, None), P(AXES, None), P(AXES), P(), P()),
        out_specs=(P(AXES, None), P(AXES, None), P(), P()),
        check_vma=False,
    )
```

time: 568 us -> 182 us (0.32)
  the two profiles are of different devices: /device:TPU:1 before, /device:TPU:255 now
where the time goes in v1:
time: 182 us; the launch traced here: 181 us
  starting transfers between devices  92.5 us (51%)
  waiting for transfers between devices  49.1 us (27%)
  other arithmetic  13.1 us (7%)
  Pallas kernels  11.3 us (6%)
  local copies, waits for them, and re-layouts  9.74 us (5%)
  between operations  4.82 us (3%)
    ppermute x17, starting transfers between devices, moved(): return lax.ppermute(block, AXES, route)  92.5 us
    ppermute x17, waiting for transfers between devices, moved(): return lax.ppermute(block, AXES, route)  49.1 us
    pallas_call x3, Pallas kernels, call(): pl.pallas_call(kernel, in_specs=scalars + arrays, out_specs=[pl.BlockSpec...  11.3 us
    unnamed x24, local copies, waits for them, and re-layouts  8.21 us
    mul x2, other arithmetic, finish(): return inv * (grad - unit * jnp.sum(unit * grad, axis=-1, keepdims=True))  5.06 us
  transfers between devices with their start and end apart: 17, of which 8 were waited for; matrix products, arithmetic and copies ran while one was open for 6% of the time, Pallas kernels for 4%

profile of v1, /device:TPU:255, one launch (start us, length us, event | category | flops | bytes accessed | tf_op | source)
XLA Modules:
  0.0 180.6 jit_solution(268969478812388362)
XLA Ops:
  0.6 5.1 %collective-permute-start = (bf16[256,1152]{1,0:T(8,128)(2,1)}, bf16[256,1152]{1,0:T(8,128)(2,1)S(1)}, u32[]{:S(2)}, u32[]{:S(2)}) collective-permute-start(bf16[256,1152]{1,0:T(8,128)(2,1)} %txt_raw.1), channel_id=1, source_target_pairs={{0,2},{1,3},{2,4},{3,5},{4,6},{5,7},{6,8},{7,9},{8,10},{9,11},{10,... | collective-permute-start | bytes 1769480 | tf_op jit(solution)/shard_map/ppermute | solution.py:24
  5.8 2.9 %collective-permute-start.1 = (bf16[256,1152]{1,0:T(8,128)(2,1)}, bf16[256,1152]{1,0:T(8,128)(2,1)S(1)}, u32[]{:S(2)}, u32[]{:S(2)}) collective-permute-start(bf16[256,1152]{1,0:T(8,128)(2,1)} %img_raw.1), channel_id=1, source_target_pairs={{0,672},{1,673},{2,674},{3,675},{4,676},{5,677},{6,678},{7,679},{8... | collective-permute-start | bytes 1769480 | tf_op jit(solution)/shard_map/ppermute | solution.py:24
  8.6 5.4 %collective-permute-start.3 = (bf16[256,1152]{1,0:T(8,128)(2,1)}, bf16[256,1152]{1,0:T(8,128)(2,1)S(1)}, u32[]{:S(2)}, u32[]{:S(2)}) collective-permute-start(bf16[256,1152]{1,0:T(8,128)(2,1)} %txt_raw.1), channel_id=1, source_target_pairs={{0,1},{1,2},{2,3},{3,4},{4,5},{5,6},{6,7},{7,8},{8,9},{9,10},{10,1... | collective-permute-start | bytes 1769480 | tf_op jit(solution)/shard_map/ppermute | solution.py:24
  14.0 2.2 %collective-permute-start.2 = (s32[256]{0:T(256)}, s32[256]{0:T(256)S(1)}, u32[]{:S(2)}, u32[]{:S(2)}) collective-permute-start(s32[256]{0:T(256)} %param.7), channel_id=1, source_target_pairs={{0,672},{1,673},{2,674},{3,675},{4,676},{5,677},{6,678},{7,679},{8... | collective-permute-start | bytes 3080 | tf_op jit(solution)/shard_map/ppermute | solution.py:24
  20.7 2.1 %shard_map.84 = (bf16[256,1152]{1,0:T(8,128)(2,1)S(1)}, bf16[256,1152]{1,0:T(8,128)(2,1)S(1)}, f32[256,1152]{1,0:T(8,128)S(1)}, f32[256,1152]{1,0:T(8,128)S(1)}, f32[8,128]{1,0:T(8,128)S(1)}) custom-call(f32[2]{0:T(128)S(1)} %pad_maximum_fusion.head, s32[3]{0:T(128)S(1)} %pad_add_fusion.start, bf16[256,1152]{1,0:T(8,128)(2,1)S(1)} %copy-done.2, ...), custom_call_target="tpu_custom_call" | custom-call | tf_op jit(solution)/shard_map/pallas_call | solution.py:112
  25.0 5.5 %shard_map.85 = (bf16[256,1152]{1,0:T(8,128)(2,1)S(1)}, f32[256,1152]{1,0:T(8,128)S(1)}, f32[256,1152]{1,0:T(8,128)S(1)}, f32[256,1152]{1,0:T(8,128)}, f32[256,1152]{1,0:T(8,128)}, /*index=5*/f32[8,128]{1,0:T(8,128)S(1)}) custom-call(f32[2]{0:T(128)S(1)} %pad_maximum_fusion.head, s32[3]{0:T(128)S(1)} %pad_add_fusion.start, ...), custom_call_target="tpu_custom_call" | custom-call | tf_op jit(solution)/shard_map/pallas_call | solution.py:112
  32.6 5.5 %collective-permute-done.3.mid_raw = bf16[256,1152]{1,0:T(8,128)(2,1)S(1)} collective-permute-done((bf16[256,1152]{1,0:T(8,128)(2,1)}, bf16[256,1152]{1,0:T(8,128)(2,1)S(1)}, u32[]{:S(2)}, u32[]{:S(2)}) %collective-permute-start.3) | collective-permute-done | bytes 589856 | tf_op jit(solution)/shard_map/ppermute | solution.py:24
  38.1 3.7 %shard_map.86 = (f32[256,1152]{1,0:T(8,128)S(1)}, f32[256,1152]{1,0:T(8,128)S(1)}, f32[256,1152]{1,0:T(8,128)S(1)}, f32[8,128]{1,0:T(8,128)S(1)}) custom-call(f32[2]{0:T(128)S(1)} %pad_maximum_fusion.head, s32[3]{0:T(128)S(1)} %pad_add_fusion.start, bf16[256,1152]{1,0:T(8,128)(2,1)S(1)} %get-tuple-element.19.img_u, ...), custom_call_target="tpu_custom_call" | custom-call | tf_op jit(solution)/shard_map/pallas_call | solution.py:112
  43.8 7.7 %collective-permute-start.7 = (f32[8,128]{1,0:T(8,128)S(1)}, f32[8,128]{1,0:T(8,128)S(1)}, u32[]{:S(2)}, u32[]{:S(2)}) collective-permute-start(f32[8,128]{1,0:T(8,128)S(1)} %get-tuple-element.33), channel_id=1, source_target_pairs={{0,384},{1,385},{2,386},{3,387},{4,388},{5,389},{6,390},{7,391},{8... | collective-permute-start | bytes 12296 | tf_op jit(solution)/shard_map/ppermute | solution.py:24
  52.5 13.3 %collective-permute-start.8 = (f32[8,128]{1,0:T(8,128)S(1)}, f32[8,128]{1,0:T(8,128)S(1)}, u32[]{:S(2)}, u32[]{:S(2)}) collective-permute-start(f32[8,128]{1,0:T(8,128)S(1)} %add.94), channel_id=1, source_target_pairs={{0,192},{1,193},{2,194},{3,195},{4,196},{5,197},{6,198},{7,199},{8... | collective-permute-start | bytes 12296 | tf_op jit(solution)/shard_map/ppermute | solution.py:24
  66.5 3.8 %collective-permute-start.9 = (f32[8,128]{1,0:T(8,128)S(1)}, f32[8,128]{1,0:T(8,128)S(1)}, u32[]{:S(2)}, u32[]{:S(2)}) collective-permute-start(f32[8,128]{1,0:T(8,128)S(1)} %add.95), channel_id=1, source_target_pairs={{0,96},{1,97},{2,98},{3,99},{4,100},{5,101},{6,102},{7,103},{8,104... | collective-permute-start | bytes 12296 | tf_op jit(solution)/shard_map/ppermute | solution.py:24
  71.0 7.4 %collective-permute-start.10 = (f32[8,128]{1,0:T(8,128)S(1)}, f32[8,128]{1,0:T(8,128)S(1)}, u32[]{:S(2)}, u32[]{:S(2)}) collective-permute-start(f32[8,128]{1,0:T(8,128)S(1)} %add.96), channel_id=1, source_target_pairs={{0,32},{1,33},{2,34},{3,35},{4,36},{5,37},{6,38},{7,39},{8,40},{9,... | collective-permute-start | bytes 12296 | tf_op jit(solution)/shard_map/ppermute | solution.py:24
  78.4 3.2 %collective-permute-start.11 = (f32[8,128]{1,0:T(8,128)S(1)}, f32[8,128]{1,0:T(8,128)S(1)}, u32[]{:S(2)}, u32[]{:S(2)}) collective-permute-start(f32[8,128]{1,0:T(8,128)S(1)} %add.96), channel_id=1, source_target_pairs={{0,64},{1,65},{2,66},{3,67},{4,68},{5,69},{6,70},{7,71},{8,72},{9,... | collective-permute-start | bytes 12296 | tf_op jit(solution)/shard_map/ppermute | solution.py:24
  81.7 5.0 %collective-permute-done.11 = f32[8,128]{1,0:T(8,128)S(1)} collective-permute-done((f32[8,128]{1,0:T(8,128)S(1)}, f32[8,128]{1,0:T(8,128)S(1)}, u32[]{:S(2)}, u32[]{:S(2)}) %collective-permute-start.11) | collective-permute-done | bytes 4128 | tf_op jit(solution)/shard_map/ppermute | solution.py:24
  86.7 4.0 %collective-permute-start.12 = (f32[8,128]{1,0:T(8,128)S(1)}, f32[8,128]{1,0:T(8,128)S(1)}, u32[]{:S(2)}, u32[]{:S(2)}) collective-permute-start(f32[8,128]{1,0:T(8,128)S(1)} %select_add_fusion), channel_id=1, source_target_pairs={{0,16},{1,17},{2,18},{3,19},{4,20},{5,21},{6,22},{7,23},{8,24},{9,... | collective-permute-start | bytes 12296 | tf_op jit(solution)/shard_map/ppermute | solution.py:24
  91.9 5.7 %collective-permute-start.13 = (f32[8,128]{1,0:T(8,128)S(1)}, f32[8,128]{1,0:T(8,128)S(1)}, u32[]{:S(2)}, u32[]{:S(2)}) collective-permute-start(f32[8,128]{1,0:T(8,128)S(1)} %add.100), channel_id=1, source_target_pairs={{0,8},{1,9},{2,10},{3,11},{4,12},{5,13},{6,14},{7,15},{8,16},{9,17... | collective-permute-start | bytes 12296 | tf_op jit(solution)/shard_map/ppermute | solution.py:24
  98.4 5.8 %collective-permute-start.14 = (f32[8,128]{1,0:T(8,128)S(1)}, f32[8,128]{1,0:T(8,128)S(1)}, u32[]{:S(2)}, u32[]{:S(2)}) collective-permute-start(f32[8,128]{1,0:T(8,128)S(1)} %add.101), channel_id=1, source_target_pairs={{0,4},{1,5},{2,6},{3,7},{4,8},{5,9},{6,10},{7,11},{8,12},{9,13},{1... | collective-permute-start | bytes 12296 | tf_op jit(solution)/shard_map/ppermute | solution.py:24
  104.3 2.3 %convert_element_type.19 = f16[256,1152]{1,0:T(8,128)(2,1)} convert(f32[256,1152]{1,0:T(8,128)} %copy-done.6) | non-fusion elementwise | flops 294912 | bytes 1769472 | tf_op jit(solution)/shard_map/convert_element_type | solution.py:177
  106.5 10.0 %collective-permute-start.4 = (f16[256,1152]{1,0:T(8,128)(2,1)}, f16[256,1152]{1,0:T(8,128)(2,1)}, u32[]{:S(2)}, u32[]{:S(2)}) collective-permute-start(f16[256,1152]{1,0:T(8,128)(2,1)} %convert_element_type.19), channel_id=1, source_target_pairs={{0,96},{1,97},{2,98},{3,99},{4,100},{5,101},{6,102},{7,103},{8,104... | collective-permute-start | bytes 1769480 | tf_op jit(solution)/shard_map/ppermute | solution.py:24
  116.6 3.4 %collective-permute-start.15 = (f32[8,128]{1,0:T(8,128)S(1)}, f32[8,128]{1,0:T(8,128)S(1)}, u32[]{:S(2)}, u32[]{:S(2)}) collective-permute-start(f32[8,128]{1,0:T(8,128)S(1)} %add.102), channel_id=1, source_target_pairs={{0,2},{1,3},{2,4},{3,5},{4,6},{5,7},{6,8},{7,9},{8,10},{9,11},{10,... | collective-permute-start | bytes 12296 | tf_op jit(solution)/shard_map/ppermute | solution.py:24
  122.1 8.9 %collective-permute-start.16 = (f32[8,128]{1,0:T(8,128)S(1)}, f32[8,128]{1,0:T(8,128)S(1)}, u32[]{:S(2)}, u32[]{:S(2)}) collective-permute-start(f32[8,128]{1,0:T(8,128)S(1)} %add.103), channel_id=1, source_target_pairs={{0,1},{1,2},{2,3},{3,4},{4,5},{5,6},{6,7},{7,8},{8,9},{9,10},{10,1... | collective-permute-start | bytes 12296 | tf_op jit(solution)/shard_map/ppermute | solution.py:24
  138.6 2.5 %fusion.9 = f32[256,1152]{1,0:T(8,128)} fusion(bf16[256,1152]{1,0:T(8,128)(2,1)S(1)} %copy-done.3, f32[256,1152]{1,0:T(8,128)S(1)} %get-tuple-element.28, f16[256,1152]{1,0:T(8,128)(2,1)} %collective-permute-done.4, f32[256]{0:T(256)S(1)} %fusion.7, f32[]{:T(128)} %bitcast, f32[256]{0:T(256)S(1)} %add_rsqrt_fusion.1), kind=kLoop, calls=%fused_computation.13 | loop fusion | flops 2654208 | bytes 3540996 | tf_op jit(solution)/shard_map/mul | solution.py:106
  141.1 34.3 %collective-permute-done.6 = f16[256,1152]{1,0:T(8,128)(2,1)} collective-permute-done((f16[256,1152]{1,0:T(8,128)(2,1)}, f16[256,1152]{1,0:T(8,128)(2,1)}, u32[]{:S(2)}, u32[]{:S(2)}) %collective-permute-start.6) | collective-permute-done | bytes 589856 | tf_op jit(solution)/shard_map/ppermute | solution.py:24
  176.9 2.5 %fusion.6 = f32[256,1152]{1,0:T(8,128)} fusion(bf16[256,1152]{1,0:T(8,128)(2,1)S(1)} %copy-done.1, f32[256]{0:T(256)S(1)} %fusion.4, f32[256]{0:T(256)S(1)} %add_rsqrt_fusion, f16[256,1152]{1,0:T(8,128)(2,1)} %collective-permute-done.6, f32[256,1152]{1,0:T(8,128)S(1)} %copy-done.11, f32[256,1152]{1,0:T(8,128)S(1)} %collective-permute-done.5, f32[]{:T(128)} %bitcast), kind=kLoop, calls=%fused_computation.10 | loop fusion | flops 2949120 | bytes 4720644 | tf_op jit(solution)/shard_map/mul | solution.py:106
  (62 shorter events, 23.6 us)
Async XLA Ops:
  0.6 24.4 %collective-permute-start = (bf16[256,1152]{1,0:T(8,128)(2,1)}, bf16[256,1152]{1,0:T(8,128)(2,1)S(1)}, u32[]{:S(2)}, u32[]{:S(2)}) collective-permute-start(bf16[256,1152]{1,0:T(8,128)(2,1)} %txt_raw.1), channel_id=1, source_target_pairs={{0,2},{1,3},{2,4},{3,5},{4,6},{5,7},{6,8},{7,9},{8,10},{9,11},{10,... | collective-permute-start | bytes 1769480 | tf_op jit(solution)/shard_map/ppermute | solution.py:24
  5.8 19.2 %collective-permute-start.1 = (bf16[256,1152]{1,0:T(8,128)(2,1)}, bf16[256,1152]{1,0:T(8,128)(2,1)S(1)}, u32[]{:S(2)}, u32[]{:S(2)}) collective-permute-start(bf16[256,1152]{1,0:T(8,128)(2,1)} %img_raw.1), channel_id=1, source_target_pairs={{0,672},{1,673},{2,674},{3,675},{4,676},{5,677},{6,678},{7,679},{8... | collective-permute-start | bytes 1769480 | tf_op jit(solution)/shard_map/ppermute | solution.py:24
  8.6 29.5 %collective-permute-start.3 = (bf16[256,1152]{1,0:T(8,128)(2,1)}, bf16[256,1152]{1,0:T(8,128)(2,1)S(1)}, u32[]{:S(2)}, u32[]{:S(2)}) collective-permute-start(bf16[256,1152]{1,0:T(8,128)(2,1)} %txt_raw.1), channel_id=1, source_target_pairs={{0,1},{1,2},{2,3},{3,4},{4,5},{5,6},{6,7},{7,8},{8,9},{9,10},{10,1... | collective-permute-start | bytes 1769480 | tf_op jit(solution)/shard_map/ppermute | solution.py:24
  14.0 10.8 %collective-permute-start.2 = (s32[256]{0:T(256)}, s32[256]{0:T(256)S(1)}, u32[]{:S(2)}, u32[]{:S(2)}) collective-permute-start(s32[256]{0:T(256)} %param.7), channel_id=1, source_target_pairs={{0,672},{1,673},{2,674},{3,675},{4,676},{5,677},{6,678},{7,679},{8... | collective-permute-start | bytes 3080 | tf_op jit(solution)/shard_map/ppermute | solution.py:24
  18.6 1.1 copy-start
  19.7 1.1 copy-start.2
  38.1 59.6 %copy-start.1 = (bf16[256,1152]{1,0:T(8,128)(2,1)S(1)}, bf16[256,1152]{1,0:T(8,128)(2,1)}, u32[]{:S(2)}) copy-start(bf16[256,1152]{1,0:T(8,128)(2,1)} %txt_raw.1) | copy-start | bytes 1769476
  41.8 1.0 copy-start.4
  43.8 8.6 %collective-permute-start.7 = (f32[8,128]{1,0:T(8,128)S(1)}, f32[8,128]{1,0:T(8,128)S(1)}, u32[]{:S(2)}, u32[]{:S(2)}) collective-permute-start(f32[8,128]{1,0:T(8,128)S(1)} %get-tuple-element.33), channel_id=1, source_target_pairs={{0,384},{1,385},{2,386},{3,387},{4,388},{5,389},{6,390},{7,391},{8... | collective-permute-start | bytes 12296 | tf_op jit(solution)/shard_map/ppermute | solution.py:24
  52.5 14.0 %collective-permute-start.8 = (f32[8,128]{1,0:T(8,128)S(1)}, f32[8,128]{1,0:T(8,128)S(1)}, u32[]{:S(2)}, u32[]{:S(2)}) collective-permute-start(f32[8,128]{1,0:T(8,128)S(1)} %add.94), channel_id=1, source_target_pairs={{0,192},{1,193},{2,194},{3,195},{4,196},{5,197},{6,198},{7,199},{8... | collective-permute-start | bytes 12296 | tf_op jit(solution)/shard_map/ppermute | solution.py:24
  66.5 4.6 %collective-permute-start.9 = (f32[8,128]{1,0:T(8,128)S(1)}, f32[8,128]{1,0:T(8,128)S(1)}, u32[]{:S(2)}, u32[]{:S(2)}) collective-permute-start(f32[8,128]{1,0:T(8,128)S(1)} %add.95), channel_id=1, source_target_pairs={{0,96},{1,97},{2,98},{3,99},{4,100},{5,101},{6,102},{7,103},{8,104... | collective-permute-start | bytes 12296 | tf_op jit(solution)/shard_map/ppermute | solution.py:24
  71.0 10.6 %collective-permute-start.10 = (f32[8,128]{1,0:T(8,128)S(1)}, f32[8,128]{1,0:T(8,128)S(1)}, u32[]{:S(2)}, u32[]{:S(2)}) collective-permute-start(f32[8,128]{1,0:T(8,128)S(1)} %add.96), channel_id=1, source_target_pairs={{0,32},{1,33},{2,34},{3,35},{4,36},{5,37},{6,38},{7,39},{8,40},{9,... | collective-permute-start | bytes 12296 | tf_op jit(solution)/shard_map/ppermute | solution.py:24
  78.4 8.3 %collective-permute-start.11 = (f32[8,128]{1,0:T(8,128)S(1)}, f32[8,128]{1,0:T(8,128)S(1)}, u32[]{:S(2)}, u32[]{:S(2)}) collective-permute-start(f32[8,128]{1,0:T(8,128)S(1)} %add.96), channel_id=1, source_target_pairs={{0,64},{1,65},{2,66},{3,67},{4,68},{5,69},{6,70},{7,71},{8,72},{9,... | collective-permute-start | bytes 12296 | tf_op jit(solution)/shard_map/ppermute | solution.py:24
  86.7 5.2 %collective-permute-start.12 = (f32[8,128]{1,0:T(8,128)S(1)}, f32[8,128]{1,0:T(8,128)S(1)}, u32[]{:S(2)}, u32[]{:S(2)}) collective-permute-start(f32[8,128]{1,0:T(8,128)S(1)} %select_add_fusion), channel_id=1, source_target_pairs={{0,16},{1,17},{2,18},{3,19},{4,20},{5,21},{6,22},{7,23},{8,24},{9,... | collective-permute-start | bytes 12296 | tf_op jit(solution)/shard_map/ppermute | solution.py:24
  91.9 28.1 %copy-start.3 = (bf16[256,1152]{1,0:T(8,128)(2,1)S(1)}, bf16[256,1152]{1,0:T(8,128)(2,1)}, u32[]{:S(2)}) copy-start(bf16[256,1152]{1,0:T(8,128)(2,1)} %img_raw.1) | copy-start | bytes 1769476
  91.9 6.5 %collective-permute-start.13 = (f32[8,128]{1,0:T(8,128)S(1)}, f32[8,128]{1,0:T(8,128)S(1)}, u32[]{:S(2)}, u32[]{:S(2)}) collective-permute-start(f32[8,128]{1,0:T(8,128)S(1)} %add.100), channel_id=1, source_target_pairs={{0,8},{1,9},{2,10},{3,11},{4,12},{5,13},{6,14},{7,15},{8,16},{9,17... | collective-permute-start | bytes 12296 | tf_op jit(solution)/shard_map/ppermute | solution.py:24
  98.4 18.1 %collective-permute-start.14 = (f32[8,128]{1,0:T(8,128)S(1)}, f32[8,128]{1,0:T(8,128)S(1)}, u32[]{:S(2)}, u32[]{:S(2)}) collective-permute-start(f32[8,128]{1,0:T(8,128)S(1)} %add.101), channel_id=1, source_target_pairs={{0,4},{1,5},{2,6},{3,7},{4,8},{5,9},{6,10},{7,11},{8,12},{9,13},{1... | collective-permute-start | bytes 12296 | tf_op jit(solution)/shard_map/ppermute | solution.py:24
  104.3 26.8 %copy-start.5 = (f32[256,1152]{1,0:T(8,128)S(1)}, f32[256,1152]{1,0:T(8,128)}, u32[]{:S(2)}) copy-start(f32[256,1152]{1,0:T(8,128)} %copy-done.4) | copy-start | bytes 3538948
  106.5 30.6 %collective-permute-start.4 = (f16[256,1152]{1,0:T(8,128)(2,1)}, f16[256,1152]{1,0:T(8,128)(2,1)}, u32[]{:S(2)}, u32[]{:S(2)}) collective-permute-start(f16[256,1152]{1,0:T(8,128)(2,1)} %convert_element_type.19), channel_id=1, source_target_pairs={{0,96},{1,97},{2,98},{3,99},{4,100},{5,101},{6,102},{7,103},{8,104... | collective-permute-start | bytes 1769480 | tf_op jit(solution)/shard_map/ppermute | solution.py:24
  116.6 5.6 %collective-permute-start.15 = (f32[8,128]{1,0:T(8,128)S(1)}, f32[8,128]{1,0:T(8,128)S(1)}, u32[]{:S(2)}, u32[]{:S(2)}) collective-permute-start(f32[8,128]{1,0:T(8,128)S(1)} %add.102), channel_id=1, source_target_pairs={{0,2},{1,3},{2,4},{3,5},{4,6},{5,7},{6,8},{7,9},{8,10},{9,11},{10,... | collective-permute-start | bytes 12296 | tf_op jit(solution)/shard_map/ppermute | solution.py:24
  120.2 55.2 %collective-permute-start.5 = (f32[256,1152]{1,0:T(8,128)}, f32[256,1152]{1,0:T(8,128)S(1)}, u32[]{:S(2)}, u32[]{:S(2)}) collective-permute-start(f32[256,1152]{1,0:T(8,128)} %get-tuple-element.31), channel_id=1, source_target_pairs={{0,94},{1,95},{2,0},{3,1},{4,2},{5,3},{6,4},{7,5},{8,6},{9,7},{10,... | collective-permute-start | bytes 3538952 | tf_op jit(solution)/shard_map/ppermute | solution.py:24
  122.1 11.7 %collective-permute-start.16 = (f32[8,128]{1,0:T(8,128)S(1)}, f32[8,128]{1,0:T(8,128)S(1)}, u32[]{:S(2)}, u32[]{:S(2)}) collective-permute-start(f32[8,128]{1,0:T(8,128)S(1)} %add.103), channel_id=1, source_target_pairs={{0,1},{1,2},{2,3},{3,4},{4,5},{5,6},{6,7},{7,8},{8,9},{9,10},{10,1... | collective-permute-start | bytes 12296 | tf_op jit(solution)/shard_map/ppermute | solution.py:24
  132.0 43.4 %collective-permute-start.6 = (f16[256,1152]{1,0:T(8,128)(2,1)}, f16[256,1152]{1,0:T(8,128)(2,1)}, u32[]{:S(2)}, u32[]{:S(2)}) collective-permute-start(f16[256,1152]{1,0:T(8,128)(2,1)} %convert_element_type.22), channel_id=1, source_target_pairs={{0,95},{1,0},{2,1},{3,2},{4,3},{5,4},{6,5},{7,6},{8,7},{9,8},{10,9... | collective-permute-start | bytes 1769480 | tf_op jit(solution)/shard_map/ppermute | solution.py:24
  138.6 36.8 %copy-start.11 = (f32[256,1152]{1,0:T(8,128)S(1)}, f32[256,1152]{1,0:T(8,128)}, u32[]{:S(2)}) copy-start(f32[256,1152]{1,0:T(8,128)} %get-tuple-element.30) | copy-start | bytes 3538948
  (5 other events, 5.1 us)

commit v2 on v1

v2 whole, which is shorter than its diff:
```python
import jax
import jax.numpy as jnp
from jax import lax
from jax.experimental import pallas as pl
from jax.experimental.pallas import tpu as pltpu
from jax.sharding import Mesh
from jax.sharding import PartitionSpec as P

IN_SPAN = 3
NORM_EPS = 1e-06
AXES = ("y_lo", "core", "z", "x", "y_hi")
SIZES = (4, 2, 12, 4, 2)
N_OUTER, N_INNER = 8, 96
SEND_SCALE = 64.0
VMEM_LIMIT = 24 * 1024 * 1024


def moved(block, outer_step, inner_step):
    route = [
        (o * N_INNER + p, (o + outer_step) % N_OUTER * N_INNER + (p + inner_step) % N_INNER)
        for o in range(N_OUTER)
        for p in range(N_INNER)
    ]
    return lax.ppermute(block, AXES, route)


def unit_of(ref):
    values = ref[...].astype(jnp.float32)
    inv = lax.rsqrt(jnp.sum(values * values, axis=-1, keepdims=True) + NORM_EPS)
    return (values * inv).astype(jnp.bfloat16)


def score(img, txt, pos, text_start, head, stats):
    cosine = lax.dot_general(
        img, txt, (((1,), (1,)), ((), ())), preferred_element_type=jnp.float32
    )
    logit = head[0] * cosine + head[1]
    ids = text_start + lax.broadcasted_iota(jnp.int32, cosine.shape, 1)
    hit = pos == ids
    z = jnp.where(hit, -logit, logit)
    tail = jnp.exp(-jnp.abs(z))
    loss = jnp.maximum(z, 0.0) + jnp.log1p(tail)
    sig = jnp.where(z >= 0.0, 1.0, tail) / (1.0 + tail)
    slope = jnp.where(hit, -sig, sig)
    for row, term in enumerate((loss, slope * cosine, slope)):
        col = jnp.sum(term, axis=0, keepdims=True)
        width = stats.shape[1]
        part = col[:, :width]
        for at in range(width, col.shape[1], width):
            part = part + col[:, at : at + width]
        stats[row : row + 1, :] += part
    return slope.astype(jnp.bfloat16)


def times(a, b):
    return jnp.dot(a, b, preferred_element_type=jnp.float32)


def times_t(a, b):
    return lax.dot_general(a, b, (((0,), (0,)), ((), ())), preferred_element_type=jnp.float32)


def unit_kernel(head, start, img_raw, txt_raw, img_u, txt_u):
    img_u[...] = unit_of(img_raw)
    txt_u[...] = unit_of(txt_raw)


def first_kernel(head, start, img_u, txt_u, pos, img_acc, txt_acc, stats):
    stats[...] = jnp.zeros_like(stats)
    s = score(img_u[...], txt_u[...], pos[...], start[0], head, stats)
    img_acc[...] = times(s, txt_u[...])
    txt_acc[...] = times_t(s, img_u[...])


def second_kernel(
    head, start, img_u, txt_u, far_u, img2_u, pos, pos2, img_in, txt_in, stats_in,
    img_acc, img2_acc, txt_acc, far_acc, stats,
):
    stats[...] = stats_in[...]
    s = score(img_u[...], far_u[...], pos[...], start[2], head, stats)
    s2 = score(img2_u[...], far_u[...], pos2[...], start[2], head, stats)
    s0 = score(img2_u[...], txt_u[...], pos2[...], start[0], head, stats)
    far_acc[...] = times_t(s, img_u[...]) + times_t(s2, img2_u[...])
    img_acc[...] = img_in[...] + times(s, far_u[...])
    img2_acc[...] = times(s2, far_u[...]) + times(s0, txt_u[...])
    txt_acc[...] = txt_in[...] + times_t(s0, img2_u[...])


def third_kernel(head, start, img_u, img2_u, mid_raw, pos, pos2, stats_in, mid_u, slope, slope2, mid_acc, stats):
    stats[...] = stats_in[...]
    mid = unit_of(mid_raw)
    mid_u[...] = mid
    s = score(img_u[...], mid, pos[...], start[1], head, stats)
    s2 = score(img2_u[...], mid, pos2[...], start[1], head, stats)
    slope[...] = s
    slope2[...] = s2
    total = times_t(s, img_u[...]) + times_t(s2, img2_u[...])
    mid_acc[...] = SEND_SCALE * total


def fourth_kernel(head, start, mid_u, slope, slope2, img_in, img2_in, img_acc, img2_acc):
    img_acc[...] = img_in[...] + times(slope[...], mid_u[...])
    total = img2_in[...] + times(slope2[...], mid_u[...])
    img2_acc[...] = SEND_SCALE * total


def finish_kernel(head, start, img_raw, txt_raw, img_total, txt_total, img_grad, txt_grad):
    for raw, total, out in ((img_raw, img_total, img_grad), (txt_raw, txt_total, txt_grad)):
        values = raw[...].astype(jnp.float32)
        inv = lax.rsqrt(jnp.sum(values * values, axis=-1, keepdims=True) + NORM_EPS)
        unit = values * inv
        grad = head[0] * total[...]
        out[...] = inv * (grad - unit * jnp.sum(unit * grad, axis=-1, keepdims=True))


def call(kernel, ins, outs):
    scalars = [pl.BlockSpec(memory_space=pltpu.SMEM)] * 2
    arrays = [pl.BlockSpec(memory_space=pltpu.VMEM)] * (len(ins) - 2)
    return pl.pallas_call(
        kernel,
        in_specs=scalars + arrays,
        out_specs=[pl.BlockSpec(memory_space=pltpu.VMEM)] * len(outs),
        out_shape=outs,
        compiler_params=pltpu.CompilerParams(vmem_limit_bytes=VMEM_LIMIT),
    )(*ins)


def sum_first(s):
    s = lax.psum(lax.psum(s, ("y_lo", "core")), "y_hi")
    return jnp.sum(lax.all_gather(s, "z"), axis=0)


def sum_last(s):
    s = s + moved(s, 0, 4)
    return s + moved(s, 0, 2)


def shards(image_emb, text_emb, positive, log_scale, logit_bias):
    rows, width = image_emb.shape
    f32, bf16 = jnp.float32, jnp.bfloat16
    temp_scale = jnp.exp(log_scale[0])
    head = jnp.stack([temp_scale, logit_bias[0]])
    device = lax.axis_index(AXES)
    outer_pos, inner_pos = device // N_INNER, device % N_INNER
    start = jnp.stack(
        [(outer_pos * N_INNER + (inner_pos - b) % N_INNER) * rows for b in range(IN_SPAN)]
    ).astype(jnp.int32)
    pos = positive.reshape(rows, 1)
    wide = jax.ShapeDtypeStruct((rows, width), f32)
    unit = jax.ShapeDtypeStruct((rows, width), bf16)
    pair = jax.ShapeDtypeStruct((rows, rows), bf16)
    sums = jax.ShapeDtypeStruct((8, 128), f32)

    mid_raw = moved(text_emb, 0, 1)
    pos2 = moved(positive, -1, 0).reshape(rows, 1)
    img_u, txt_u = call(unit_kernel, (head, start, image_emb, text_emb), [unit, unit])
    img2_u = moved(img_u, -1, 0)
    far_u = moved(txt_u, 0, 2)
    img_acc, txt_acc, stats = call(
        first_kernel, (head, start, img_u, txt_u, pos), [wide, wide, sums]
    )
    img_acc, img2_acc, txt_acc, far_acc, stats = call(
        second_kernel,
        (head, start, img_u, txt_u, far_u, img2_u, pos, pos2, img_acc, txt_acc, stats),
        [wide, wide, wide, wide, sums],
    )
    far_back = moved(far_acc, 0, -2)
    mid_u, slope, slope2, mid_acc, stats = call(
        third_kernel,
        (head, start, img_u, img2_u, mid_raw, pos, pos2, stats),
        [unit, pair, pair, wide, sums],
    )
    mid_back = moved(mid_acc.astype(jnp.float16), 0, -1)
    img_acc, img2_acc = call(
        fourth_kernel,
        (head, start, mid_u, slope, slope2, img_acc, img2_acc),
        [wide, wide],
    )
    img_back = moved(img2_acc.astype(jnp.float16), 1, 0)
    always = lax.optimization_barrier(jnp.bool_(True))
    stats = lax.cond(always, sum_first, jnp.zeros_like, stats)
    stats, far_back, mid_back, img_back = lax.optimization_barrier(
        (stats, far_back, mid_back, img_back)
    )
    totals = jnp.sum(sum_last(stats), axis=1)

    img_total = img_acc + img_back.astype(f32) * (1.0 / SEND_SCALE)
    txt_total = txt_acc + far_back + mid_back.astype(f32) * (1.0 / SEND_SCALE)
    image_grad, text_grad = call(
        finish_kernel,
        (head, start, image_emb, text_emb, img_total, txt_total),
        [wide, wide],
    )
    pair_count = f32(rows * N_OUTER * N_INNER * 2 * IN_SPAN * rows)
    loss = (totals[0] / pair_count).reshape(1)
    head_grad = jnp.stack([temp_scale * totals[1], totals[2]]) / pair_count
    return (image_grad, text_grad, loss, head_grad)


def solution(mesh):
    fine = Mesh(mesh.devices.reshape(SIZES), AXES)
    return jax.shard_map(
        shards,
        mesh=fine,
        in_specs=(P(AXES, None), P(AXES, None), P(AXES), P(), P()),
        out_specs=(P(AXES, None), P(AXES, None), P(), P()),
        check_vma=False,
    )
```

time: 182 us -> 171 us (0.940)
  the two profiles are of different devices: /device:TPU:255 before, /device:TPU:8 now
where the time goes in v2:
time: 171 us; the launch traced here: 170 us
  blocking collectives  67.2 us (39%)
  starting transfers between devices  36.3 us (21%)
  waiting for transfers between devices  35.8 us (21%)
  Pallas kernels  13 us (8%)
  local copies, waits for them, and re-layouts  7.57 us (4%)
  other arithmetic  6 us (4%)
  between operations  4.61 us (3%)
    psum x2, blocking collectives, sum_first(): s = lax.psum(lax.psum(s, ('y_lo', 'core')), 'y_hi')  37 us
    ppermute x9, starting transfers between devices, moved(): return lax.ppermute(block, AXES, route)  36.3 us
    ppermute x9, waiting for transfers between devices, moved(): return lax.ppermute(block, AXES, route)  35.8 us
    all_gather x1, blocking collectives, sum_first(): return jnp.sum(lax.all_gather(s, 'z'), axis=0)  30.2 us
    pallas_call x6, Pallas kernels, call(): pl.pallas_call(kernel, in_specs=scalars + arrays, out_specs=[pl.BlockSpec...  13 us
    unnamed x22, local copies, waits for them, and re-layouts  6.71 us
  transfers between devices with their start and end apart: 9, of which 4 were waited for; matrix products, arithmetic and copies ran while one was open for 3% of the time, Pallas kernels for 7%

profile of v2, /device:TPU:8, one launch (start us, length us, event | category | flops | bytes accessed | tf_op | source)
XLA Modules:
  0.0 170.5 jit_solution(8859862056852978040)
XLA Ops:
  5.3 1.9 %collective-permute-start = (bf16[256,1152]{1,0:T(8,128)(2,1)S(1)}, bf16[256,1152]{1,0:T(8,128)(2,1)S(1)}, u32[]{:S(2)}, u32[]{:S(2)}) collective-permute-start(bf16[256,1152]{1,0:T(8,128)(2,1)S(1)} %get-tuple-element.31.img_u), channel_id=1, source_target_pairs={{0,672},{1,673},{2,674},{3,675},{4,676},{5,677},{6,678},{7,679},{8... | collective-permute-start | bytes 1769480 | tf_op jit(solution)/shard_map/ppermute | solution.py:24
  7.2 3.4 %collective-permute-start.3 = (bf16[256,1152]{1,0:T(8,128)(2,1)S(1)}, bf16[256,1152]{1,0:T(8,128)(2,1)S(1)}, u32[]{:S(2)}, u32[]{:S(2)}) collective-permute-start(bf16[256,1152]{1,0:T(8,128)(2,1)S(1)} %get-tuple-element.32.txt_u), channel_id=1, source_target_pairs={{0,2},{1,3},{2,4},{3,5},{4,6},{5,7},{6,8},{7,9},{8,10},{9,11},{10,... | collective-permute-start | bytes 1769480 | tf_op jit(solution)/shard_map/ppermute | solution.py:24
  10.6 10.0 %collective-permute-start.2 = (s32[256]{0:T(256)S(1)}, s32[256]{0:T(256)S(1)}, u32[]{:S(2)}, u32[]{:S(2)}) collective-permute-start(s32[256]{0:T(256)S(1)} %copy-done.10), channel_id=1, source_target_pairs={{0,672},{1,673},{2,674},{3,675},{4,676},{5,677},{6,678},{7,679},{8... | collective-permute-start | bytes 3080 | tf_op jit(solution)/shard_map/ppermute | solution.py:24
  20.6 1.9 %collective-permute-start.1 = (bf16[256,1152]{1,0:T(8,128)(2,1)S(1)}, bf16[256,1152]{1,0:T(8,128)(2,1)}, u32[]{:S(2)}, u32[]{:S(2)}) collective-permute-start(bf16[256,1152]{1,0:T(8,128)(2,1)S(1)} %copy-done.3), channel_id=1, source_target_pairs={{0,1},{1,2},{2,3},{3,4},{4,5},{5,6},{6,7},{7,8},{8,9},{9,10},{10,1... | collective-permute-start | bytes 1769480 | tf_op jit(solution)/shard_map/ppermute | solution.py:24
  22.7 1.8 %shard_map.85 = (f32[256,1152]{1,0:T(8,128)S(1)}, f32[256,1152]{1,0:T(8,128)S(1)}, f32[8,128]{1,0:T(8,128)S(1)}) custom-call(f32[2]{0:T(128)S(1)} %pad_maximum_fusion.head, s32[3]{0:T(128)S(1)} %pad_add_fusion.start, bf16[256,1152]{1,0:T(8,128)(2,1)S(1)} %get-tuple-element.31.img_u, bf16[256,1152]{1,0:T(8,128)(2,1)S(1)} %get-tuple-element.32.txt_u, ...), custom_call_target="tpu_custom_call" | custom-call | tf_op jit(solution)/shard_map/pallas_call | solution.py:119
  26.7 11.2 %collective-permute-done.3.far_u = bf16[256,1152]{1,0:T(8,128)(2,1)S(1)} collective-permute-done((bf16[256,1152]{1,0:T(8,128)(2,1)S(1)}, bf16[256,1152]{1,0:T(8,128)(2,1)S(1)}, u32[]{:S(2)}, u32[]{:S(2)}) %collective-permute-start.3) | collective-permute-done | bytes 589856 | tf_op jit(solution)/shard_map/ppermute | solution.py:24
  38.0 1.3 copy-done.7
  39.2 1.3 copy-done.9
  40.5 3.8 %shard_map.86 = (f32[256,1152]{1,0:T(8,128)S(1)}, f32[256,1152]{1,0:T(8,128)S(1)}, f32[256,1152]{1,0:T(8,128)S(1)}, f32[256,1152]{1,0:T(8,128)}, f32[8,128]{1,0:T(8,128)S(1)}) custom-call(f32[2]{0:T(128)S(1)} %pad_maximum_fusion.head, s32[3]{0:T(128)S(1)} %pad_add_fusion.start, bf16[256,1152]{1,0:T(8,128)(2,1)S(1)} %get-tuple-element.31.img_u, ...), custom_call_target="tpu_custom_call" | custom-call | tf_op jit(solution)/shard_map/pallas_call | solution.py:119
  44.3 5.1 %collective-permute-start.4 = (f32[256,1152]{1,0:T(8,128)}, f32[256,1152]{1,0:T(8,128)}, u32[]{:S(2)}, u32[]{:S(2)}) collective-permute-start(f32[256,1152]{1,0:T(8,128)} %get-tuple-element.44), channel_id=1, source_target_pairs={{0,94},{1,95},{2,0},{3,1},{4,2},{5,3},{6,4},{7,5},{8,6},{9,7},{10,... | collective-permute-start | bytes 3538952 | tf_op jit(solution)/shard_map/ppermute | solution.py:24
  49.4 15.1 %collective-permute-done.1.mid_raw = bf16[256,1152]{1,0:T(8,128)(2,1)} collective-permute-done((bf16[256,1152]{1,0:T(8,128)(2,1)S(1)}, bf16[256,1152]{1,0:T(8,128)(2,1)}, u32[]{:S(2)}, u32[]{:S(2)}) %collective-permute-start.1) | collective-permute-done | bytes 589856 | tf_op jit(solution)/shard_map/ppermute | solution.py:24
  64.5 2.7 %shard_map.87 = (bf16[256,1152]{1,0:T(8,128)(2,1)S(1)}, bf16[256,256]{1,0:T(8,128)(2,1)S(1)}, bf16[256,256]{1,0:T(8,128)(2,1)S(1)}, f32[256,1152]{1,0:T(8,128)S(1)}, f32[8,128]{1,0:T(8,128)S(1)}) custom-call(f32[2]{0:T(128)S(1)} %pad_maximum_fusion.head, s32[3]{0:T(128)S(1)} %pad_add_fusion.start, bf16[256,1152]{1,0:T(8,128)(2,1)S(1)} %get-tuple-element.31.img_u, ...), custom_call_target="tpu_custom_call" | custom-call | tf_op jit(solution)/shard_map/pallas_call | solution.py:119
  69.2 2.0 %collective-permute-start.6 = (f16[256,1152]{1,0:T(8,128)(2,1)}, f16[256,1152]{1,0:T(8,128)(2,1)S(1)}, u32[]{:S(2)}, u32[]{:S(2)}) collective-permute-start(f16[256,1152]{1,0:T(8,128)(2,1)} %convert_element_type.17), channel_id=1, source_target_pairs={{0,96},{1,97},{2,98},{3,99},{4,100},{5,101},{6,102},{7,103},{8,104... | collective-permute-start | bytes 1769480 | tf_op jit(solution)/shard_map/ppermute | solution.py:24
  72.2 8.0 %collective-permute-start.5 = (f16[256,1152]{1,0:T(8,128)(2,1)}, f16[256,1152]{1,0:T(8,128)(2,1)}, u32[]{:S(2)}, u32[]{:S(2)}) collective-permute-start(f16[256,1152]{1,0:T(8,128)(2,1)} %convert_element_type.16), channel_id=1, source_target_pairs={{0,95},{1,0},{2,1},{3,2},{4,3},{5,4},{6,5},{7,6},{8,7},{9,8},{10,9... | collective-permute-start | bytes 1769480 | tf_op jit(solution)/shard_map/ppermute | solution.py:24
  80.2 68.1 %conditional.1 = (f32[8,128]{1,0:T(8,128)S(1)}) conditional(s32[]{:T(128)} %convert_element_type.15, () %tuple.15, f32[8,128]{1,0:T(8,128)S(1)} %get-tuple-element.43), branch_computations={%region_0.1_spmd, %region_1.5_spmd} | conditional | flops 13312 | bytes 122892 | solution.py:181
  80.2 28.2 %psum.12 = f32[8,128]{1,0:T(8,128)S(1)} all-reduce(f32[8,128]{1,0:T(8,128)S(1)} %param.1), channel_id=1, replica_groups=mesh['y_lo'=4,'core'=2,'z'=12,'x'=4,'y_hi'=2] {'y_lo','core'}, use_global_device_ids=true, to_apply=%region_2.2 | all-reduce | flops 1024 | bytes 8192 | tf_op jit(solution)/shard_map/cond/branch_1_fun/psum | solution.py:129
  108.4 8.8 %psum.13 = f32[1,8,128]{2,1,0:T(8,128)S(1)} all-reduce(f32[1,8,128]{2,1,0:T(8,128)S(1)} %bitcast.6), channel_id=1, replica_groups=mesh['y_lo'=4,'core'=2,'z'=12,'x'=4,'y_hi'=2] {'y_hi'}, use_global_device_ids=true, to_apply=%region_3.3 | all-reduce | flops 1024 | bytes 8192 | tf_op jit(solution)/shard_map/cond/branch_1_fun/psum | solution.py:129
  117.2 30.2 %all_gather.5 = f32[12,8,128]{2,1,0:T(8,128)} all-gather(f32[1,8,128]{2,1,0:T(8,128)S(1)} %psum.13), channel_id=1, replica_groups=mesh['y_lo'=4,'core'=2,'z'=12,'x'=4,'y_hi'=2] {'z'}, dimensions={0}, use_global_device_ids=true | all-gather | bytes 53248 | tf_op jit(solution)/shard_map/cond/branch_1_fun/all_gather | solution.py:130
  148.3 1.9 %collective-permute-start.7 = (f32[8,128]{1,0:T(8,128)S(1)}, f32[8,128]{1,0:T(8,128)S(1)}, u32[]{:S(2)}, u32[]{:S(2)}) collective-permute-start(f32[8,128]{1,0:T(8,128)S(1)} %get-tuple-element.59), channel_id=1, source_target_pairs={{0,4},{1,5},{2,6},{3,7},{4,8},{5,9},{6,10},{7,11},{8,12},{9,13},{1... | collective-permute-start | bytes 12296 | tf_op jit(solution)/shard_map/ppermute | solution.py:24
  150.2 7.2 %collective-permute-done.7 = f32[8,128]{1,0:T(8,128)S(1)} collective-permute-done((f32[8,128]{1,0:T(8,128)S(1)}, f32[8,128]{1,0:T(8,128)S(1)}, u32[]{:S(2)}, u32[]{:S(2)}) %collective-permute-start.7) | collective-permute-done | bytes 4128 | tf_op jit(solution)/shard_map/ppermute | solution.py:24
  157.4 1.9 %collective-permute-start.8 = (f32[8,128]{1,0:T(8,128)S(1)}, f32[8,128]{1,0:T(8,128)S(1)}, u32[]{:S(2)}, u32[]{:S(2)}) collective-permute-start(f32[8,128]{1,0:T(8,128)S(1)} %add.70), channel_id=1, source_target_pairs={{0,2},{1,3},{2,4},{3,5},{4,6},{5,7},{6,8},{7,9},{8,10},{9,11},{10,... | collective-permute-start | bytes 12296 | tf_op jit(solution)/shard_map/ppermute | solution.py:24
  159.4 1.9 %multiply_add_fusion = (f32[256,1152]{1,0:T(8,128)S(1)}, f32[256,1152]{1,0:T(8,128)S(1)}) fusion(f16[256,1152]{1,0:T(8,128)(2,1)} %collective-permute-done.5, f32[256,1152]{1,0:T(8,128)S(1)} %copy-done.5, f32[256,1152]{1,0:T(8,128)} %collective-permute-done.4, f32[256,1152]{1,0:T(8,128)S(1)} %get-tuple-element.42, f16[256,1152]{1,0:T(8,128)(2,1)S(1)} %collective-permute-done.6), kind=kLoop, calls=%fused_computation | loop fusion | flops 2064384 | bytes 7077888 | tf_op jit(solution)/shard_map/add | solution.py:188
  161.3 2.7 %shard_map.89 = (f32[256,1152]{1,0:T(8,128)}, f32[256,1152]{1,0:T(8,128)}) custom-call(f32[2]{0:T(128)S(1)} %pad_maximum_fusion.head, s32[3]{0:T(128)S(1)} %pad_add_fusion.start, bf16[256,1152]{1,0:T(8,128)(2,1)S(1)} %copy-done.1, bf16[256,1152]{1,0:T(8,128)(2,1)S(1)} %copy-done.3, f32[256,1152]{1,0:T(8,128)S(1)} %get-tuple-element.58.img_total, ...), custom_call_target="tpu_custom_call" | custom-call | tf_op jit(solution)/shard_map/pallas_call | solution.py:119
  164.0 2.3 %collective-permute-done.8 = f32[8,128]{1,0:T(8,128)S(1)} collective-permute-done((f32[8,128]{1,0:T(8,128)S(1)}, f32[8,128]{1,0:T(8,128)S(1)}, u32[]{:S(2)}, u32[]{:S(2)}) %collective-permute-start.8) | collective-permute-done | bytes 4128 | tf_op jit(solution)/shard_map/ppermute | solution.py:24
  (38 shorter events, 11.1 us)
Async XLA Ops:
  0.6 10.0 %copy-start.10 = (s32[256]{0:T(256)S(1)}, s32[256]{0:T(256)}, u32[]{:S(2)}) copy-start(s32[256]{0:T(256)} %param.9) | copy-start | bytes 3076
  2.2 1.1 copy-start
  3.3 1.1 copy-start.2
  4.4 16.3 %copy-start.3 = (bf16[256,1152]{1,0:T(8,128)(2,1)S(1)}, bf16[256,1152]{1,0:T(8,128)(2,1)}, u32[]{:S(2)}) copy-start(bf16[256,1152]{1,0:T(8,128)(2,1)} %txt_raw.3) | copy-start | bytes 1769476
  5.3 21.5 %collective-permute-start = (bf16[256,1152]{1,0:T(8,128)(2,1)S(1)}, bf16[256,1152]{1,0:T(8,128)(2,1)S(1)}, u32[]{:S(2)}, u32[]{:S(2)}) collective-permute-start(bf16[256,1152]{1,0:T(8,128)(2,1)S(1)} %get-tuple-element.31.img_u), channel_id=1, source_target_pairs={{0,672},{1,673},{2,674},{3,675},{4,676},{5,677},{6,678},{7,679},{8... | collective-permute-start | bytes 1769480 | tf_op jit(solution)/shard_map/ppermute | solution.py:24
  7.2 30.8 %collective-permute-start.3 = (bf16[256,1152]{1,0:T(8,128)(2,1)S(1)}, bf16[256,1152]{1,0:T(8,128)(2,1)S(1)}, u32[]{:S(2)}, u32[]{:S(2)}) collective-permute-start(bf16[256,1152]{1,0:T(8,128)(2,1)S(1)} %get-tuple-element.32.txt_u), channel_id=1, source_target_pairs={{0,2},{1,3},{2,4},{3,5},{4,6},{5,7},{6,8},{7,9},{8,10},{9,11},{10,... | collective-permute-start | bytes 1769480 | tf_op jit(solution)/shard_map/ppermute | solution.py:24
  10.6 16.0 %collective-permute-start.2 = (s32[256]{0:T(256)S(1)}, s32[256]{0:T(256)S(1)}, u32[]{:S(2)}, u32[]{:S(2)}) collective-permute-start(s32[256]{0:T(256)S(1)} %copy-done.10), channel_id=1, source_target_pairs={{0,672},{1,673},{2,674},{3,675},{4,676},{5,677},{6,678},{7,679},{8... | collective-permute-start | bytes 3080 | tf_op jit(solution)/shard_map/ppermute | solution.py:24
  20.6 43.9 %collective-permute-start.1 = (bf16[256,1152]{1,0:T(8,128)(2,1)S(1)}, bf16[256,1152]{1,0:T(8,128)(2,1)}, u32[]{:S(2)}, u32[]{:S(2)}) collective-permute-start(bf16[256,1152]{1,0:T(8,128)(2,1)S(1)} %copy-done.3), channel_id=1, source_target_pairs={{0,1},{1,2},{2,3},{3,4},{4,5},{5,6},{6,7},{7,8},{8,9},{9,10},{10,1... | collective-permute-start | bytes 1769480 | tf_op jit(solution)/shard_map/ppermute | solution.py:24
  24.5 1.0 copy-start.6
  25.6 1.0 copy-start.8
  38.0 1.3 copy-start.7
  39.2 1.3 copy-start.9
  44.3 24.1 %copy-start.4 = (f32[256,1152]{1,0:T(8,128)}, f32[256,1152]{1,0:T(8,128)S(1)}, u32[]{:S(2)}) copy-start(f32[256,1152]{1,0:T(8,128)S(1)} %get-tuple-element.48) | copy-start | bytes 3538948
  44.3 104.0 %collective-permute-start.4 = (f32[256,1152]{1,0:T(8,128)}, f32[256,1152]{1,0:T(8,128)}, u32[]{:S(2)}, u32[]{:S(2)}) collective-permute-start(f32[256,1152]{1,0:T(8,128)} %get-tuple-element.44), channel_id=1, source_target_pairs={{0,94},{1,95},{2,0},{3,1},{4,2},{5,3},{6,4},{7,5},{8,6},{9,7},{10,... | collective-permute-start | bytes 3538952 | tf_op jit(solution)/shard_map/ppermute | solution.py:24
  69.2 90.1 %copy-start.5 = (f32[256,1152]{1,0:T(8,128)S(1)}, f32[256,1152]{1,0:T(8,128)}, u32[]{:S(2)}) copy-start(f32[256,1152]{1,0:T(8,128)} %copy-done.4) | copy-start | bytes 3538948
  69.2 79.0 %collective-permute-start.6 = (f16[256,1152]{1,0:T(8,128)(2,1)}, f16[256,1152]{1,0:T(8,128)(2,1)S(1)}, u32[]{:S(2)}, u32[]{:S(2)}) collective-permute-start(f16[256,1152]{1,0:T(8,128)(2,1)} %convert_element_type.17), channel_id=1, source_target_pairs={{0,96},{1,97},{2,98},{3,99},{4,100},{5,101},{6,102},{7,103},{8,104... | collective-permute-start | bytes 1769480 | tf_op jit(solution)/shard_map/ppermute | solution.py:24
  72.2 76.1 %collective-permute-start.5 = (f16[256,1152]{1,0:T(8,128)(2,1)}, f16[256,1152]{1,0:T(8,128)(2,1)}, u32[]{:S(2)}, u32[]{:S(2)}) collective-permute-start(f16[256,1152]{1,0:T(8,128)(2,1)} %convert_element_type.16), channel_id=1, source_target_pairs={{0,95},{1,0},{2,1},{3,2},{4,3},{5,4},{6,5},{7,6},{8,7},{9,8},{10,9... | collective-permute-start | bytes 1769480 | tf_op jit(solution)/shard_map/ppermute | solution.py:24
  148.3 9.1 %collective-permute-start.7 = (f32[8,128]{1,0:T(8,128)S(1)}, f32[8,128]{1,0:T(8,128)S(1)}, u32[]{:S(2)}, u32[]{:S(2)}) collective-permute-start(f32[8,128]{1,0:T(8,128)S(1)} %get-tuple-element.59), channel_id=1, source_target_pairs={{0,4},{1,5},{2,6},{3,7},{4,8},{5,9},{6,10},{7,11},{8,12},{9,13},{1... | collective-permute-start | bytes 12296 | tf_op jit(solution)/shard_map/ppermute | solution.py:24
  157.4 8.8 %collective-permute-start.8 = (f32[8,128]{1,0:T(8,128)S(1)}, f32[8,128]{1,0:T(8,128)S(1)}, u32[]{:S(2)}, u32[]{:S(2)}) collective-permute-start(f32[8,128]{1,0:T(8,128)S(1)} %add.70), channel_id=1, source_target_pairs={{0,2},{1,3},{2,4},{3,5},{4,6},{5,7},{6,8},{7,9},{8,10},{9,11},{10,... | collective-permute-start | bytes 12296 | tf_op jit(solution)/shard_map/ppermute | solution.py:24
  159.3 1.9 %copy-start.1 = (bf16[256,1152]{1,0:T(8,128)(2,1)S(1)}, bf16[256,1152]{1,0:T(8,128)(2,1)}, u32[]{:S(2)}) copy-start(bf16[256,1152]{1,0:T(8,128)(2,1)} %img_raw.3) | copy-start | bytes 1769476

commit v3 on v2

--- a/solution.py
+++ b/solution.py
@@ -22,6 +22,26 @@
         for p in range(N_INNER)
     ]
     return lax.ppermute(block, AXES, route)
+
+
+def half_way():
+    route = []
+    for device in range(N_OUTER * N_INNER):
+        o, p = divmod(device, N_INNER)
+        y = p % 2 * 4 + o // 2
+        y = (y + (2 if o % 2 == 0 else 6)) % 8
+        route.append((device, (y % 4 * 2 + o % 2) * N_INNER + p // 2 * 2 + y // 4))
+    return route
+
+
+def one_step_in_two(block, sign):
+    first = half_way()
+    ends = [
+        (there, o * N_INNER + (p + sign) % N_INNER)
+        for device, there in first
+        for o, p in [divmod(device, N_INNER)]
+    ]
+    return lax.ppermute(lax.ppermute(block, AXES, first), AXES, ends)
 
 
 def unit_of(ref):
@@ -126,13 +146,14 @@
 
 
 def sum_first(s):
-    s = lax.psum(lax.psum(s, ("y_lo", "core")), "y_hi")
-    return jnp.sum(lax.all_gather(s, "z"), axis=0)
+    s = jnp.sum(lax.all_gather(s, "z"), axis=0)
+    s = jnp.sum(lax.all_gather(s, "x"), axis=0)
+    return lax.psum(s, ("y_lo", "core"))
 
 
 def sum_last(s):
-    s = s + moved(s, 0, 4)
-    return s + moved(s, 0, 2)
+    route = [(device, device ^ 1) for device in range(N_OUTER * N_INNER)]
+    return s + lax.ppermute(s, AXES, route)
 
 
 def shards(image_emb, text_emb, positive, log_scale, logit_bias):
@@ -151,7 +172,7 @@
     pair = jax.ShapeDtypeStruct((rows, rows), bf16)
     sums = jax.ShapeDtypeStruct((8, 128), f32)
 
-    mid_raw = moved(text_emb, 0, 1)
+    mid_raw = one_step_in_two(text_emb, 1)
     pos2 = moved(positive, -1, 0).reshape(rows, 1)
     img_u, txt_u = call(unit_kernel, (head, start, image_emb, text_emb), [unit, unit])
     img2_u = moved(img_u, -1, 0)

time: 171 us -> 170 us (level)
  the two profiles are of different devices: /device:TPU:8 before, /device:TPU:1 now
where the time goes in v3:
time: 170 us
  blocking collectives  78.2 us (46%)
  starting transfers between devices  43.1 us (25%)
  waiting for transfers between devices  16.2 us (10%)
  Pallas kernels  13 us (8%)
  local copies, waits for them, and re-layouts  9.46 us (6%)
  other arithmetic  5.11 us (3%)
  between operations  4.6 us (3%)
    all_gather x1, blocking collectives, sum_first(): s = jnp.sum(lax.all_gather(s, 'z'), axis=0)  41.5 us
    ppermute x6, starting transfers between devices, moved(): return lax.ppermute(block, AXES, route)  28.8 us
    psum x1, blocking collectives, sum_first(): return lax.psum(s, ('y_lo', 'core'))  27.6 us
    ppermute x6, waiting for transfers between devices, moved(): return lax.ppermute(block, AXES, route)  13.7 us
    pallas_call x6, Pallas kernels, call(): pl.pallas_call(kernel, in_specs=scalars + arrays, out_specs=[pl.BlockSpec...  13 us
    ppermute x2, starting transfers between devices, one_step_in_two(): return lax.ppermute(lax.ppermute(block, AXES, first), AXES, ends)  12.5 us
    all_gather x1, blocking collectives, sum_first(): s = jnp.sum(lax.all_gather(s, 'x'), axis=0)  9.15 us
    unnamed x22, local copies, waits for them, and re-layouts  8.6 us
  transfers between devices with their start and end apart: 9, of which 3 were waited for; matrix products, arithmetic and copies ran while one was open for 2% of the time, Pallas kernels for 8%

profile of v3, /device:TPU:1, one launch (start us, length us, event | category | flops | bytes accessed | tf_op | source)
XLA Modules:
  0.0 169.8 jit_solution(18280627818698763268)
XLA Ops:
  0.6 6.7 %collective-permute-start.1 = (bf16[256,1152]{1,0:T(8,128)(2,1)}, bf16[256,1152]{1,0:T(8,128)(2,1)}, u32[]{:S(2)}, u32[]{:S(2)}) collective-permute-start(bf16[256,1152]{1,0:T(8,128)(2,1)} %txt_raw.3), channel_id=1, source_target_pairs={{0,384},{1,385},{2,386},{3,387},{4,388},{5,389},{6,390},{7,391},{8... | collective-permute-start | bytes 1769480 | tf_op jit(solution)/shard_map/ppermute | solution.py:44
  12.0 7.6 %collective-permute-start = (bf16[256,1152]{1,0:T(8,128)(2,1)S(1)}, bf16[256,1152]{1,0:T(8,128)(2,1)S(1)}, u32[]{:S(2)}, u32[]{:S(2)}) collective-permute-start(bf16[256,1152]{1,0:T(8,128)(2,1)S(1)} %get-tuple-element.31.img_u), channel_id=1, source_target_pairs={{0,672},{1,673},{2,674},{3,675},{4,676},{5,677},{6,678},{7,679},{8... | collective-permute-start | bytes 1769480 | tf_op jit(solution)/shard_map/ppermute | solution.py:24
  19.6 1.9 %collective-permute-start.4 = (bf16[256,1152]{1,0:T(8,128)(2,1)S(1)}, bf16[256,1152]{1,0:T(8,128)(2,1)S(1)}, u32[]{:S(2)}, u32[]{:S(2)}) collective-permute-start(bf16[256,1152]{1,0:T(8,128)(2,1)S(1)} %get-tuple-element.32.txt_u), channel_id=1, source_target_pairs={{0,2},{1,3},{2,4},{3,5},{4,6},{5,7},{6,8},{7,9},{8,10},{9,11},{10,... | collective-permute-start | bytes 1769480 | tf_op jit(solution)/shard_map/ppermute | solution.py:24
  21.6 1.9 %collective-permute-start.3 = (s32[256]{0:T(256)S(1)}, s32[256]{0:T(256)S(1)}, u32[]{:S(2)}, u32[]{:S(2)}) collective-permute-start(s32[256]{0:T(256)S(1)} %copy-done.10), channel_id=1, source_target_pairs={{0,672},{1,673},{2,674},{3,675},{4,676},{5,677},{6,678},{7,679},{8... | collective-permute-start | bytes 3080 | tf_op jit(solution)/shard_map/ppermute | solution.py:24
  23.5 5.8 %collective-permute-start.2 = (bf16[256,1152]{1,0:T(8,128)(2,1)}, bf16[256,1152]{1,0:T(8,128)(2,1)}, u32[]{:S(2)}, u32[]{:S(2)}) collective-permute-start(bf16[256,1152]{1,0:T(8,128)(2,1)} %collective-permute-done.1), channel_id=1, source_target_pairs={{384,1},{385,2},{386,3},{387,4},{388,5},{389,6},{390,7},{391,8},{3... | collective-permute-start | bytes 1769480 | tf_op jit(solution)/shard_map/ppermute | solution.py:44
  29.4 1.8 %shard_map.85 = (f32[256,1152]{1,0:T(8,128)S(1)}, f32[256,1152]{1,0:T(8,128)S(1)}, f32[8,128]{1,0:T(8,128)S(1)}) custom-call(f32[2]{0:T(128)S(1)} %pad_maximum_fusion.head, s32[3]{0:T(128)S(1)} %pad_add_fusion.start, bf16[256,1152]{1,0:T(8,128)(2,1)S(1)} %get-tuple-element.31.img_u, bf16[256,1152]{1,0:T(8,128)(2,1)S(1)} %get-tuple-element.32.txt_u, ...), custom_call_target="tpu_custom_call" | custom-call | tf_op jit(solution)/shard_map/pallas_call | solution.py:139
  33.4 13.7 %collective-permute-done.4.far_u = bf16[256,1152]{1,0:T(8,128)(2,1)S(1)} collective-permute-done((bf16[256,1152]{1,0:T(8,128)(2,1)S(1)}, bf16[256,1152]{1,0:T(8,128)(2,1)S(1)}, u32[]{:S(2)}, u32[]{:S(2)}) %collective-permute-start.4) | collective-permute-done | bytes 589856 | tf_op jit(solution)/shard_map/ppermute | solution.py:24
  48.0 1.3 copy-done.5
  49.2 1.3 copy-done.7
  51.6 3.7 %shard_map.86 = (f32[256,1152]{1,0:T(8,128)S(1)}, f32[256,1152]{1,0:T(8,128)S(1)}, f32[256,1152]{1,0:T(8,128)S(1)}, f32[256,1152]{1,0:T(8,128)}, f32[8,128]{1,0:T(8,128)S(1)}) custom-call(f32[2]{0:T(128)S(1)} %pad_maximum_fusion.head, s32[3]{0:T(128)S(1)} %pad_add_fusion.start, bf16[256,1152]{1,0:T(8,128)(2,1)S(1)} %get-tuple-element.31.img_u, ...), custom_call_target="tpu_custom_call" | custom-call | tf_op jit(solution)/shard_map/pallas_call | solution.py:139
  55.3 2.6 %collective-permute-start.5 = (f32[256,1152]{1,0:T(8,128)}, f32[256,1152]{1,0:T(8,128)}, u32[]{:S(2)}, u32[]{:S(2)}) collective-permute-start(f32[256,1152]{1,0:T(8,128)} %get-tuple-element.44), channel_id=1, source_target_pairs={{0,94},{1,95},{2,0},{3,1},{4,2},{5,3},{6,4},{7,5},{8,6},{9,7},{10,... | collective-permute-start | bytes 3538952 | tf_op jit(solution)/shard_map/ppermute | solution.py:24
  58.8 2.7 %shard_map.87 = (bf16[256,1152]{1,0:T(8,128)(2,1)S(1)}, bf16[256,256]{1,0:T(8,128)(2,1)S(1)}, bf16[256,256]{1,0:T(8,128)(2,1)S(1)}, f32[256,1152]{1,0:T(8,128)S(1)}, f32[8,128]{1,0:T(8,128)S(1)}) custom-call(f32[2]{0:T(128)S(1)} %pad_maximum_fusion.head, s32[3]{0:T(128)S(1)} %pad_add_fusion.start, bf16[256,1152]{1,0:T(8,128)(2,1)S(1)} %get-tuple-element.31.img_u, ...), custom_call_target="tpu_custom_call" | custom-call | tf_op jit(solution)/shard_map/pallas_call | solution.py:139
  61.4 1.1 shard_map.88
  63.4 12.7 %collective-permute-start.7 = (f16[256,1152]{1,0:T(8,128)(2,1)}, f16[256,1152]{1,0:T(8,128)(2,1)S(1)}, u32[]{:S(2)}, u32[]{:S(2)}) collective-permute-start(f16[256,1152]{1,0:T(8,128)(2,1)} %convert_element_type.17), channel_id=1, source_target_pairs={{0,96},{1,97},{2,98},{3,99},{4,100},{5,101},{6,102},{7,103},{8,104... | collective-permute-start | bytes 1769480 | tf_op jit(solution)/shard_map/ppermute | solution.py:24
  77.1 1.9 %collective-permute-start.6 = (f16[256,1152]{1,0:T(8,128)(2,1)}, f16[256,1152]{1,0:T(8,128)(2,1)}, u32[]{:S(2)}, u32[]{:S(2)}) collective-permute-start(f16[256,1152]{1,0:T(8,128)(2,1)} %convert_element_type.16), channel_id=1, source_target_pairs={{0,95},{1,0},{2,1},{3,2},{4,3},{5,4},{6,5},{7,6},{8,7},{9,8},{10,9... | collective-permute-start | bytes 1769480 | tf_op jit(solution)/shard_map/ppermute | solution.py:24
  79.0 78.2 %conditional.1 = (f32[8,128]{1,0:T(8,128)S(1)}) conditional(s32[]{:T(128)} %convert_element_type.15, () %tuple.15, f32[8,128]{1,0:T(8,128)S(1)} %get-tuple-element.43), branch_computations={%region_0.1_spmd, %region_1.5_spmd} | conditional | flops 15360 | bytes 155656 | solution.py:202
  79.0 41.5 %all-gather = f32[96,128]{1,0:T(8,128)S(1)} all-gather(f32[8,128]{1,0:T(8,128)S(1)} %param.1), channel_id=2, replica_groups=mesh['y_lo'=4,'core'=2,'z'=12,'x'=4,'y_hi'=2] {'z'}, dimensions={0}, use_global_device_ids=true | all-gather | bytes 53248 | tf_op jit(solution)/shard_map/cond/branch_1_fun/all_gather | solution.py:149
  120.5 9.1 %all-gather.1 = f32[32,128]{1,0:T(8,128)S(1)} all-gather(f32[8,128]{1,0:T(8,128)S(1)} %bitcast_reduce_fusion), channel_id=3, replica_groups=mesh['y_lo'=4,'core'=2,'z'=12,'x'=4,'y_hi'=2] {'x'}, dimensions={0}, use_global_device_ids=true | all-gather | bytes 20480 | tf_op jit(solution)/shard_map/cond/branch_1_fun/all_gather | solution.py:150
  129.6 27.6 %psum.6 = f32[8,128]{1,0:T(8,128)S(1)} all-reduce(f32[8,128]{1,0:T(8,128)S(1)} %bitcast_reduce_fusion.1), channel_id=1, replica_groups=mesh['y_lo'=4,'core'=2,'z'=12,'x'=4,'y_hi'=2] {'y_lo','core'}, use_global_device_ids=true, to_apply=%region_4.4 | all-reduce | flops 1024 | bytes 8192 | tf_op jit(solution)/shard_map/cond/branch_1_fun/psum | solution.py:151
  157.2 1.9 %collective-permute-start.8 = (f32[8,128]{1,0:T(8,128)S(1)}, f32[8,128]{1,0:T(8,128)S(1)}, u32[]{:S(2)}, u32[]{:S(2)}) collective-permute-start(f32[8,128]{1,0:T(8,128)S(1)} %get-tuple-element.59), channel_id=1, source_target_pairs={{0,1},{1,0},{2,3},{3,2},{4,5},{5,4},{6,7},{7,6},{8,9},{9,8},{10,11... | collective-permute-start | bytes 12296 | tf_op jit(solution)/shard_map/ppermute | solution.py:156
  159.2 1.8 %multiply_add_fusion = (f32[256,1152]{1,0:T(8,128)S(1)}, f32[256,1152]{1,0:T(8,128)S(1)}) fusion(f16[256,1152]{1,0:T(8,128)(2,1)} %collective-permute-done.6, f32[256,1152]{1,0:T(8,128)S(1)} %get-tuple-element.48, f32[256,1152]{1,0:T(8,128)} %collective-permute-done.5, f32[256,1152]{1,0:T(8,128)S(1)} %get-tuple-element.42, ...), kind=kLoop, calls=%fused_computation.2 | loop fusion | flops 2064384 | bytes 7077888 | tf_op jit(solution)/shard_map/add | solution.py:209
  161.0 2.7 %shard_map.89 = (f32[256,1152]{1,0:T(8,128)}, f32[256,1152]{1,0:T(8,128)}) custom-call(f32[2]{0:T(128)S(1)} %pad_maximum_fusion.head, s32[3]{0:T(128)S(1)} %pad_add_fusion.start, bf16[256,1152]{1,0:T(8,128)(2,1)S(1)} %copy-done.1, bf16[256,1152]{1,0:T(8,128)(2,1)S(1)} %copy-done.3, f32[256,1152]{1,0:T(8,128)S(1)} %get-tuple-element.58.img_total, ...), custom_call_target="tpu_custom_call" | custom-call | tf_op jit(solution)/shard_map/pallas_call | solution.py:139
  163.8 1.7 %collective-permute-done.8 = f32[8,128]{1,0:T(8,128)S(1)} collective-permute-done((f32[8,128]{1,0:T(8,128)S(1)}, f32[8,128]{1,0:T(8,128)S(1)}, u32[]{:S(2)}, u32[]{:S(2)}) %collective-permute-start.8) | collective-permute-done | bytes 4128 | tf_op jit(solution)/shard_map/ppermute | solution.py:156
  166.9 1.2 maximum_multiply_fusion
  (38 shorter events, 10.7 us)
Async XLA Ops:
  0.6 20.9 %copy-start.10 = (s32[256]{0:T(256)S(1)}, s32[256]{0:T(256)}, u32[]{:S(2)}) copy-start(s32[256]{0:T(256)} %param.9) | copy-start | bytes 3076
  0.6 22.9 %collective-permute-start.1 = (bf16[256,1152]{1,0:T(8,128)(2,1)}, bf16[256,1152]{1,0:T(8,128)(2,1)}, u32[]{:S(2)}, u32[]{:S(2)}) collective-permute-start(bf16[256,1152]{1,0:T(8,128)(2,1)} %txt_raw.3), channel_id=1, source_target_pairs={{0,384},{1,385},{2,386},{3,387},{4,388},{5,389},{6,390},{7,391},{8... | collective-permute-start | bytes 1769480 | tf_op jit(solution)/shard_map/ppermute | solution.py:44
  8.9 1.1 copy-start
  10.0 1.1 copy-start.2
  12.0 21.4 %collective-permute-start = (bf16[256,1152]{1,0:T(8,128)(2,1)S(1)}, bf16[256,1152]{1,0:T(8,128)(2,1)S(1)}, u32[]{:S(2)}, u32[]{:S(2)}) collective-permute-start(bf16[256,1152]{1,0:T(8,128)(2,1)S(1)} %get-tuple-element.31.img_u), channel_id=1, source_target_pairs={{0,672},{1,673},{2,674},{3,675},{4,676},{5,677},{6,678},{7,679},{8... | collective-permute-start | bytes 1769480 | tf_op jit(solution)/shard_map/ppermute | solution.py:24
  19.6 27.5 %collective-permute-start.4 = (bf16[256,1152]{1,0:T(8,128)(2,1)S(1)}, bf16[256,1152]{1,0:T(8,128)(2,1)S(1)}, u32[]{:S(2)}, u32[]{:S(2)}) collective-permute-start(bf16[256,1152]{1,0:T(8,128)(2,1)S(1)} %get-tuple-element.32.txt_u), channel_id=1, source_target_pairs={{0,2},{1,3},{2,4},{3,5},{4,6},{5,7},{6,8},{7,9},{8,10},{9,11},{10,... | collective-permute-start | bytes 1769480 | tf_op jit(solution)/shard_map/ppermute | solution.py:24
  21.6 11.7 %collective-permute-start.3 = (s32[256]{0:T(256)S(1)}, s32[256]{0:T(256)S(1)}, u32[]{:S(2)}, u32[]{:S(2)}) collective-permute-start(s32[256]{0:T(256)S(1)} %copy-done.10), channel_id=1, source_target_pairs={{0,672},{1,673},{2,674},{3,675},{4,676},{5,677},{6,678},{7,679},{8... | collective-permute-start | bytes 3080 | tf_op jit(solution)/shard_map/ppermute | solution.py:24
  23.5 35.2 %collective-permute-start.2 = (bf16[256,1152]{1,0:T(8,128)(2,1)}, bf16[256,1152]{1,0:T(8,128)(2,1)}, u32[]{:S(2)}, u32[]{:S(2)}) collective-permute-start(bf16[256,1152]{1,0:T(8,128)(2,1)} %collective-permute-done.1), channel_id=1, source_target_pairs={{384,1},{385,2},{386,3},{387,4},{388,5},{389,6},{390,7},{391,8},{3... | collective-permute-start | bytes 1769480 | tf_op jit(solution)/shard_map/ppermute | solution.py:44
  31.3 1.0 copy-start.4
  32.3 1.0 copy-start.6
  47.1 0.8 copy-start.8
  48.0 1.3 copy-start.5
  49.2 1.3 copy-start.7
  50.5 1.1 copy-start.9
  55.3 101.9 %collective-permute-start.5 = (f32[256,1152]{1,0:T(8,128)}, f32[256,1152]{1,0:T(8,128)}, u32[]{:S(2)}, u32[]{:S(2)}) collective-permute-start(f32[256,1152]{1,0:T(8,128)} %get-tuple-element.44), channel_id=1, source_target_pairs={{0,94},{1,95},{2,0},{3,1},{4,2},{5,3},{6,4},{7,5},{8,6},{9,7},{10,... | collective-permute-start | bytes 3538952 | tf_op jit(solution)/shard_map/ppermute | solution.py:24
  63.4 93.8 %collective-permute-start.7 = (f16[256,1152]{1,0:T(8,128)(2,1)}, f16[256,1152]{1,0:T(8,128)(2,1)S(1)}, u32[]{:S(2)}, u32[]{:S(2)}) collective-permute-start(f16[256,1152]{1,0:T(8,128)(2,1)} %convert_element_type.17), channel_id=1, source_target_pairs={{0,96},{1,97},{2,98},{3,99},{4,100},{5,101},{6,102},{7,103},{8,104... | collective-permute-start | bytes 1769480 | tf_op jit(solution)/shard_map/ppermute | solution.py:24
  77.1 80.2 %collective-permute-start.6 = (f16[256,1152]{1,0:T(8,128)(2,1)}, f16[256,1152]{1,0:T(8,128)(2,1)}, u32[]{:S(2)}, u32[]{:S(2)}) collective-permute-start(f16[256,1152]{1,0:T(8,128)(2,1)} %convert_element_type.16), channel_id=1, source_target_pairs={{0,95},{1,0},{2,1},{3,2},{4,3},{5,4},{6,5},{7,6},{8,7},{9,8},{10,9... | collective-permute-start | bytes 1769480 | tf_op jit(solution)/shard_map/ppermute | solution.py:24
  157.2 8.3 %collective-permute-start.8 = (f32[8,128]{1,0:T(8,128)S(1)}, f32[8,128]{1,0:T(8,128)S(1)}, u32[]{:S(2)}, u32[]{:S(2)}) collective-permute-start(f32[8,128]{1,0:T(8,128)S(1)} %get-tuple-element.59), channel_id=1, source_target_pairs={{0,1},{1,0},{2,3},{3,2},{4,5},{5,4},{6,7},{7,6},{8,9},{9,8},{10,11... | collective-permute-start | bytes 12296 | tf_op jit(solution)/shard_map/ppermute | solution.py:156
  159.2 1.9 %copy-start.1 = (bf16[256,1152]{1,0:T(8,128)(2,1)S(1)}, bf16[256,1152]{1,0:T(8,128)(2,1)}, u32[]{:S(2)}) copy-start(bf16[256,1152]{1,0:T(8,128)(2,1)} %img_raw.3) | copy-start | bytes 1769476
  159.2 1.9 %copy-start.3 = (bf16[256,1152]{1,0:T(8,128)(2,1)S(1)}, bf16[256,1152]{1,0:T(8,128)(2,1)}, u32[]{:S(2)}) copy-start(bf16[256,1152]{1,0:T(8,128)(2,1)} %txt_raw.3) | copy-start | bytes 1769476

commit v4 on v3

--- a/solution.py
+++ b/solution.py
@@ -12,7 +12,7 @@
 SIZES = (4, 2, 12, 4, 2)
 N_OUTER, N_INNER = 8, 96
 SEND_SCALE = 64.0
-VMEM_LIMIT = 24 * 1024 * 1024
+VMEM_LIMIT = 14 * 1024 * 1024
 
 
 def moved(block, outer_step, inner_step):
@@ -145,10 +145,12 @@
     )(*ins)
 
 
-def sum_first(s):
-    s = jnp.sum(lax.all_gather(s, "z"), axis=0)
-    s = jnp.sum(lax.all_gather(s, "x"), axis=0)
-    return lax.psum(s, ("y_lo", "core"))
+def sum_z(s):
+    return jnp.sum(lax.all_gather(s, "z"), axis=0)
+
+
+def sum_x_y_lo(s):
+    return lax.psum(jnp.sum(lax.all_gather(s, "x"), axis=0), ("y_lo", "core"))
 
 
 def sum_last(s):
@@ -185,28 +187,32 @@
         (head, start, img_u, txt_u, far_u, img2_u, pos, pos2, img_acc, txt_acc, stats),
         [wide, wide, wide, wide, sums],
     )
-    far_back = moved(far_acc, 0, -2)
+    far_back = moved((SEND_SCALE * far_acc).astype(jnp.float16), 0, -2)
     mid_u, slope, slope2, mid_acc, stats = call(
         third_kernel,
         (head, start, img_u, img2_u, mid_raw, pos, pos2, stats),
         [unit, pair, pair, wide, sums],
     )
-    mid_back = moved(mid_acc.astype(jnp.float16), 0, -1)
     img_acc, img2_acc = call(
         fourth_kernel,
         (head, start, mid_u, slope, slope2, img_acc, img2_acc),
         [wide, wide],
     )
-    img_back = moved(img2_acc.astype(jnp.float16), 1, 0)
     always = lax.optimization_barrier(jnp.bool_(True))
-    stats = lax.cond(always, sum_first, jnp.zeros_like, stats)
+    stats = lax.cond(always, sum_z, jnp.zeros_like, stats)
+    stats, mid_half, img_half = lax.optimization_barrier(
+        (stats, mid_acc.astype(jnp.float16), img2_acc.astype(jnp.float16))
+    )
+    mid_back = moved(mid_half, 0, -1)
+    img_back = moved(img_half, 1, 0)
+    stats = lax.cond(always, sum_x_y_lo, jnp.zeros_like, stats)
     stats, far_back, mid_back, img_back = lax.optimization_barrier(
         (stats, far_back, mid_back, img_back)
     )
     totals = jnp.sum(sum_last(stats), axis=1)
 
     img_total = img_acc + img_back.astype(f32) * (1.0 / SEND_SCALE)
-    txt_total = txt_acc + far_back + mid_back.astype(f32) * (1.0 / SEND_SCALE)
+    txt_total = txt_acc + (far_back.astype(f32) + mid_back.astype(f32)) * (1.0 / SEND_SCALE)
     image_grad, text_grad = call(
         finish_kernel,
         (head, start, image_emb, text_emb, img_total, txt_total),

time: 170 us -> 150 us (0.88)
  blocking collectives: 78.2 us -> 54.8 us
  starting transfers between devices: 43.1 us -> 62.1 us
  waiting for transfers between devices: 16.2 us -> 0.03 us
    all_gather x2, blocking collectives: 50.6 us -> 31.5 us  [the longest x1 21.6 us: sum_z(): return jnp.sum(lax.all_gather(s, 'z'), axis=0)]
    ppermute x6, starting transfers between devices: 28.8 us -> 45.2 us  [moved(): return lax.ppermute(block, AXES, route)]
    ppermute x6, waiting for transfers between devices: 13.7 us -> 0.02 us  [moved(): return lax.ppermute(block, AXES, route)]
    psum x1, blocking collectives: 27.6 us -> 23.3 us  [sum_x_y_lo(): return lax.psum(jnp.sum(lax.all_gather(s, 'x'), axis=0), ('y_lo', 'core'))]
    ppermute x1, starting transfers between devices: 1.92 us -> 4.48 us  [sum_last(): return s + lax.ppermute(s, AXES, route)]
    ppermute x1, waiting for transfers between devices: 1.7 us -> 0.01 us  [sum_last(): return s + lax.ppermute(s, AXES, route)]
  transfers between devices with their start and end apart: 9 -> 9, of which waited for: 3 -> 0; matrix products, arithmetic and copies ran while one was open for 2% -> 3% of each run, Pallas kernels for 8% -> 8%
where the time goes in v4:
time: 150 us; the launch traced here: 149 us
  starting transfers between devices  62.1 us (41%)
  blocking collectives  54.8 us (37%)
  Pallas kernels  12.3 us (8%)
  local copies, waits for them, and re-layouts  9.55 us (6%)
  other arithmetic  5.08 us (3%)
  between operations  4.77 us (3%)
    ppermute x6, starting transfers between devices, moved(): return lax.ppermute(block, AXES, route)  45.2 us
    psum x1, blocking collectives, sum_x_y_lo(): return lax.psum(jnp.sum(lax.all_gather(s, 'x'), axis=0), ('y_lo', 'core'))  23.3 us
    all_gather x1, blocking collectives, sum_z(): return jnp.sum(lax.all_gather(s, 'z'), axis=0)  21.6 us
    ppermute x2, starting transfers between devices, one_step_in_two(): return lax.ppermute(lax.ppermute(block, AXES, first), AXES, ends)  12.5 us
    pallas_call x6, Pallas kernels, call(): pl.pallas_call(kernel, in_specs=scalars + arrays, out_specs=[pl.BlockSpec...  12.3 us
    all_gather x1, blocking collectives, sum_x_y_lo(): return lax.psum(jnp.sum(lax.all_gather(s, 'x'), axis=0), ('y_lo', 'core'))  9.89 us
    unnamed x22, local copies, waits for them, and re-layouts  8.62 us
    ppermute x1, starting transfers between devices, sum_last(): return s + lax.ppermute(s, AXES, route)  4.48 us
  transfers between devices with their start and end apart: 9, of which 0 were waited for; matrix products, arithmetic and copies ran while one was open for 3% of the time, Pallas kernels for 8%

profile of v4, /device:TPU:1, one launch (start us, length us, event | category | flops | bytes accessed | tf_op | source)
XLA Modules:
  0.0 148.6 jit_solution(14111317301082853676)
XLA Ops:
  0.6 6.7 %collective-permute-start.1 = (bf16[256,1152]{1,0:T(8,128)(2,1)}, bf16[256,1152]{1,0:T(8,128)(2,1)}, u32[]{:S(2)}, u32[]{:S(2)}) collective-permute-start(bf16[256,1152]{1,0:T(8,128)(2,1)} %txt_raw.3), channel_id=1, source_target_pairs={{0,384},{1,385},{2,386},{3,387},{4,388},{5,389},{6,390},{7,391},{8... | collective-permute-start | bytes 1769480 | tf_op jit(solution)/shard_map/ppermute | solution.py:44
  8.9 1.1 copy-done
  12.0 7.6 %collective-permute-start = (bf16[256,1152]{1,0:T(8,128)(2,1)S(1)}, bf16[256,1152]{1,0:T(8,128)(2,1)S(1)}, u32[]{:S(2)}, u32[]{:S(2)}) collective-permute-start(bf16[256,1152]{1,0:T(8,128)(2,1)S(1)} %get-tuple-element.38.img_u), channel_id=1, source_target_pairs={{0,672},{1,673},{2,674},{3,675},{4,676},{5,677},{6,678},{7,679},{8... | collective-permute-start | bytes 1769480 | tf_op jit(solution)/shard_map/ppermute | solution.py:24
  19.6 1.9 %collective-permute-start.4 = (bf16[256,1152]{1,0:T(8,128)(2,1)S(1)}, bf16[256,1152]{1,0:T(8,128)(2,1)S(1)}, u32[]{:S(2)}, u32[]{:S(2)}) collective-permute-start(bf16[256,1152]{1,0:T(8,128)(2,1)S(1)} %get-tuple-element.39.txt_u), channel_id=1, source_target_pairs={{0,2},{1,3},{2,4},{3,5},{4,6},{5,7},{6,8},{7,9},{8,10},{9,11},{10,... | collective-permute-start | bytes 1769480 | tf_op jit(solution)/shard_map/ppermute | solution.py:24
  21.6 5.8 %collective-permute-start.2 = (bf16[256,1152]{1,0:T(8,128)(2,1)}, bf16[256,1152]{1,0:T(8,128)(2,1)}, u32[]{:S(2)}, u32[]{:S(2)}) collective-permute-start(bf16[256,1152]{1,0:T(8,128)(2,1)} %collective-permute-done.1), channel_id=1, source_target_pairs={{384,1},{385,2},{386,3},{387,4},{388,5},{389,6},{390,7},{391,8},{3... | collective-permute-start | bytes 1769480 | tf_op jit(solution)/shard_map/ppermute | solution.py:44
  27.3 15.7 %collective-permute-start.3 = (s32[256]{0:T(256)S(1)}, s32[256]{0:T(256)S(1)}, u32[]{:S(2)}, u32[]{:S(2)}) collective-permute-start(s32[256]{0:T(256)S(1)} %copy-done.10), channel_id=1, source_target_pairs={{0,672},{1,673},{2,674},{3,675},{4,676},{5,677},{6,678},{7,679},{8... | collective-permute-start | bytes 3080 | tf_op jit(solution)/shard_map/ppermute | solution.py:24
  43.1 1.8 %shard_map.85 = (f32[256,1152]{1,0:T(8,128)S(1)}, f32[256,1152]{1,0:T(8,128)S(1)}, f32[8,128]{1,0:T(8,128)S(1)}) custom-call(f32[2]{0:T(128)S(1)} %pad_maximum_fusion.head, s32[3]{0:T(128)S(1)} %pad_add_fusion.start, bf16[256,1152]{1,0:T(8,128)(2,1)S(1)} %get-tuple-element.38.img_u, bf16[256,1152]{1,0:T(8,128)(2,1)S(1)} %get-tuple-element.39.txt_u, ...), custom_call_target="tpu_custom_call" | custom-call | tf_op jit(solution)/shard_map/pallas_call | solution.py:139
  48.0 1.3 copy-done.5
  49.3 1.3 copy-done.7
  51.7 3.0 %shard_map.86 = (f32[256,1152]{1,0:T(8,128)S(1)}, f32[256,1152]{1,0:T(8,128)S(1)}, f32[256,1152]{1,0:T(8,128)S(1)}, f32[256,1152]{1,0:T(8,128)S(1)}, f32[8,128]{1,0:T(8,128)S(1)}) custom-call(f32[2]{0:T(128)S(1)} %pad_maximum_fusion.head, s32[3]{0:T(128)S(1)} %pad_add_fusion.start, bf16[256,1152]{1,0:T(8,128)(2,1)S(1)} %get-tuple-element.38.img_u, ...), custom_call_target="tpu_custom_call" | custom-call | tf_op jit(solution)/shard_map/pallas_call | solution.py:139
  55.5 4.5 %collective-permute-start.5 = (f16[256,1152]{1,0:T(8,128)(2,1)}, f16[256,1152]{1,0:T(8,128)(2,1)}, u32[]{:S(2)}, u32[]{:S(2)}) collective-permute-start(f16[256,1152]{1,0:T(8,128)(2,1)} %multiply_convert_fusion), channel_id=1, source_target_pairs={{0,94},{1,95},{2,0},{3,1},{4,2},{5,3},{6,4},{7,5},{8,6},{9,7},{10,... | collective-permute-start | bytes 1769480 | tf_op jit(solution)/shard_map/ppermute | solution.py:24
  60.1 2.7 %shard_map.87 = (bf16[256,1152]{1,0:T(8,128)(2,1)S(1)}, bf16[256,256]{1,0:T(8,128)(2,1)S(1)}, bf16[256,256]{1,0:T(8,128)(2,1)S(1)}, f32[256,1152]{1,0:T(8,128)S(1)}, f32[8,128]{1,0:T(8,128)S(1)}) custom-call(f32[2]{0:T(128)S(1)} %pad_maximum_fusion.head, s32[3]{0:T(128)S(1)} %pad_add_fusion.start, bf16[256,1152]{1,0:T(8,128)(2,1)S(1)} %get-tuple-element.38.img_u, ...), custom_call_target="tpu_custom_call" | custom-call | tf_op jit(solution)/shard_map/pallas_call | solution.py:139
  62.8 1.1 shard_map.88
  64.8 21.6 %conditional.2 = (f32[8,128]{1,0:T(8,128)S(1)}) conditional(s32[]{:T(128)} %convert_element_type.22, () %tuple.23, f32[8,128]{1,0:T(8,128)S(1)} %get-tuple-element.50), branch_computations={%region_0.1_spmd, %region_1.3_spmd} | conditional | flops 11264 | bytes 106504 | solution.py:202
  64.8 21.6 %all-gather = f32[96,128]{1,0:T(8,128)S(1)} all-gather(f32[8,128]{1,0:T(8,128)S(1)} %param.1), channel_id=2, replica_groups=mesh['y_lo'=4,'core'=2,'z'=12,'x'=4,'y_hi'=2] {'z'}, dimensions={0}, use_global_device_ids=true | all-gather | bytes 53248 | tf_op jit(solution)/shard_map/cond/branch_1_fun/all_gather | solution.py:149
  86.4 2.8 %collective-permute-start.6 = (f16[256,1152]{1,0:T(8,128)(2,1)}, f16[256,1152]{1,0:T(8,128)(2,1)S(1)}, u32[]{:S(2)}, u32[]{:S(2)}) collective-permute-start(f16[256,1152]{1,0:T(8,128)(2,1)} %convert_element_type.23), channel_id=1, source_target_pairs={{0,95},{1,0},{2,1},{3,2},{4,3},{5,4},{6,5},{7,6},{8,7},{9,8},{10,9... | collective-permute-start | bytes 1769480 | tf_op jit(solution)/shard_map/ppermute | solution.py:24
  89.2 12.7 %collective-permute-start.7 = (f16[256,1152]{1,0:T(8,128)(2,1)S(1)}, f16[256,1152]{1,0:T(8,128)(2,1)}, u32[]{:S(2)}, u32[]{:S(2)}) collective-permute-start(f16[256,1152]{1,0:T(8,128)(2,1)S(1)} %convert_element_type.24), channel_id=1, source_target_pairs={{0,96},{1,97},{2,98},{3,99},{4,100},{5,101},{6,102},{7,103},{8,104... | collective-permute-start | bytes 1769480 | tf_op jit(solution)/shard_map/ppermute | solution.py:24
  101.9 33.2 %conditional.3 = (f32[8,128]{1,0:T(8,128)S(1)}) conditional(s32[]{:T(128)} %convert_element_type.22, () %tuple.22, f32[8,128]{1,0:T(8,128)S(1)} %get-tuple-element.69), branch_computations={%region_3.4_spmd, %region_4.7_spmd} | conditional | flops 4096 | bytes 49160 | solution.py:208
  101.9 9.9 %all-gather.1 = f32[32,128]{1,0:T(8,128)S(1)} all-gather(f32[8,128]{1,0:T(8,128)S(1)} %param.3), channel_id=3, replica_groups=mesh['y_lo'=4,'core'=2,'z'=12,'x'=4,'y_hi'=2] {'x'}, dimensions={0}, use_global_device_ids=true | all-gather | bytes 20480 | tf_op jit(solution)/shard_map/cond/branch_1_fun/all_gather | solution.py:153
  111.8 23.3 %psum.6 = f32[8,128]{1,0:T(8,128)S(1)} all-reduce(f32[8,128]{1,0:T(8,128)S(1)} %bitcast_reduce_fusion.1), channel_id=1, replica_groups=mesh['y_lo'=4,'core'=2,'z'=12,'x'=4,'y_hi'=2] {'y_lo','core'}, use_global_device_ids=true, to_apply=%region_6.6 | all-reduce | flops 1024 | bytes 8192 | tf_op jit(solution)/shard_map/cond/branch_1_fun/psum | solution.py:153
  135.1 4.5 %collective-permute-start.8 = (f32[8,128]{1,0:T(8,128)S(1)}, f32[8,128]{1,0:T(8,128)S(1)}, u32[]{:S(2)}, u32[]{:S(2)}) collective-permute-start(f32[8,128]{1,0:T(8,128)S(1)} %get-tuple-element.70), channel_id=1, source_target_pairs={{0,1},{1,0},{2,3},{3,2},{4,5},{5,4},{6,7},{7,6},{8,9},{9,8},{10,11... | collective-permute-start | bytes 12296 | tf_op jit(solution)/shard_map/ppermute | solution.py:158
  139.6 1.7 %multiply_add_fusion = (f32[256,1152]{1,0:T(8,128)S(1)}, f32[256,1152]{1,0:T(8,128)S(1)}) fusion(f32[256,1152]{1,0:T(8,128)S(1)} %get-tuple-element.58, f16[256,1152]{1,0:T(8,128)(2,1)S(1)} %collective-permute-done.6, f16[256,1152]{1,0:T(8,128)(2,1)} %collective-permute-done.5, f32[256,1152]{1,0:T(8,128)S(1)} %get-tuple-element.49, ...), kind=kLoop, calls=%fused_computation.2 | loop fusion | flops 2359296 | bytes 6488064 | tf_op jit(solution)/shard_map/add | solution.py:215
  141.3 2.7 %shard_map.89 = (f32[256,1152]{1,0:T(8,128)}, f32[256,1152]{1,0:T(8,128)}) custom-call(f32[2]{0:T(128)S(1)} %pad_maximum_fusion.head, s32[3]{0:T(128)S(1)} %pad_add_fusion.start, bf16[256,1152]{1,0:T(8,128)(2,1)S(1)} %copy-done.1, bf16[256,1152]{1,0:T(8,128)(2,1)S(1)} %copy-done.3, f32[256,1152]{1,0:T(8,128)S(1)} %get-tuple-element.68.img_total, ...), custom_call_target="tpu_custom_call" | custom-call | tf_op jit(solution)/shard_map/pallas_call | solution.py:139
  145.5 1.2 maximum_multiply_fusion
  (40 shorter events, 9.0 us)
Async XLA Ops:
  0.6 26.7 %copy-start.10 = (s32[256]{0:T(256)S(1)}, s32[256]{0:T(256)}, u32[]{:S(2)}) copy-start(s32[256]{0:T(256)} %param.11) | copy-start | bytes 3076
  0.6 20.9 %collective-permute-start.1 = (bf16[256,1152]{1,0:T(8,128)(2,1)}, bf16[256,1152]{1,0:T(8,128)(2,1)}, u32[]{:S(2)}, u32[]{:S(2)}) collective-permute-start(bf16[256,1152]{1,0:T(8,128)(2,1)} %txt_raw.3), channel_id=1, source_target_pairs={{0,384},{1,385},{2,386},{3,387},{4,388},{5,389},{6,390},{7,391},{8... | collective-permute-start | bytes 1769480 | tf_op jit(solution)/shard_map/ppermute | solution.py:44
  8.9 1.1 copy-start
  10.0 1.1 copy-start.2
  12.0 35.2 %collective-permute-start = (bf16[256,1152]{1,0:T(8,128)(2,1)S(1)}, bf16[256,1152]{1,0:T(8,128)(2,1)S(1)}, u32[]{:S(2)}, u32[]{:S(2)}) collective-permute-start(bf16[256,1152]{1,0:T(8,128)(2,1)S(1)} %get-tuple-element.38.img_u), channel_id=1, source_target_pairs={{0,672},{1,673},{2,674},{3,675},{4,676},{5,677},{6,678},{7,679},{8... | collective-permute-start | bytes 1769480 | tf_op jit(solution)/shard_map/ppermute | solution.py:24
  19.6 27.6 %collective-permute-start.4 = (bf16[256,1152]{1,0:T(8,128)(2,1)S(1)}, bf16[256,1152]{1,0:T(8,128)(2,1)S(1)}, u32[]{:S(2)}, u32[]{:S(2)}) collective-permute-start(bf16[256,1152]{1,0:T(8,128)(2,1)S(1)} %get-tuple-element.39.txt_u), channel_id=1, source_target_pairs={{0,2},{1,3},{2,4},{3,5},{4,6},{5,7},{6,8},{7,9},{8,10},{9,11},{10,... | collective-permute-start | bytes 1769480 | tf_op jit(solution)/shard_map/ppermute | solution.py:24
  21.6 38.5 %collective-permute-start.2 = (bf16[256,1152]{1,0:T(8,128)(2,1)}, bf16[256,1152]{1,0:T(8,128)(2,1)}, u32[]{:S(2)}, u32[]{:S(2)}) collective-permute-start(bf16[256,1152]{1,0:T(8,128)(2,1)} %collective-permute-done.1), channel_id=1, source_target_pairs={{384,1},{385,2},{386,3},{387,4},{388,5},{389,6},{390,7},{391,8},{3... | collective-permute-start | bytes 1769480 | tf_op jit(solution)/shard_map/ppermute | solution.py:44
  27.3 19.7 %collective-permute-start.3 = (s32[256]{0:T(256)S(1)}, s32[256]{0:T(256)S(1)}, u32[]{:S(2)}, u32[]{:S(2)}) collective-permute-start(s32[256]{0:T(256)S(1)} %copy-done.10), channel_id=1, source_target_pairs={{0,672},{1,673},{2,674},{3,675},{4,676},{5,677},{6,678},{7,679},{8... | collective-permute-start | bytes 3080 | tf_op jit(solution)/shard_map/ppermute | solution.py:24
  45.0 1.0 copy-start.4
  46.0 1.0 copy-start.6
  47.2 0.9 copy-start.8
  48.0 1.3 copy-start.5
  49.3 1.3 copy-start.7
  50.6 1.1 copy-start.9
  55.5 79.5 %collective-permute-start.5 = (f16[256,1152]{1,0:T(8,128)(2,1)}, f16[256,1152]{1,0:T(8,128)(2,1)}, u32[]{:S(2)}, u32[]{:S(2)}) collective-permute-start(f16[256,1152]{1,0:T(8,128)(2,1)} %multiply_convert_fusion), channel_id=1, source_target_pairs={{0,94},{1,95},{2,0},{3,1},{4,2},{5,3},{6,4},{7,5},{8,6},{9,7},{10,... | collective-permute-start | bytes 1769480 | tf_op jit(solution)/shard_map/ppermute | solution.py:24
  86.4 48.6 %collective-permute-start.6 = (f16[256,1152]{1,0:T(8,128)(2,1)}, f16[256,1152]{1,0:T(8,128)(2,1)S(1)}, u32[]{:S(2)}, u32[]{:S(2)}) collective-permute-start(f16[256,1152]{1,0:T(8,128)(2,1)} %convert_element_type.23), channel_id=1, source_target_pairs={{0,95},{1,0},{2,1},{3,2},{4,3},{5,4},{6,5},{7,6},{8,7},{9,8},{10,9... | collective-permute-start | bytes 1769480 | tf_op jit(solution)/shard_map/ppermute | solution.py:24
  89.2 45.9 %collective-permute-start.7 = (f16[256,1152]{1,0:T(8,128)(2,1)S(1)}, f16[256,1152]{1,0:T(8,128)(2,1)}, u32[]{:S(2)}, u32[]{:S(2)}) collective-permute-start(f16[256,1152]{1,0:T(8,128)(2,1)S(1)} %convert_element_type.24), channel_id=1, source_target_pairs={{0,96},{1,97},{2,98},{3,99},{4,100},{5,101},{6,102},{7,103},{8,104... | collective-permute-start | bytes 1769480 | tf_op jit(solution)/shard_map/ppermute | solution.py:24
  135.1 9.0 %collective-permute-start.8 = (f32[8,128]{1,0:T(8,128)S(1)}, f32[8,128]{1,0:T(8,128)S(1)}, u32[]{:S(2)}, u32[]{:S(2)}) collective-permute-start(f32[8,128]{1,0:T(8,128)S(1)} %get-tuple-element.70), channel_id=1, source_target_pairs={{0,1},{1,0},{2,3},{3,2},{4,5},{5,4},{6,7},{7,6},{8,9},{9,8},{10,11... | collective-permute-start | bytes 12296 | tf_op jit(solution)/shard_map/ppermute | solution.py:158
  139.6 1.7 %copy-start.1 = (bf16[256,1152]{1,0:T(8,128)(2,1)S(1)}, bf16[256,1152]{1,0:T(8,128)(2,1)}, u32[]{:S(2)}) copy-start(bf16[256,1152]{1,0:T(8,128)(2,1)} %img_raw.3) | copy-start | bytes 1769476
  139.6 1.7 %copy-start.3 = (bf16[256,1152]{1,0:T(8,128)(2,1)S(1)}, bf16[256,1152]{1,0:T(8,128)(2,1)}, u32[]{:S(2)}) copy-start(bf16[256,1152]{1,0:T(8,128)(2,1)} %txt_raw.3) | copy-start | bytes 1769476

commit v5 on v4

--- a/solution.py
+++ b/solution.py
@@ -12,6 +12,7 @@
 SIZES = (4, 2, 12, 4, 2)
 N_OUTER, N_INNER = 8, 96
 SEND_SCALE = 64.0
+CODE = 128
 VMEM_LIMIT = 14 * 1024 * 1024
 
 
@@ -80,42 +81,56 @@
     return lax.dot_general(a, b, (((0,), (0,)), ((), ())), preferred_element_type=jnp.float32)
 
 
-def unit_kernel(head, start, img_raw, txt_raw, img_u, txt_u):
-    img_u[...] = unit_of(img_raw)
+def unit_kernel(head, start, img_raw, txt_raw, pos, img_u, txt_u):
+    width = txt_u.shape[1]
+    img_u[:, :width] = unit_of(img_raw)
     txt_u[...] = unit_of(txt_raw)
-
-
-def first_kernel(head, start, img_u, txt_u, pos, img_acc, txt_acc, stats):
+    lane = lax.broadcasted_iota(jnp.int32, (pos.shape[0], CODE), 1)
+    index = pos[...]
+    code = jnp.where(lane == 0, index & 255, (index >> 8) & 255)
+    code = jnp.where(lane == 2, index >> 16, code)
+    img_u[:, width:] = code.astype(jnp.float32).astype(jnp.bfloat16)
+
+
+def decoded(img2, width):
+    code = img2[:, width:].astype(jnp.float32)
+    index = code[:, 0:1] + 256.0 * code[:, 1:2] + 65536.0 * code[:, 2:3]
+    return img2[:, :width], index.astype(jnp.int32)
+
+
+def first_kernel(head, start, img_u, txt_u, pos, slope, stats):
     stats[...] = jnp.zeros_like(stats)
-    s = score(img_u[...], txt_u[...], pos[...], start[0], head, stats)
-    img_acc[...] = times(s, txt_u[...])
-    txt_acc[...] = times_t(s, img_u[...])
+    img = img_u[:, : txt_u.shape[1]]
+    slope[...] = score(img, txt_u[...], pos[...], start[0], head, stats)
 
 
 def second_kernel(
-    head, start, img_u, txt_u, far_u, img2_u, pos, pos2, img_in, txt_in, stats_in,
+    head, start, img_u, txt_u, far_u, img2_u, pos, slope, stats_in,
     img_acc, img2_acc, txt_acc, far_acc, stats,
 ):
     stats[...] = stats_in[...]
-    s = score(img_u[...], far_u[...], pos[...], start[2], head, stats)
-    s2 = score(img2_u[...], far_u[...], pos2[...], start[2], head, stats)
-    s0 = score(img2_u[...], txt_u[...], pos2[...], start[0], head, stats)
-    far_acc[...] = times_t(s, img_u[...]) + times_t(s2, img2_u[...])
-    img_acc[...] = img_in[...] + times(s, far_u[...])
+    img = img_u[:, : txt_u.shape[1]]
+    img2, pos2 = decoded(img2_u, txt_u.shape[1])
+    s = score(img, far_u[...], pos[...], start[2], head, stats)
+    s2 = score(img2, far_u[...], pos2, start[2], head, stats)
+    s0 = score(img2, txt_u[...], pos2, start[0], head, stats)
+    far_acc[...] = SEND_SCALE * (times_t(s, img) + times_t(s2, img2))
+    img_acc[...] = times(slope[...], txt_u[...]) + times(s, far_u[...])
     img2_acc[...] = times(s2, far_u[...]) + times(s0, txt_u[...])
-    txt_acc[...] = txt_in[...] + times_t(s0, img2_u[...])
-
-
-def third_kernel(head, start, img_u, img2_u, mid_raw, pos, pos2, stats_in, mid_u, slope, slope2, mid_acc, stats):
+    txt_acc[...] = times_t(slope[...], img) + times_t(s0, img2)
+
+
+def third_kernel(head, start, img_u, img2_u, mid_raw, pos, stats_in, mid_u, slope, slope2, mid_acc, stats):
     stats[...] = stats_in[...]
     mid = unit_of(mid_raw)
     mid_u[...] = mid
-    s = score(img_u[...], mid, pos[...], start[1], head, stats)
-    s2 = score(img2_u[...], mid, pos2[...], start[1], head, stats)
+    img = img_u[:, : mid.shape[1]]
+    img2, pos2 = decoded(img2_u, mid.shape[1])
+    s = score(img, mid, pos[...], start[1], head, stats)
+    s2 = score(img2, mid, pos2, start[1], head, stats)
     slope[...] = s
     slope2[...] = s2
-    total = times_t(s, img_u[...]) + times_t(s2, img2_u[...])
-    mid_acc[...] = SEND_SCALE * total
+    mid_acc[...] = SEND_SCALE * (times_t(s, img) + times_t(s2, img2))
 
 
 def fourth_kernel(head, start, mid_u, slope, slope2, img_in, img2_in, img_acc, img2_acc):
@@ -175,22 +190,19 @@
     sums = jax.ShapeDtypeStruct((8, 128), f32)
 
     mid_raw = one_step_in_two(text_emb, 1)
-    pos2 = moved(positive, -1, 0).reshape(rows, 1)
-    img_u, txt_u = call(unit_kernel, (head, start, image_emb, text_emb), [unit, unit])
+    marked = jax.ShapeDtypeStruct((rows, width + CODE), bf16)
+    img_u, txt_u = call(unit_kernel, (head, start, image_emb, text_emb, pos), [marked, unit])
     img2_u = moved(img_u, -1, 0)
     far_u = moved(txt_u, 0, 2)
-    img_acc, txt_acc, stats = call(
-        first_kernel, (head, start, img_u, txt_u, pos), [wide, wide, sums]
-    )
+    slope, stats = call(first_kernel, (head, start, img_u, txt_u, pos), [pair, sums])
     img_acc, img2_acc, txt_acc, far_acc, stats = call(
         second_kernel,
-        (head, start, img_u, txt_u, far_u, img2_u, pos, pos2, img_acc, txt_acc, stats),
+        (head, start, img_u, txt_u, far_u, img2_u, pos, slope, stats),
         [wide, wide, wide, wide, sums],
     )
-    far_back = moved((SEND_SCALE * far_acc).astype(jnp.float16), 0, -2)
     mid_u, slope, slope2, mid_acc, stats = call(
         third_kernel,
-        (head, start, img_u, img2_u, mid_raw, pos, pos2, stats),
+        (head, start, img_u, img2_u, mid_raw, pos, stats),
         [unit, pair, pair, wide, sums],
     )
     img_acc, img2_acc = call(
@@ -200,11 +212,13 @@
     )
     always = lax.optimization_barrier(jnp.bool_(True))
     stats = lax.cond(always, sum_z, jnp.zeros_like, stats)
-    stats, mid_half, img_half = lax.optimization_barrier(
-        (stats, mid_acc.astype(jnp.float16), img2_acc.astype(jnp.float16))
+    half = jnp.float16
+    stats, mid_half, img_half, far_half = lax.optimization_barrier(
+        (stats, mid_acc.astype(half), img2_acc.astype(half), far_acc.astype(half))
     )
     mid_back = moved(mid_half, 0, -1)
     img_back = moved(img_half, 1, 0)
+    far_back = moved(far_half, 0, -2)
     stats = lax.cond(always, sum_x_y_lo, jnp.zeros_like, stats)
     stats, far_back, mid_back, img_back = lax.optimization_barrier(
         (stats, far_back, mid_back, img_back)

time: 150 us -> 149 us (level)
  waiting for transfers between devices: 0.03 us -> 25.8 us
  starting transfers between devices: 62.1 us -> 40.7 us
  local copies, waits for them, and re-layouts: 9.55 us -> 5.44 us
    ppermute x6 -> x5, starting transfers between devices: 45.2 us -> 24.6 us  [moved(): return lax.ppermute(block, AXES, route)]
    ppermute x6 -> x5, waiting for transfers between devices: 0.02 us -> 15.8 us  [moved(): return lax.ppermute(block, AXES, route)]
    ppermute x2, waiting for transfers between devices: 0.01 us -> 9.97 us  [one_step_in_two(): return lax.ppermute(lax.ppermute(block, AXES, first), AXES, ends)]
    all_gather x1, blocking collectives: 21.6 us -> 15.5 us  [sum_z(): return jnp.sum(lax.all_gather(s, 'z'), axis=0)]
    psum x1, blocking collectives: 23.3 us -> 28.9 us  [sum_x_y_lo(): return lax.psum(jnp.sum(lax.all_gather(s, 'x'), axis=0), ('y_lo', 'core'))]
    unnamed x22 -> x12, local copies, waits for them, and re-layouts: 8.62 us -> 4.02 us
  transfers between devices with their start and end apart: 9 -> 8, of which waited for: 0 -> 3; matrix products, arithmetic and copies ran while one was open for 3% -> 2% of each run, Pallas kernels for 8% -> 6%
where the time goes in v5:
time: 149 us; the launch traced here: 148 us
  blocking collectives  54.4 us (37%)
  starting transfers between devices  40.7 us (27%)
  waiting for transfers between devices  25.8 us (17%)
  Pallas kernels  12 us (8%)
  local copies, waits for them, and re-layouts  5.44 us (4%)
  other arithmetic  5.05 us (3%)
  between operations  4.67 us (3%)
    psum x1, blocking collectives, sum_x_y_lo(): return lax.psum(jnp.sum(lax.all_gather(s, 'x'), axis=0), ('y_lo', 'core'))  28.9 us
    ppermute x5, starting transfers between devices, moved(): return lax.ppermute(block, AXES, route)  24.6 us
    ppermute x5, waiting for transfers between devices, moved(): return lax.ppermute(block, AXES, route)  15.8 us
    all_gather x1, blocking collectives, sum_z(): return jnp.sum(lax.all_gather(s, 'z'), axis=0)  15.5 us
    ppermute x2, starting transfers between devices, one_step_in_two(): return lax.ppermute(lax.ppermute(block, AXES, first), AXES, ends)  12.5 us
    pallas_call x6, Pallas kernels, call(): pl.pallas_call(kernel, in_specs=scalars + arrays, out_specs=[pl.BlockSpec...  12 us
    all_gather x1, blocking collectives, sum_x_y_lo(): return lax.psum(jnp.sum(lax.all_gather(s, 'x'), axis=0), ('y_lo', 'core'))  10 us
    ppermute x2, waiting for transfers between devices, one_step_in_two(): return lax.ppermute(lax.ppermute(block, AXES, first), AXES, ends)  9.97 us
  transfers between devices with their start and end apart: 8, of which 3 were waited for; matrix products, arithmetic and copies ran while one was open for 2% of the time, Pallas kernels for 6%

profile of v5, /device:TPU:1, one launch (start us, length us, event | category | flops | bytes accessed | tf_op | source)
XLA Modules:
  0.0 148.1 jit_solution(9297332438464277875)
XLA Ops:
  0.6 6.7 %collective-permute-start.1 = (bf16[256,1152]{1,0:T(8,128)(2,1)}, bf16[256,1152]{1,0:T(8,128)(2,1)}, u32[]{:S(2)}, u32[]{:S(2)}) collective-permute-start(bf16[256,1152]{1,0:T(8,128)(2,1)} %txt_raw.3), channel_id=1, source_target_pairs={{0,384},{1,385},{2,386},{3,387},{4,388},{5,389},{6,390},{7,391},{8... | collective-permute-start | bytes 1769480 | tf_op jit(solution)/shard_map/ppermute | solution.py:45
  9.8 1.1 copy-done
  10.8 1.1 copy-done.2
  12.9 7.6 %collective-permute-start = (bf16[256,1280]{1,0:T(8,128)(2,1)S(1)}, bf16[256,1280]{1,0:T(8,128)(2,1)S(1)}, u32[]{:S(2)}, u32[]{:S(2)}) collective-permute-start(bf16[256,1280]{1,0:T(8,128)(2,1)S(1)} %get-tuple-element.38.img_u), channel_id=1, source_target_pairs={{0,672},{1,673},{2,674},{3,675},{4,676},{5,677},{6,678},{7,679},{8... | collective-permute-start | bytes 1966088 | tf_op jit(solution)/shard_map/ppermute | solution.py:25
  20.6 1.9 %collective-permute-start.3 = (bf16[256,1152]{1,0:T(8,128)(2,1)S(1)}, bf16[256,1152]{1,0:T(8,128)(2,1)S(1)}, u32[]{:S(2)}, u32[]{:S(2)}) collective-permute-start(bf16[256,1152]{1,0:T(8,128)(2,1)S(1)} %get-tuple-element.39.txt_u), channel_id=1, source_target_pairs={{0,2},{1,3},{2,4},{3,5},{4,6},{5,7},{6,8},{7,9},{8,10},{9,11},{10,... | collective-permute-start | bytes 1769480 | tf_op jit(solution)/shard_map/ppermute | solution.py:25
  22.5 5.8 %collective-permute-start.2 = (bf16[256,1152]{1,0:T(8,128)(2,1)}, bf16[256,1152]{1,0:T(8,128)(2,1)}, u32[]{:S(2)}, u32[]{:S(2)}) collective-permute-start(bf16[256,1152]{1,0:T(8,128)(2,1)} %collective-permute-done.1), channel_id=1, source_target_pairs={{384,1},{385,2},{386,3},{387,4},{388,5},{389,6},{390,7},{391,8},{3... | collective-permute-start | bytes 1769480 | tf_op jit(solution)/shard_map/ppermute | solution.py:45
  28.3 1.1 shard_map.85
  29.4 15.7 %collective-permute-done.3.far_u = bf16[256,1152]{1,0:T(8,128)(2,1)S(1)} collective-permute-done((bf16[256,1152]{1,0:T(8,128)(2,1)S(1)}, bf16[256,1152]{1,0:T(8,128)(2,1)S(1)}, u32[]{:S(2)}, u32[]{:S(2)}) %collective-permute-start.3) | collective-permute-done | bytes 589856 | tf_op jit(solution)/shard_map/ppermute | solution.py:25
  46.0 1.1 copy-done.5
  47.1 3.3 %shard_map.86 = (f32[256,1152]{1,0:T(8,128)S(1)}, f32[256,1152]{1,0:T(8,128)S(1)}, f32[256,1152]{1,0:T(8,128)S(1)}, f32[256,1152]{1,0:T(8,128)S(1)}, f32[8,128]{1,0:T(8,128)S(1)}) custom-call(f32[2]{0:T(128)S(1)} %pad_maximum_fusion.head, s32[3]{0:T(128)S(1)} %pad_add_fusion.start, bf16[256,1280]{1,0:T(8,128)(2,1)S(1)} %get-tuple-element.38.img_u, ...), custom_call_target="tpu_custom_call" | custom-call | tf_op jit(solution)/shard_map/pallas_call | solution.py:154
  50.4 10.0 %collective-permute-done.2.mid_raw = bf16[256,1152]{1,0:T(8,128)(2,1)} collective-permute-done((bf16[256,1152]{1,0:T(8,128)(2,1)}, bf16[256,1152]{1,0:T(8,128)(2,1)}, u32[]{:S(2)}, u32[]{:S(2)}) %collective-permute-start.2) | collective-permute-done | bytes 589856 | tf_op jit(solution)/shard_map/ppermute | solution.py:45
  60.4 2.7 %shard_map.87 = (bf16[256,1152]{1,0:T(8,128)(2,1)S(1)}, bf16[256,256]{1,0:T(8,128)(2,1)S(1)}, bf16[256,256]{1,0:T(8,128)(2,1)S(1)}, f32[256,1152]{1,0:T(8,128)S(1)}, f32[8,128]{1,0:T(8,128)S(1)}) custom-call(f32[2]{0:T(128)S(1)} %pad_maximum_fusion.head, s32[3]{0:T(128)S(1)} %pad_add_fusion.start, bf16[256,1280]{1,0:T(8,128)(2,1)S(1)} %get-tuple-element.38.img_u, ...), custom_call_target="tpu_custom_call" | custom-call | tf_op jit(solution)/shard_map/pallas_call | solution.py:154
  65.9 15.5 %conditional.2 = (f32[8,128]{1,0:T(8,128)S(1)}) conditional(s32[]{:T(128)} %convert_element_type.22, () %tuple.23, f32[8,128]{1,0:T(8,128)S(1)} %get-tuple-element.49), branch_computations={%region_0.1_spmd, %region_1.3_spmd} | conditional | flops 11264 | bytes 106504 | solution.py:214
  65.9 15.5 %all-gather = f32[96,128]{1,0:T(8,128)S(1)} all-gather(f32[8,128]{1,0:T(8,128)S(1)} %param.1), channel_id=2, replica_groups=mesh['y_lo'=4,'core'=2,'z'=12,'x'=4,'y_hi'=2] {'z'}, dimensions={0}, use_global_device_ids=true | all-gather | bytes 53248 | tf_op jit(solution)/shard_map/cond/branch_1_fun/all_gather | solution.py:164
  81.5 1.9 %collective-permute-start.4 = (f16[256,1152]{1,0:T(8,128)(2,1)S(1)}, f16[256,1152]{1,0:T(8,128)(2,1)S(1)}, u32[]{:S(2)}, u32[]{:S(2)}) collective-permute-start(f16[256,1152]{1,0:T(8,128)(2,1)S(1)} %convert_element_type.25), channel_id=1, source_target_pairs={{0,94},{1,95},{2,0},{3,1},{4,2},{5,3},{6,4},{7,5},{8,6},{9,7},{10,... | collective-permute-start | bytes 1769480 | tf_op jit(solution)/shard_map/ppermute | solution.py:25
  83.4 3.5 %collective-permute-start.5 = (f16[256,1152]{1,0:T(8,128)(2,1)}, f16[256,1152]{1,0:T(8,128)(2,1)}, u32[]{:S(2)}, u32[]{:S(2)}) collective-permute-start(f16[256,1152]{1,0:T(8,128)(2,1)} %convert_element_type.23), channel_id=1, source_target_pairs={{0,95},{1,0},{2,1},{3,2},{4,3},{5,4},{6,5},{7,6},{8,7},{9,8},{10,9... | collective-permute-start | bytes 1769480 | tf_op jit(solution)/shard_map/ppermute | solution.py:25
  86.9 9.7 %collective-permute-start.6 = (f16[256,1152]{1,0:T(8,128)(2,1)}, f16[256,1152]{1,0:T(8,128)(2,1)}, u32[]{:S(2)}, u32[]{:S(2)}) collective-permute-start(f16[256,1152]{1,0:T(8,128)(2,1)} %convert_element_type.24), channel_id=1, source_target_pairs={{0,96},{1,97},{2,98},{3,99},{4,100},{5,101},{6,102},{7,103},{8,104... | collective-permute-start | bytes 1769480 | tf_op jit(solution)/shard_map/ppermute | solution.py:25
  96.5 38.9 %conditional.3 = (f32[8,128]{1,0:T(8,128)S(1)}) conditional(s32[]{:T(128)} %convert_element_type.22, () %tuple.22, f32[8,128]{1,0:T(8,128)S(1)} %get-tuple-element.69), branch_computations={%region_3.4_spmd, %region_4.7_spmd} | conditional | flops 4096 | bytes 49160 | solution.py:222
  96.5 10.0 %all-gather.1 = f32[32,128]{1,0:T(8,128)S(1)} all-gather(f32[8,128]{1,0:T(8,128)S(1)} %param.3), channel_id=3, replica_groups=mesh['y_lo'=4,'core'=2,'z'=12,'x'=4,'y_hi'=2] {'x'}, dimensions={0}, use_global_device_ids=true | all-gather | bytes 20480 | tf_op jit(solution)/shard_map/cond/branch_1_fun/all_gather | solution.py:168
  106.5 28.9 %psum.6 = f32[8,128]{1,0:T(8,128)S(1)} all-reduce(f32[8,128]{1,0:T(8,128)S(1)} %bitcast_reduce_fusion.1), channel_id=1, replica_groups=mesh['y_lo'=4,'core'=2,'z'=12,'x'=4,'y_hi'=2] {'y_lo','core'}, use_global_device_ids=true, to_apply=%region_6.6 | all-reduce | flops 1024 | bytes 8192 | tf_op jit(solution)/shard_map/cond/branch_1_fun/psum | solution.py:168
  135.5 3.6 %collective-permute-start.7 = (f32[8,128]{1,0:T(8,128)S(1)}, f32[8,128]{1,0:T(8,128)S(1)}, u32[]{:S(2)}, u32[]{:S(2)}) collective-permute-start(f32[8,128]{1,0:T(8,128)S(1)} %get-tuple-element.70), channel_id=1, source_target_pairs={{0,1},{1,0},{2,3},{3,2},{4,5},{5,4},{6,7},{7,6},{8,9},{9,8},{10,11... | collective-permute-start | bytes 12296 | tf_op jit(solution)/shard_map/ppermute | solution.py:173
  139.1 1.7 %multiply_add_fusion = (f32[256,1152]{1,0:T(8,128)S(1)}, f32[256,1152]{1,0:T(8,128)S(1)}) fusion(f32[256,1152]{1,0:T(8,128)S(1)} %get-tuple-element.58, f16[256,1152]{1,0:T(8,128)(2,1)} %collective-permute-done.5, f16[256,1152]{1,0:T(8,128)(2,1)S(1)} %collective-permute-done.4, f32[256,1152]{1,0:T(8,128)S(1)} %get-tuple-element.48, ...), kind=kLoop, calls=%fused_computation.2 | loop fusion | flops 2359296 | bytes 6488064 | tf_op jit(solution)/shard_map/add | solution.py:229
  140.9 2.7 %shard_map.89 = (f32[256,1152]{1,0:T(8,128)}, f32[256,1152]{1,0:T(8,128)}) custom-call(f32[2]{0:T(128)S(1)} %pad_maximum_fusion.head, s32[3]{0:T(128)S(1)} %pad_add_fusion.start, bf16[256,1152]{1,0:T(8,128)(2,1)S(1)} %copy-done.1, bf16[256,1152]{1,0:T(8,128)(2,1)S(1)} %copy-done.3, f32[256,1152]{1,0:T(8,128)S(1)} %get-tuple-element.68.img_total, ...), custom_call_target="tpu_custom_call" | custom-call | tf_op jit(solution)/shard_map/pallas_call | solution.py:154
  145.7 1.2 maximum_multiply_fusion
  (27 shorter events, 6.6 us)
Async XLA Ops:
  0.6 21.9 %collective-permute-start.1 = (bf16[256,1152]{1,0:T(8,128)(2,1)}, bf16[256,1152]{1,0:T(8,128)(2,1)}, u32[]{:S(2)}, u32[]{:S(2)}) collective-permute-start(bf16[256,1152]{1,0:T(8,128)(2,1)} %txt_raw.3), channel_id=1, source_target_pairs={{0,384},{1,385},{2,386},{3,387},{4,388},{5,389},{6,390},{7,391},{8... | collective-permute-start | bytes 1769480 | tf_op jit(solution)/shard_map/ppermute | solution.py:45
  9.8 1.1 copy-start
  10.8 1.1 copy-start.2
  12.9 33.1 %collective-permute-start = (bf16[256,1280]{1,0:T(8,128)(2,1)S(1)}, bf16[256,1280]{1,0:T(8,128)(2,1)S(1)}, u32[]{:S(2)}, u32[]{:S(2)}) collective-permute-start(bf16[256,1280]{1,0:T(8,128)(2,1)S(1)} %get-tuple-element.38.img_u), channel_id=1, source_target_pairs={{0,672},{1,673},{2,674},{3,675},{4,676},{5,677},{6,678},{7,679},{8... | collective-permute-start | bytes 1966088 | tf_op jit(solution)/shard_map/ppermute | solution.py:25
  20.6 24.6 %collective-permute-start.3 = (bf16[256,1152]{1,0:T(8,128)(2,1)S(1)}, bf16[256,1152]{1,0:T(8,128)(2,1)S(1)}, u32[]{:S(2)}, u32[]{:S(2)}) collective-permute-start(bf16[256,1152]{1,0:T(8,128)(2,1)S(1)} %get-tuple-element.39.txt_u), channel_id=1, source_target_pairs={{0,2},{1,3},{2,4},{3,5},{4,6},{5,7},{6,8},{7,9},{8,10},{9,11},{10,... | collective-permute-start | bytes 1769480 | tf_op jit(solution)/shard_map/ppermute | solution.py:25
  22.5 37.9 %collective-permute-start.2 = (bf16[256,1152]{1,0:T(8,128)(2,1)}, bf16[256,1152]{1,0:T(8,128)(2,1)}, u32[]{:S(2)}, u32[]{:S(2)}) collective-permute-start(bf16[256,1152]{1,0:T(8,128)(2,1)} %collective-permute-done.1), channel_id=1, source_target_pairs={{384,1},{385,2},{386,3},{387,4},{388,5},{389,6},{390,7},{391,8},{3... | collective-permute-start | bytes 1769480 | tf_op jit(solution)/shard_map/ppermute | solution.py:45
  45.2 0.8 copy-start.4
  46.0 1.1 copy-start.5
  81.5 54.0 %collective-permute-start.4 = (f16[256,1152]{1,0:T(8,128)(2,1)S(1)}, f16[256,1152]{1,0:T(8,128)(2,1)S(1)}, u32[]{:S(2)}, u32[]{:S(2)}) collective-permute-start(f16[256,1152]{1,0:T(8,128)(2,1)S(1)} %convert_element_type.25), channel_id=1, source_target_pairs={{0,94},{1,95},{2,0},{3,1},{4,2},{5,3},{6,4},{7,5},{8,6},{9,7},{10,... | collective-permute-start | bytes 1769480 | tf_op jit(solution)/shard_map/ppermute | solution.py:25
  83.4 52.1 %collective-permute-start.5 = (f16[256,1152]{1,0:T(8,128)(2,1)}, f16[256,1152]{1,0:T(8,128)(2,1)}, u32[]{:S(2)}, u32[]{:S(2)}) collective-permute-start(f16[256,1152]{1,0:T(8,128)(2,1)} %convert_element_type.23), channel_id=1, source_target_pairs={{0,95},{1,0},{2,1},{3,2},{4,3},{5,4},{6,5},{7,6},{8,7},{9,8},{10,9... | collective-permute-start | bytes 1769480 | tf_op jit(solution)/shard_map/ppermute | solution.py:25
  86.9 48.6 %collective-permute-start.6 = (f16[256,1152]{1,0:T(8,128)(2,1)}, f16[256,1152]{1,0:T(8,128)(2,1)}, u32[]{:S(2)}, u32[]{:S(2)}) collective-permute-start(f16[256,1152]{1,0:T(8,128)(2,1)} %convert_element_type.24), channel_id=1, source_target_pairs={{0,96},{1,97},{2,98},{3,99},{4,100},{5,101},{6,102},{7,103},{8,104... | collective-permute-start | bytes 1769480 | tf_op jit(solution)/shard_map/ppermute | solution.py:25
  135.5 8.3 %collective-permute-start.7 = (f32[8,128]{1,0:T(8,128)S(1)}, f32[8,128]{1,0:T(8,128)S(1)}, u32[]{:S(2)}, u32[]{:S(2)}) collective-permute-start(f32[8,128]{1,0:T(8,128)S(1)} %get-tuple-element.70), channel_id=1, source_target_pairs={{0,1},{1,0},{2,3},{3,2},{4,5},{5,4},{6,7},{7,6},{8,9},{9,8},{10,11... | collective-permute-start | bytes 12296 | tf_op jit(solution)/shard_map/ppermute | solution.py:173
  139.1 1.8 %copy-start.1 = (bf16[256,1152]{1,0:T(8,128)(2,1)S(1)}, bf16[256,1152]{1,0:T(8,128)(2,1)}, u32[]{:S(2)}) copy-start(bf16[256,1152]{1,0:T(8,128)(2,1)} %img_raw.3) | copy-start | bytes 1769476
  139.1 1.8 %copy-start.3 = (bf16[256,1152]{1,0:T(8,128)(2,1)S(1)}, bf16[256,1152]{1,0:T(8,128)(2,1)}, u32[]{:S(2)}) copy-start(bf16[256,1152]{1,0:T(8,128)(2,1)} %txt_raw.3) | copy-start | bytes 1769476

commit v6 on v5

--- a/solution.py
+++ b/solution.py
@@ -160,12 +160,13 @@
     )(*ins)
 
 
-def sum_z(s):
-    return jnp.sum(lax.all_gather(s, "z"), axis=0)
-
-
-def sum_x_y_lo(s):
-    return lax.psum(jnp.sum(lax.all_gather(s, "x"), axis=0), ("y_lo", "core"))
+def sum_y_lo(s):
+    return lax.psum(s, ("y_lo", "core"))
+
+
+def sum_z_x(s):
+    s = jnp.sum(lax.all_gather(s, "z"), axis=0)
+    return jnp.sum(lax.all_gather(s, "x"), axis=0)
 
 
 def sum_last(s):
@@ -211,17 +212,17 @@
         [wide, wide],
     )
     always = lax.optimization_barrier(jnp.bool_(True))
-    stats = lax.cond(always, sum_z, jnp.zeros_like, stats)
+    stats = lax.cond(always, sum_y_lo, jnp.zeros_like, stats)
     half = jnp.float16
     stats, mid_half, img_half, far_half = lax.optimization_barrier(
         (stats, mid_acc.astype(half), img2_acc.astype(half), far_acc.astype(half))
     )
+    far_back = moved(far_half, 0, -2)
+    img_back = moved(img_half, 1, 0)
     mid_back = moved(mid_half, 0, -1)
-    img_back = moved(img_half, 1, 0)
-    far_back = moved(far_half, 0, -2)
-    stats = lax.cond(always, sum_x_y_lo, jnp.zeros_like, stats)
-    stats, far_back, mid_back, img_back = lax.optimization_barrier(
-        (stats, far_back, mid_back, img_back)
+    stats = lax.cond(always, sum_z_x, jnp.zeros_like, stats)
+    stats, mid_back, img_back, far_back = lax.optimization_barrier(
+        (stats, mid_back, img_back, far_back)
     )
     totals = jnp.sum(sum_last(stats), axis=1)
 

time: 149 us -> 162 us (1.087)
  the two profiles are of different devices: /device:TPU:1 before, /device:TPU:4 now
where the time goes in v6:
time: 162 us; the launch traced here: 161 us
  blocking collectives  86.9 us (54%)
  starting transfers between devices  39 us (24%)
  Pallas kernels  12 us (7%)
  waiting for transfers between devices  7.97 us (5%)
  local copies, waits for them, and re-layouts  5.44 us (3%)
  other arithmetic  5.04 us (3%)
  between operations  4.66 us (3%)
    all_gather x1, blocking collectives, sum_z_x(): return jnp.sum(lax.all_gather(s, 'x'), axis=0)  36.5 us
    all_gather x1, blocking collectives, sum_z_x(): s = jnp.sum(lax.all_gather(s, 'z'), axis=0)  30.6 us
    psum x1, blocking collectives, sum_y_lo(): return lax.psum(s, ('y_lo', 'core'))  19.8 us
    ppermute x2, starting transfers between devices, one_step_in_two(): return lax.ppermute(lax.ppermute(block, AXES, first), AXES, ends)  19.2 us
    ppermute x5, starting transfers between devices, moved(): return lax.ppermute(block, AXES, route)  13.7 us
    pallas_call x6, Pallas kernels, call(): pl.pallas_call(kernel, in_specs=scalars + arrays, out_specs=[pl.BlockSpec...  12 us
    ppermute x2, waiting for transfers between devices, one_step_in_two(): return lax.ppermute(lax.ppermute(block, AXES, first), AXES, ends)  6.25 us
    ppermute x1, starting transfers between devices, sum_last(): return s + lax.ppermute(s, AXES, route)  6.08 us
  transfers between devices with their start and end apart: 8, of which 3 were waited for; matrix products, arithmetic and copies ran while one was open for 2% of the time, Pallas kernels for 5%

profile of v6, /device:TPU:4, one launch (start us, length us, event | category | flops | bytes accessed | tf_op | source)
XLA Modules:
  0.0 160.9 jit_solution(5192003181006802535)
XLA Ops:
  0.6 4.5 %collective-permute-start.1 = (bf16[256,1152]{1,0:T(8,128)(2,1)}, bf16[256,1152]{1,0:T(8,128)(2,1)}, u32[]{:S(2)}, u32[]{:S(2)}) collective-permute-start(bf16[256,1152]{1,0:T(8,128)(2,1)} %txt_raw.3), channel_id=1, source_target_pairs={{0,384},{1,385},{2,386},{3,387},{4,388},{5,389},{6,390},{7,391},{8... | collective-permute-start | bytes 1769480 | tf_op jit(solution)/shard_map/ppermute | solution.py:45
  7.5 1.1 copy-done
  10.7 2.4 %collective-permute-start = (bf16[256,1280]{1,0:T(8,128)(2,1)S(1)}, bf16[256,1280]{1,0:T(8,128)(2,1)S(1)}, u32[]{:S(2)}, u32[]{:S(2)}) collective-permute-start(bf16[256,1280]{1,0:T(8,128)(2,1)S(1)} %get-tuple-element.38.img_u), channel_id=1, source_target_pairs={{0,672},{1,673},{2,674},{3,675},{4,676},{5,677},{6,678},{7,679},{8... | collective-permute-start | bytes 1966088 | tf_op jit(solution)/shard_map/ppermute | solution.py:25
  13.1 3.1 %collective-permute-start.3 = (bf16[256,1152]{1,0:T(8,128)(2,1)S(1)}, bf16[256,1152]{1,0:T(8,128)(2,1)S(1)}, u32[]{:S(2)}, u32[]{:S(2)}) collective-permute-start(bf16[256,1152]{1,0:T(8,128)(2,1)S(1)} %get-tuple-element.39.txt_u), channel_id=1, source_target_pairs={{0,2},{1,3},{2,4},{3,5},{4,6},{5,7},{6,8},{7,9},{8,10},{9,11},{10,... | collective-permute-start | bytes 1769480 | tf_op jit(solution)/shard_map/ppermute | solution.py:25
  16.3 1.5 collective-permute-done.1
  17.8 14.7 %collective-permute-start.2 = (bf16[256,1152]{1,0:T(8,128)(2,1)}, bf16[256,1152]{1,0:T(8,128)(2,1)}, u32[]{:S(2)}, u32[]{:S(2)}) collective-permute-start(bf16[256,1152]{1,0:T(8,128)(2,1)} %collective-permute-done.1), channel_id=1, source_target_pairs={{384,1},{385,2},{386,3},{387,4},{388,5},{389,6},{390,7},{391,8},{3... | collective-permute-start | bytes 1769480 | tf_op jit(solution)/shard_map/ppermute | solution.py:45
  32.4 1.1 shard_map.85
  33.6 1.7 %collective-permute-done.3.far_u = bf16[256,1152]{1,0:T(8,128)(2,1)S(1)} collective-permute-done((bf16[256,1152]{1,0:T(8,128)(2,1)S(1)}, bf16[256,1152]{1,0:T(8,128)(2,1)S(1)}, u32[]{:S(2)}, u32[]{:S(2)}) %collective-permute-start.3) | collective-permute-done | bytes 589856 | tf_op jit(solution)/shard_map/ppermute | solution.py:25
  36.1 1.1 copy-done.5
  37.2 3.3 %shard_map.86 = (f32[256,1152]{1,0:T(8,128)S(1)}, f32[256,1152]{1,0:T(8,128)S(1)}, f32[256,1152]{1,0:T(8,128)S(1)}, f32[256,1152]{1,0:T(8,128)S(1)}, f32[8,128]{1,0:T(8,128)S(1)}) custom-call(f32[2]{0:T(128)S(1)} %pad_maximum_fusion.head, s32[3]{0:T(128)S(1)} %pad_add_fusion.start, bf16[256,1280]{1,0:T(8,128)(2,1)S(1)} %get-tuple-element.38.img_u, ...), custom_call_target="tpu_custom_call" | custom-call | tf_op jit(solution)/shard_map/pallas_call | solution.py:154
  40.5 4.8 %collective-permute-done.2.mid_raw = bf16[256,1152]{1,0:T(8,128)(2,1)} collective-permute-done((bf16[256,1152]{1,0:T(8,128)(2,1)}, bf16[256,1152]{1,0:T(8,128)(2,1)}, u32[]{:S(2)}, u32[]{:S(2)}) %collective-permute-start.2) | collective-permute-done | bytes 589856 | tf_op jit(solution)/shard_map/ppermute | solution.py:45
  45.3 2.7 %shard_map.87 = (bf16[256,1152]{1,0:T(8,128)(2,1)S(1)}, bf16[256,256]{1,0:T(8,128)(2,1)S(1)}, bf16[256,256]{1,0:T(8,128)(2,1)S(1)}, f32[256,1152]{1,0:T(8,128)S(1)}, f32[8,128]{1,0:T(8,128)S(1)}) custom-call(f32[2]{0:T(128)S(1)} %pad_maximum_fusion.head, s32[3]{0:T(128)S(1)} %pad_add_fusion.start, bf16[256,1280]{1,0:T(8,128)(2,1)S(1)} %get-tuple-element.38.img_u, ...), custom_call_target="tpu_custom_call" | custom-call | tf_op jit(solution)/shard_map/pallas_call | solution.py:154
  50.8 19.8 %conditional.2 = (f32[8,128]{1,0:T(8,128)S(1)}) conditional(s32[]{:T(128)} %convert_element_type.22, () %tuple.23, f32[8,128]{1,0:T(8,128)S(1)} %get-tuple-element.49), branch_computations={%region_0.1_spmd, %region_1.3_spmd} | conditional | flops 1024 | bytes 8200 | solution.py:215
  50.8 19.8 %psum.6 = f32[8,128]{1,0:T(8,128)S(1)} all-reduce(f32[8,128]{1,0:T(8,128)S(1)} %param.1), channel_id=1, replica_groups=mesh['y_lo'=4,'core'=2,'z'=12,'x'=4,'y_hi'=2] {'y_lo','core'}, use_global_device_ids=true, to_apply=%region_2.2 | all-reduce | flops 1024 | bytes 8192 | tf_op jit(solution)/shard_map/cond/branch_1_fun/psum | solution.py:164
  70.6 1.9 %collective-permute-start.4 = (f16[256,1152]{1,0:T(8,128)(2,1)}, f16[256,1152]{1,0:T(8,128)(2,1)S(1)}, u32[]{:S(2)}, u32[]{:S(2)}) collective-permute-start(f16[256,1152]{1,0:T(8,128)(2,1)} %convert_element_type.23), channel_id=1, source_target_pairs={{0,95},{1,0},{2,1},{3,2},{4,3},{5,4},{6,5},{7,6},{8,7},{9,8},{10,9... | collective-permute-start | bytes 1769480 | tf_op jit(solution)/shard_map/ppermute | solution.py:25
  72.5 1.9 %collective-permute-start.5 = (f16[256,1152]{1,0:T(8,128)(2,1)}, f16[256,1152]{1,0:T(8,128)(2,1)}, u32[]{:S(2)}, u32[]{:S(2)}) collective-permute-start(f16[256,1152]{1,0:T(8,128)(2,1)} %convert_element_type.24), channel_id=1, source_target_pairs={{0,96},{1,97},{2,98},{3,99},{4,100},{5,101},{6,102},{7,103},{8,104... | collective-permute-start | bytes 1769480 | tf_op jit(solution)/shard_map/ppermute | solution.py:25
  74.5 4.4 %collective-permute-start.6 = (f16[256,1152]{1,0:T(8,128)(2,1)S(1)}, f16[256,1152]{1,0:T(8,128)(2,1)}, u32[]{:S(2)}, u32[]{:S(2)}) collective-permute-start(f16[256,1152]{1,0:T(8,128)(2,1)S(1)} %convert_element_type.25), channel_id=1, source_target_pairs={{0,94},{1,95},{2,0},{3,1},{4,2},{5,3},{6,4},{7,5},{8,6},{9,7},{10,... | collective-permute-start | bytes 1769480 | tf_op jit(solution)/shard_map/ppermute | solution.py:25
  78.8 67.1 %conditional.3 = (f32[8,128]{1,0:T(8,128)S(1)}) conditional(s32[]{:T(128)} %convert_element_type.22, () %tuple.22, f32[8,128]{1,0:T(8,128)S(1)} %get-tuple-element.69), branch_computations={%region_3.4_spmd, %region_4.7_spmd} | conditional | flops 14336 | bytes 147464 | solution.py:223
  78.8 30.6 %all-gather = f32[96,128]{1,0:T(8,128)S(1)} all-gather(f32[8,128]{1,0:T(8,128)S(1)} %param.3), channel_id=2, replica_groups=mesh['y_lo'=4,'core'=2,'z'=12,'x'=4,'y_hi'=2] {'z'}, dimensions={0}, use_global_device_ids=true | all-gather | bytes 53248 | tf_op jit(solution)/shard_map/cond/branch_1_fun/all_gather | solution.py:168
  109.5 36.5 %all-gather.1 = f32[32,128]{1,0:T(8,128)S(1)} all-gather(f32[8,128]{1,0:T(8,128)S(1)} %bitcast_reduce_fusion), channel_id=3, replica_groups=mesh['y_lo'=4,'core'=2,'z'=12,'x'=4,'y_hi'=2] {'x'}, dimensions={0}, use_global_device_ids=true | all-gather | bytes 20480 | tf_op jit(solution)/shard_map/cond/branch_1_fun/all_gather | solution.py:169
  146.0 6.1 %collective-permute-start.7 = (f32[8,128]{1,0:T(8,128)S(1)}, f32[8,128]{1,0:T(8,128)S(1)}, u32[]{:S(2)}, u32[]{:S(2)}) collective-permute-start(f32[8,128]{1,0:T(8,128)S(1)} %get-tuple-element.70), channel_id=1, source_target_pairs={{0,1},{1,0},{2,3},{3,2},{4,5},{5,4},{6,7},{7,6},{8,9},{9,8},{10,11... | collective-permute-start | bytes 12296 | tf_op jit(solution)/shard_map/ppermute | solution.py:174
  152.1 1.7 %multiply_add_fusion = (f32[256,1152]{1,0:T(8,128)S(1)}, f32[256,1152]{1,0:T(8,128)S(1)}) fusion(f32[256,1152]{1,0:T(8,128)S(1)} %get-tuple-element.58, f16[256,1152]{1,0:T(8,128)(2,1)S(1)} %collective-permute-done.4, f16[256,1152]{1,0:T(8,128)(2,1)} %collective-permute-done.6, f32[256,1152]{1,0:T(8,128)S(1)} %get-tuple-element.48, ...), kind=kLoop, calls=%fused_computation.2 | loop fusion | flops 2359296 | bytes 6488064 | tf_op jit(solution)/shard_map/add | solution.py:230
  153.8 2.7 %shard_map.89 = (f32[256,1152]{1,0:T(8,128)}, f32[256,1152]{1,0:T(8,128)}) custom-call(f32[2]{0:T(128)S(1)} %pad_maximum_fusion.head, s32[3]{0:T(128)S(1)} %pad_add_fusion.start, bf16[256,1152]{1,0:T(8,128)(2,1)S(1)} %copy-done.1, bf16[256,1152]{1,0:T(8,128)(2,1)S(1)} %copy-done.3, f32[256,1152]{1,0:T(8,128)S(1)} %get-tuple-element.68.img_total, ...), custom_call_target="tpu_custom_call" | custom-call | tf_op jit(solution)/shard_map/pallas_call | solution.py:154
  158.6 1.2 maximum_multiply_fusion
  (27 shorter events, 7.5 us)
Async XLA Ops:
  0.6 17.1 %collective-permute-start.1 = (bf16[256,1152]{1,0:T(8,128)(2,1)}, bf16[256,1152]{1,0:T(8,128)(2,1)}, u32[]{:S(2)}, u32[]{:S(2)}) collective-permute-start(bf16[256,1152]{1,0:T(8,128)(2,1)} %txt_raw.3), channel_id=1, source_target_pairs={{0,384},{1,385},{2,386},{3,387},{4,388},{5,389},{6,390},{7,391},{8... | collective-permute-start | bytes 1769480 | tf_op jit(solution)/shard_map/ppermute | solution.py:45
  7.5 1.1 copy-start
  8.6 1.1 copy-start.2
  10.7 25.4 %collective-permute-start = (bf16[256,1280]{1,0:T(8,128)(2,1)S(1)}, bf16[256,1280]{1,0:T(8,128)(2,1)S(1)}, u32[]{:S(2)}, u32[]{:S(2)}) collective-permute-start(bf16[256,1280]{1,0:T(8,128)(2,1)S(1)} %get-tuple-element.38.img_u), channel_id=1, source_target_pairs={{0,672},{1,673},{2,674},{3,675},{4,676},{5,677},{6,678},{7,679},{8... | collective-permute-start | bytes 1966088 | tf_op jit(solution)/shard_map/ppermute | solution.py:25
  13.1 22.1 %collective-permute-start.3 = (bf16[256,1152]{1,0:T(8,128)(2,1)S(1)}, bf16[256,1152]{1,0:T(8,128)(2,1)S(1)}, u32[]{:S(2)}, u32[]{:S(2)}) collective-permute-start(bf16[256,1152]{1,0:T(8,128)(2,1)S(1)} %get-tuple-element.39.txt_u), channel_id=1, source_target_pairs={{0,2},{1,3},{2,4},{3,5},{4,6},{5,7},{6,8},{7,9},{8,10},{9,11},{10,... | collective-permute-start | bytes 1769480 | tf_op jit(solution)/shard_map/ppermute | solution.py:25
  17.8 27.5 %collective-permute-start.2 = (bf16[256,1152]{1,0:T(8,128)(2,1)}, bf16[256,1152]{1,0:T(8,128)(2,1)}, u32[]{:S(2)}, u32[]{:S(2)}) collective-permute-start(bf16[256,1152]{1,0:T(8,128)(2,1)} %collective-permute-done.1), channel_id=1, source_target_pairs={{384,1},{385,2},{386,3},{387,4},{388,5},{389,6},{390,7},{391,8},{3... | collective-permute-start | bytes 1769480 | tf_op jit(solution)/shard_map/ppermute | solution.py:45
  35.3 0.8 copy-start.4
  36.1 1.1 copy-start.5
  70.6 75.4 %collective-permute-start.4 = (f16[256,1152]{1,0:T(8,128)(2,1)}, f16[256,1152]{1,0:T(8,128)(2,1)S(1)}, u32[]{:S(2)}, u32[]{:S(2)}) collective-permute-start(f16[256,1152]{1,0:T(8,128)(2,1)} %convert_element_type.23), channel_id=1, source_target_pairs={{0,95},{1,0},{2,1},{3,2},{4,3},{5,4},{6,5},{7,6},{8,7},{9,8},{10,9... | collective-permute-start | bytes 1769480 | tf_op jit(solution)/shard_map/ppermute | solution.py:25
  72.5 73.4 %collective-permute-start.5 = (f16[256,1152]{1,0:T(8,128)(2,1)}, f16[256,1152]{1,0:T(8,128)(2,1)}, u32[]{:S(2)}, u32[]{:S(2)}) collective-permute-start(f16[256,1152]{1,0:T(8,128)(2,1)} %convert_element_type.24), channel_id=1, source_target_pairs={{0,96},{1,97},{2,98},{3,99},{4,100},{5,101},{6,102},{7,103},{8,104... | collective-permute-start | bytes 1769480 | tf_op jit(solution)/shard_map/ppermute | solution.py:25
  74.5 71.5 %collective-permute-start.6 = (f16[256,1152]{1,0:T(8,128)(2,1)S(1)}, f16[256,1152]{1,0:T(8,128)(2,1)}, u32[]{:S(2)}, u32[]{:S(2)}) collective-permute-start(f16[256,1152]{1,0:T(8,128)(2,1)S(1)} %convert_element_type.25), channel_id=1, source_target_pairs={{0,94},{1,95},{2,0},{3,1},{4,2},{5,3},{6,4},{7,5},{8,6},{9,7},{10,... | collective-permute-start | bytes 1769480 | tf_op jit(solution)/shard_map/ppermute | solution.py:25
  146.0 10.6 %collective-permute-start.7 = (f32[8,128]{1,0:T(8,128)S(1)}, f32[8,128]{1,0:T(8,128)S(1)}, u32[]{:S(2)}, u32[]{:S(2)}) collective-permute-start(f32[8,128]{1,0:T(8,128)S(1)} %get-tuple-element.70), channel_id=1, source_target_pairs={{0,1},{1,0},{2,3},{3,2},{4,5},{5,4},{6,7},{7,6},{8,9},{9,8},{10,11... | collective-permute-start | bytes 12296 | tf_op jit(solution)/shard_map/ppermute | solution.py:174
  152.1 1.7 %copy-start.1 = (bf16[256,1152]{1,0:T(8,128)(2,1)S(1)}, bf16[256,1152]{1,0:T(8,128)(2,1)}, u32[]{:S(2)}) copy-start(bf16[256,1152]{1,0:T(8,128)(2,1)} %img_raw.3) | copy-start | bytes 1769476
  152.1 1.7 %copy-start.3 = (bf16[256,1152]{1,0:T(8,128)(2,1)S(1)}, bf16[256,1152]{1,0:T(8,128)(2,1)}, u32[]{:S(2)}) copy-start(bf16[256,1152]{1,0:T(8,128)(2,1)} %txt_raw.3) | copy-start | bytes 1769476

commit v7 on v5

--- a/solution.py
+++ b/solution.py
@@ -35,14 +35,12 @@
     return route
 
 
-def one_step_in_two(block, sign):
-    first = half_way()
-    ends = [
+def second_half(sign):
+    return [
         (there, o * N_INNER + (p + sign) % N_INNER)
-        for device, there in first
+        for device, there in half_way()
         for o, p in [divmod(device, N_INNER)]
     ]
-    return lax.ppermute(lax.ppermute(block, AXES, first), AXES, ends)
 
 
 def unit_of(ref):
@@ -189,7 +187,8 @@
     pair = jax.ShapeDtypeStruct((rows, rows), bf16)
     sums = jax.ShapeDtypeStruct((8, 128), f32)
 
-    mid_raw = one_step_in_two(text_emb, 1)
+    mid_raw = lax.ppermute(text_emb, AXES, half_way())
+    mid_raw = lax.ppermute(mid_raw, AXES, second_half(1))
     marked = jax.ShapeDtypeStruct((rows, width + CODE), bf16)
     img_u, txt_u = call(unit_kernel, (head, start, image_emb, text_emb, pos), [marked, unit])
     img2_u = moved(img_u, -1, 0)
@@ -211,17 +210,18 @@
         [wide, wide],
     )
     always = lax.optimization_barrier(jnp.bool_(True))
+    half = jnp.float16
+    mid_back = lax.ppermute(mid_acc.astype(half), AXES, half_way())
     stats = lax.cond(always, sum_z, jnp.zeros_like, stats)
-    half = jnp.float16
-    stats, mid_half, img_half, far_half = lax.optimization_barrier(
-        (stats, mid_acc.astype(half), img2_acc.astype(half), far_acc.astype(half))
-    )
-    mid_back = moved(mid_half, 0, -1)
-    img_back = moved(img_half, 1, 0)
-    far_back = moved(far_half, 0, -2)
+    stats, mid_back, img_back, far_back = lax.optimization_barrier(
+        (stats, mid_back, img2_acc.astype(half), far_acc.astype(half))
+    )
+    mid_back = lax.ppermute(mid_back, AXES, second_half(-1))
+    img_back = moved(img_back, 1, 0)
+    far_back = moved(far_back, 0, -2)
     stats = lax.cond(always, sum_x_y_lo, jnp.zeros_like, stats)
-    stats, far_back, mid_back, img_back = lax.optimization_barrier(
-        (stats, far_back, mid_back, img_back)
+    stats, mid_back, img_back, far_back = lax.optimization_barrier(
+        (stats, mid_back, img_back, far_back)
     )
     totals = jnp.sum(sum_last(stats), axis=1)
 

time: 149 us -> 156 us (1.047)
  starting transfers between devices: 40.7 us -> 50.2 us
  blocking collectives: 54.4 us -> 50.6 us
    psum x1, blocking collectives: 28.9 us -> 14.8 us  [sum_x_y_lo(): return lax.psum(jnp.sum(lax.all_gather(s, 'x'), axis=0), ('y_lo', 'core'))]
    all_gather x1, blocking collectives: 10 us -> 19.3 us  [sum_x_y_lo(): return lax.psum(jnp.sum(lax.all_gather(s, 'x'), axis=0), ('y_lo', 'core'))]
    ppermute x1, starting transfers between devices: 3.62 us -> 10.2 us  [sum_last(): return s + lax.ppermute(s, AXES, route)]
    ppermute x2 -> x4, starting transfers between devices: 12.5 us -> 17.4 us  [the longest x1 6.71 us: shards(): mid_raw = lax.ppermute(text_emb, AXES, half_way())]
    ppermute x5 -> x4, starting transfers between devices: 24.6 us -> 22.6 us  [moved(): return lax.ppermute(block, AXES, route)]
    unnamed x12 -> x16, local copies, waits for them, and re-layouts: 4.02 us -> 5.03 us
    ppermute x2 -> x4, waiting for transfers between devices: 9.97 us -> 10.7 us  [the longest x1 10.7 us: shards(): mid_raw = lax.ppermute(mid_raw, AXES, second_half(1))]
    ppermute x5 -> x4, waiting for transfers between devices: 15.8 us -> 15.7 us  [moved(): return lax.ppermute(block, AXES, route)]
  transfers between devices with their start and end apart: 8 -> 9, of which waited for: 3 -> 2; matrix products, arithmetic and copies ran while one was open for 2% -> 3% of each run, Pallas kernels for 6% -> 6%
where the time goes in v7:
time: 156 us
  blocking collectives  50.6 us (32%)
  starting transfers between devices  50.2 us (32%)
  waiting for transfers between devices  26.4 us (17%)
  Pallas kernels  11.5 us (7%)
  local copies, waits for them, and re-layouts  6.48 us (4%)
  other arithmetic  5.8 us (4%)
  between operations  4.69 us (3%)
    ppermute x4, starting transfers between devices, moved(): return lax.ppermute(block, AXES, route)  22.6 us
    all_gather x1, blocking collectives, sum_x_y_lo(): return lax.psum(jnp.sum(lax.all_gather(s, 'x'), axis=0), ('y_lo', 'core'))  19.3 us
    all_gather x1, blocking collectives, sum_z(): return jnp.sum(lax.all_gather(s, 'z'), axis=0)  16.5 us
    ppermute x4, waiting for transfers between devices, moved(): return lax.ppermute(block, AXES, route)  15.7 us
    psum x1, blocking collectives, sum_x_y_lo(): return lax.psum(jnp.sum(lax.all_gather(s, 'x'), axis=0), ('y_lo', 'core'))  14.8 us
    pallas_call x6, Pallas kernels, call(): pl.pallas_call(kernel, in_specs=scalars + arrays, out_specs=[pl.BlockSpec...  11.5 us
    ppermute x1, waiting for transfers between devices, shards(): mid_raw = lax.ppermute(mid_raw, AXES, second_half(1))  10.7 us
    ppermute x1, starting transfers between devices, sum_last(): return s + lax.ppermute(s, AXES, route)  10.2 us
  transfers between devices with their start and end apart: 9, of which 2 were waited for; matrix products, arithmetic and copies ran while one was open for 3% of the time, Pallas kernels for 6%

profile of v7, /device:TPU:1, one launch (start us, length us, event | category | flops | bytes accessed | tf_op | source)
XLA Modules:
  0.0 155.7 jit_solution(16004133854186216098)
XLA Ops:
  0.6 6.7 %collective-permute-start.1 = (bf16[256,1152]{1,0:T(8,128)(2,1)}, bf16[256,1152]{1,0:T(8,128)(2,1)S(1)}, u32[]{:S(2)}, u32[]{:S(2)}) collective-permute-start(bf16[256,1152]{1,0:T(8,128)(2,1)} %txt_raw.3), channel_id=1, source_target_pairs={{0,384},{1,385},{2,386},{3,387},{4,388},{5,389},{6,390},{7,391},{8... | collective-permute-start | bytes 1769480 | tf_op jit(solution)/shard_map/ppermute | solution.py:190
  12.9 7.6 %collective-permute-start = (bf16[256,1280]{1,0:T(8,128)(2,1)S(1)}, bf16[256,1280]{1,0:T(8,128)(2,1)S(1)}, u32[]{:S(2)}, u32[]{:S(2)}) collective-permute-start(bf16[256,1280]{1,0:T(8,128)(2,1)S(1)} %get-tuple-element.38.img_u), channel_id=1, source_target_pairs={{0,672},{1,673},{2,674},{3,675},{4,676},{5,677},{6,678},{7,679},{8... | collective-permute-start | bytes 1966088 | tf_op jit(solution)/shard_map/ppermute | solution.py:25
  20.6 1.9 %collective-permute-start.3 = (bf16[256,1152]{1,0:T(8,128)(2,1)S(1)}, bf16[256,1152]{1,0:T(8,128)(2,1)S(1)}, u32[]{:S(2)}, u32[]{:S(2)}) collective-permute-start(bf16[256,1152]{1,0:T(8,128)(2,1)S(1)} %get-tuple-element.39.txt_u), channel_id=1, source_target_pairs={{0,2},{1,3},{2,4},{3,5},{4,6},{5,7},{6,8},{7,9},{8,10},{9,11},{10,... | collective-permute-start | bytes 1769480 | tf_op jit(solution)/shard_map/ppermute | solution.py:25
  22.5 5.8 %collective-permute-start.2 = (bf16[256,1152]{1,0:T(8,128)(2,1)S(1)}, bf16[256,1152]{1,0:T(8,128)(2,1)S(1)}, u32[]{:S(2)}, u32[]{:S(2)}) collective-permute-start(bf16[256,1152]{1,0:T(8,128)(2,1)S(1)} %collective-permute-done.1), channel_id=1, source_target_pairs={{384,1},{385,2},{386,3},{387,4},{388,5},{389,6},{390,7},{391,8},{3... | collective-permute-start | bytes 1769480 | tf_op jit(solution)/shard_map/ppermute | solution.py:191
  28.3 1.1 shard_map.85
  29.4 15.7 %collective-permute-done.3.far_u = bf16[256,1152]{1,0:T(8,128)(2,1)S(1)} collective-permute-done((bf16[256,1152]{1,0:T(8,128)(2,1)S(1)}, bf16[256,1152]{1,0:T(8,128)(2,1)S(1)}, u32[]{:S(2)}, u32[]{:S(2)}) %collective-permute-start.3) | collective-permute-done | bytes 589856 | tf_op jit(solution)/shard_map/ppermute | solution.py:25
  45.2 3.3 %shard_map.86 = (f32[256,1152]{1,0:T(8,128)S(1)}, f32[256,1152]{1,0:T(8,128)S(1)}, f32[256,1152]{1,0:T(8,128)S(1)}, f32[256,1152]{1,0:T(8,128)S(1)}, f32[8,128]{1,0:T(8,128)S(1)}) custom-call(f32[2]{0:T(128)S(1)} %pad_maximum_fusion.head, s32[3]{0:T(128)S(1)} %pad_add_fusion.start, bf16[256,1280]{1,0:T(8,128)(2,1)S(1)} %get-tuple-element.38.img_u, ...), custom_call_target="tpu_custom_call" | custom-call | tf_op jit(solution)/shard_map/pallas_call | solution.py:152
  49.5 10.7 %collective-permute-done.2.mid_raw = bf16[256,1152]{1,0:T(8,128)(2,1)S(1)} collective-permute-done((bf16[256,1152]{1,0:T(8,128)(2,1)S(1)}, bf16[256,1152]{1,0:T(8,128)(2,1)S(1)}, u32[]{:S(2)}, u32[]{:S(2)}) %collective-permute-start.2) | collective-permute-done | bytes 589856 | tf_op jit(solution)/shard_map/ppermute | solution.py:191
  60.1 2.2 %shard_map.87 = (bf16[256,1152]{1,0:T(8,128)(2,1)S(1)}, bf16[256,256]{1,0:T(8,128)(2,1)S(1)}, bf16[256,256]{1,0:T(8,128)(2,1)S(1)}, f32[256,1152]{1,0:T(8,128)S(1)}, f32[8,128]{1,0:T(8,128)S(1)}) custom-call(f32[2]{0:T(128)S(1)} %pad_maximum_fusion.head, s32[3]{0:T(128)S(1)} %pad_add_fusion.start, bf16[256,1280]{1,0:T(8,128)(2,1)S(1)} %get-tuple-element.38.img_u, ...), custom_call_target="tpu_custom_call" | custom-call | tf_op jit(solution)/shard_map/pallas_call | solution.py:152
  63.2 1.9 %collective-permute-start.4 = (f16[256,1152]{1,0:T(8,128)(2,1)}, f16[256,1152]{1,0:T(8,128)(2,1)}, u32[]{:S(2)}, u32[]{:S(2)}) collective-permute-start(f16[256,1152]{1,0:T(8,128)(2,1)} %convert_element_type.23), channel_id=1, source_target_pairs={{0,384},{1,385},{2,386},{3,387},{4,388},{5,389},{6,390},{7,391},{8... | collective-permute-start | bytes 1769480 | tf_op jit(solution)/shard_map/ppermute | solution.py:214
  66.6 1.3 copy-done.7
  67.9 1.1 shard_map.88
  69.9 16.5 %conditional.2 = (f32[8,128]{1,0:T(8,128)S(1)}) conditional(s32[]{:T(128)} %convert_element_type.22, () %tuple.23, f32[8,128]{1,0:T(8,128)S(1)} %get-tuple-element.49), branch_computations={%region_0.1_spmd, %region_1.3_spmd} | conditional | flops 11264 | bytes 106504 | solution.py:215
  69.9 16.5 %all-gather = f32[96,128]{1,0:T(8,128)S(1)} all-gather(f32[8,128]{1,0:T(8,128)S(1)} %param.1), channel_id=2, replica_groups=mesh['y_lo'=4,'core'=2,'z'=12,'x'=4,'y_hi'=2] {'z'}, dimensions={0}, use_global_device_ids=true | all-gather | bytes 53248 | tf_op jit(solution)/shard_map/cond/branch_1_fun/all_gather | solution.py:162
  86.4 3.1 %collective-permute-start.5 = (f16[256,1152]{1,0:T(8,128)(2,1)}, f16[256,1152]{1,0:T(8,128)(2,1)S(1)}, u32[]{:S(2)}, u32[]{:S(2)}) collective-permute-start(f16[256,1152]{1,0:T(8,128)(2,1)} %collective-permute-done.4), channel_id=1, source_target_pairs={{384,95},{385,0},{386,1},{387,2},{388,3},{389,4},{390,5},{391,6},{... | collective-permute-start | bytes 1769480 | tf_op jit(solution)/shard_map/ppermute | solution.py:219
  89.5 8.4 %collective-permute-start.6 = (f16[256,1152]{1,0:T(8,128)(2,1)}, f16[256,1152]{1,0:T(8,128)(2,1)}, u32[]{:S(2)}, u32[]{:S(2)}) collective-permute-start(f16[256,1152]{1,0:T(8,128)(2,1)} %convert_element_type.24), channel_id=1, source_target_pairs={{0,96},{1,97},{2,98},{3,99},{4,100},{5,101},{6,102},{7,103},{8,104... | collective-permute-start | bytes 1769480 | tf_op jit(solution)/shard_map/ppermute | solution.py:25
  97.9 4.6 %collective-permute-start.7 = (f16[256,1152]{1,0:T(8,128)(2,1)}, f16[256,1152]{1,0:T(8,128)(2,1)}, u32[]{:S(2)}, u32[]{:S(2)}) collective-permute-start(f16[256,1152]{1,0:T(8,128)(2,1)} %convert_element_type.25), channel_id=1, source_target_pairs={{0,94},{1,95},{2,0},{3,1},{4,2},{5,3},{6,4},{7,5},{8,6},{9,7},{10,... | collective-permute-start | bytes 1769480 | tf_op jit(solution)/shard_map/ppermute | solution.py:25
  102.5 34.1 %conditional.3 = (f32[8,128]{1,0:T(8,128)S(1)}) conditional(s32[]{:T(128)} %convert_element_type.22, () %tuple.22, f32[8,128]{1,0:T(8,128)S(1)} %get-tuple-element.69), branch_computations={%region_3.4_spmd, %region_4.7_spmd} | conditional | flops 4096 | bytes 49160 | solution.py:222
  102.5 19.3 %all-gather.1 = f32[32,128]{1,0:T(8,128)S(1)} all-gather(f32[8,128]{1,0:T(8,128)S(1)} %param.3), channel_id=3, replica_groups=mesh['y_lo'=4,'core'=2,'z'=12,'x'=4,'y_hi'=2] {'x'}, dimensions={0}, use_global_device_ids=true | all-gather | bytes 20480 | tf_op jit(solution)/shard_map/cond/branch_1_fun/all_gather | solution.py:166
  121.9 14.8 %psum.6 = f32[8,128]{1,0:T(8,128)S(1)} all-reduce(f32[8,128]{1,0:T(8,128)S(1)} %bitcast_reduce_fusion.1), channel_id=1, replica_groups=mesh['y_lo'=4,'core'=2,'z'=12,'x'=4,'y_hi'=2] {'y_lo','core'}, use_global_device_ids=true, to_apply=%region_6.6 | all-reduce | flops 1024 | bytes 8192 | tf_op jit(solution)/shard_map/cond/branch_1_fun/psum | solution.py:166
  136.7 10.2 %collective-permute-start.8 = (f32[8,128]{1,0:T(8,128)S(1)}, f32[8,128]{1,0:T(8,128)S(1)}, u32[]{:S(2)}, u32[]{:S(2)}) collective-permute-start(f32[8,128]{1,0:T(8,128)S(1)} %get-tuple-element.70), channel_id=1, source_target_pairs={{0,1},{1,0},{2,3},{3,2},{4,5},{5,4},{6,7},{7,6},{8,9},{9,8},{10,11... | collective-permute-start | bytes 12296 | tf_op jit(solution)/shard_map/ppermute | solution.py:171
  146.9 1.6 %multiply_add_fusion = (f32[256,1152]{1,0:T(8,128)S(1)}, f32[256,1152]{1,0:T(8,128)S(1)}) fusion(f32[256,1152]{1,0:T(8,128)S(1)} %get-tuple-element.58, f16[256,1152]{1,0:T(8,128)(2,1)S(1)} %collective-permute-done.5, f16[256,1152]{1,0:T(8,128)(2,1)} %collective-permute-done.7, f32[256,1152]{1,0:T(8,128)S(1)} %get-tuple-element.48, ...), kind=kLoop, calls=%fused_computation.2 | loop fusion | flops 2359296 | bytes 6488064 | tf_op jit(solution)/shard_map/add | solution.py:229
  148.6 2.7 %shard_map.89 = (f32[256,1152]{1,0:T(8,128)}, f32[256,1152]{1,0:T(8,128)}) custom-call(f32[2]{0:T(128)S(1)} %pad_maximum_fusion.head, s32[3]{0:T(128)S(1)} %pad_add_fusion.start, bf16[256,1152]{1,0:T(8,128)(2,1)S(1)} %copy-done.1, bf16[256,1152]{1,0:T(8,128)(2,1)S(1)} %copy-done.3, f32[256,1152]{1,0:T(8,128)S(1)} %get-tuple-element.68.img_total, ...), custom_call_target="tpu_custom_call" | custom-call | tf_op jit(solution)/shard_map/pallas_call | solution.py:152
  153.4 1.2 maximum_multiply_fusion
  (33 shorter events, 9.2 us)
Async XLA Ops:
  0.6 21.9 %collective-permute-start.1 = (bf16[256,1152]{1,0:T(8,128)(2,1)}, bf16[256,1152]{1,0:T(8,128)(2,1)S(1)}, u32[]{:S(2)}, u32[]{:S(2)}) collective-permute-start(bf16[256,1152]{1,0:T(8,128)(2,1)} %txt_raw.3), channel_id=1, source_target_pairs={{0,384},{1,385},{2,386},{3,387},{4,388},{5,389},{6,390},{7,391},{8... | collective-permute-start | bytes 1769480 | tf_op jit(solution)/shard_map/ppermute | solution.py:190
  9.7 1.1 copy-start
  10.8 1.1 copy-start.2
  12.9 32.2 %collective-permute-start = (bf16[256,1280]{1,0:T(8,128)(2,1)S(1)}, bf16[256,1280]{1,0:T(8,128)(2,1)S(1)}, u32[]{:S(2)}, u32[]{:S(2)}) collective-permute-start(bf16[256,1280]{1,0:T(8,128)(2,1)S(1)} %get-tuple-element.38.img_u), channel_id=1, source_target_pairs={{0,672},{1,673},{2,674},{3,675},{4,676},{5,677},{6,678},{7,679},{8... | collective-permute-start | bytes 1966088 | tf_op jit(solution)/shard_map/ppermute | solution.py:25
  20.6 24.6 %collective-permute-start.3 = (bf16[256,1152]{1,0:T(8,128)(2,1)S(1)}, bf16[256,1152]{1,0:T(8,128)(2,1)S(1)}, u32[]{:S(2)}, u32[]{:S(2)}) collective-permute-start(bf16[256,1152]{1,0:T(8,128)(2,1)S(1)} %get-tuple-element.39.txt_u), channel_id=1, source_target_pairs={{0,2},{1,3},{2,4},{3,5},{4,6},{5,7},{6,8},{7,9},{8,10},{9,11},{10,... | collective-permute-start | bytes 1769480 | tf_op jit(solution)/shard_map/ppermute | solution.py:25
  22.5 37.6 %collective-permute-start.2 = (bf16[256,1152]{1,0:T(8,128)(2,1)S(1)}, bf16[256,1152]{1,0:T(8,128)(2,1)S(1)}, u32[]{:S(2)}, u32[]{:S(2)}) collective-permute-start(bf16[256,1152]{1,0:T(8,128)(2,1)S(1)} %collective-permute-done.1), channel_id=1, source_target_pairs={{384,1},{385,2},{386,3},{387,4},{388,5},{389,6},{390,7},{391,8},{3... | collective-permute-start | bytes 1769480 | tf_op jit(solution)/shard_map/ppermute | solution.py:191
  48.4 1.0 copy-start.6
  49.5 13.8 %copy-start.4 = (f32[256,1152]{1,0:T(8,128)}, f32[256,1152]{1,0:T(8,128)S(1)}, u32[]{:S(2)}) copy-start(f32[256,1152]{1,0:T(8,128)S(1)} %get-tuple-element.46.img_in) | copy-start | bytes 3538948
  63.2 23.2 %collective-permute-start.4 = (f16[256,1152]{1,0:T(8,128)(2,1)}, f16[256,1152]{1,0:T(8,128)(2,1)}, u32[]{:S(2)}, u32[]{:S(2)}) collective-permute-start(f16[256,1152]{1,0:T(8,128)(2,1)} %convert_element_type.23), channel_id=1, source_target_pairs={{0,384},{1,385},{2,386},{3,387},{4,388},{5,389},{6,390},{7,391},{8... | collective-permute-start | bytes 1769480 | tf_op jit(solution)/shard_map/ppermute | solution.py:214
  65.1 1.5 copy-start.5
  66.6 1.3 copy-start.7
  86.4 50.2 %collective-permute-start.5 = (f16[256,1152]{1,0:T(8,128)(2,1)}, f16[256,1152]{1,0:T(8,128)(2,1)S(1)}, u32[]{:S(2)}, u32[]{:S(2)}) collective-permute-start(f16[256,1152]{1,0:T(8,128)(2,1)} %collective-permute-done.4), channel_id=1, source_target_pairs={{384,95},{385,0},{386,1},{387,2},{388,3},{389,4},{390,5},{391,6},{... | collective-permute-start | bytes 1769480 | tf_op jit(solution)/shard_map/ppermute | solution.py:219
  89.5 47.2 %collective-permute-start.6 = (f16[256,1152]{1,0:T(8,128)(2,1)}, f16[256,1152]{1,0:T(8,128)(2,1)}, u32[]{:S(2)}, u32[]{:S(2)}) collective-permute-start(f16[256,1152]{1,0:T(8,128)(2,1)} %convert_element_type.24), channel_id=1, source_target_pairs={{0,96},{1,97},{2,98},{3,99},{4,100},{5,101},{6,102},{7,103},{8,104... | collective-permute-start | bytes 1769480 | tf_op jit(solution)/shard_map/ppermute | solution.py:25
  97.9 38.8 %collective-permute-start.7 = (f16[256,1152]{1,0:T(8,128)(2,1)}, f16[256,1152]{1,0:T(8,128)(2,1)}, u32[]{:S(2)}, u32[]{:S(2)}) collective-permute-start(f16[256,1152]{1,0:T(8,128)(2,1)} %convert_element_type.25), channel_id=1, source_target_pairs={{0,94},{1,95},{2,0},{3,1},{4,2},{5,3},{6,4},{7,5},{8,6},{9,7},{10,... | collective-permute-start | bytes 1769480 | tf_op jit(solution)/shard_map/ppermute | solution.py:25
  136.7 14.7 %collective-permute-start.8 = (f32[8,128]{1,0:T(8,128)S(1)}, f32[8,128]{1,0:T(8,128)S(1)}, u32[]{:S(2)}, u32[]{:S(2)}) collective-permute-start(f32[8,128]{1,0:T(8,128)S(1)} %get-tuple-element.70), channel_id=1, source_target_pairs={{0,1},{1,0},{2,3},{3,2},{4,5},{5,4},{6,7},{7,6},{8,9},{9,8},{10,11... | collective-permute-start | bytes 12296 | tf_op jit(solution)/shard_map/ppermute | solution.py:171
  146.9 1.7 %copy-start.1 = (bf16[256,1152]{1,0:T(8,128)(2,1)S(1)}, bf16[256,1152]{1,0:T(8,128)(2,1)}, u32[]{:S(2)}) copy-start(bf16[256,1152]{1,0:T(8,128)(2,1)} %img_raw.3) | copy-start | bytes 1769476
  146.9 1.7 %copy-start.3 = (bf16[256,1152]{1,0:T(8,128)(2,1)S(1)}, bf16[256,1152]{1,0:T(8,128)(2,1)}, u32[]{:S(2)}) copy-start(bf16[256,1152]{1,0:T(8,128)(2,1)} %txt_raw.3) | copy-start | bytes 1769476
